TPU v7x, 32 devices: a whole 2x2x4 slice. The times are simulated.
32 devices in a mesh: row: 4 (over z), col: 8 (over y, x, core).
Axes of the slice: x: 2, y: 2, z: 4, core: 2. Of those that a mesh axis runs over, the one named last changes fastest.
Arguments:
- tokens: bfloat16 [576, 8192], P('col', 'row'), may hold values from -6 to 6
- out_grad: bfloat16 [576, 8192], P('col', 'row'), may hold values from -6 to 6
- gate_pre: bfloat16 [576, 28672], P('row', 'col'), may hold values from -8 to 8
- up_pre: bfloat16 [576, 28672], P('row', 'col'), may hold values from -6 to 6
- w_gate: bfloat16 [8192, 28672], P('row', 'col'), may hold values from -0.125 to 0.125
- w_up: bfloat16 [8192, 28672], P('row', 'col'), may hold values from -0.125 to 0.125
- w_down: bfloat16 [28672, 8192], P('col', 'row'), may hold values from -0.0625 to 0.0625
- mask_gate: int32 [128, 448], P('row', 'col'), may hold values 0 or 1
- mask_up: int32 [128, 448], P('row', 'col'), may hold values 0 or 1
- mask_down: int32 [448, 128], P('col', 'row'), may hold values 0 or 1
Outputs:
- grad_x: bfloat16 [576, 8192], P('col', 'row')
- grad_gate: bfloat16 [8192, 28672], P('row', 'col')
- grad_up: bfloat16 [8192, 28672], P('row', 'col')
- grad_down: bfloat16 [28672, 8192], P('col', 'row')
All inputs are finite; a program needn't handle non-finite values. No bound on the sum of `mask_gate` or of `mask_up` or of `mask_down` on one device may be relied on, other than what follows from the above.
Results may differ from a plain program's by a relative error of at most 0.0049.
Values may be sent and summed in bfloat16 or wider, within the bound.
No kernel may reach another device: no remote copies, remote signals or barrier semaphores. Data moves between devices by JAX's collectives and lax.ppermute only.
A program may use at most 192 MiB of HBM per device.

v0:
```python
import jax
import jax.numpy as jnp
from jax import lax
from jax.sharding import PartitionSpec as P

TILE = 64


def expand(keep_mask):
    small = keep_mask.astype(jnp.bfloat16)
    return jnp.repeat(jnp.repeat(small, TILE, axis=0), TILE, axis=1)


def contract_last(left, right):
    return lax.dot_general(
        left, right, (((1,), (1,)), ((), ())), preferred_element_type=jnp.float32
    )


def contract_first(left, right):
    return lax.dot_general(
        left, right, (((0,), (0,)), ((), ())), preferred_element_type=jnp.float32
    )


def gate_arith(gate_pre, up_pre):
    gate_val = gate_pre.astype(jnp.float32)
    up_val = up_pre.astype(jnp.float32)
    sigmoid_g = jax.nn.sigmoid(gate_val)
    silu_g = gate_val * sigmoid_g
    return (gate_val, up_val, sigmoid_g, silu_g)


def gate_grads(d_hidden, gate_val, up_val, sigmoid_g, silu_g):
    d_gate = (d_hidden * up_val * sigmoid_g * (1.0 + gate_val * (1.0 - sigmoid_g))).astype(
        jnp.bfloat16
    )
    d_up = (d_hidden * silu_g).astype(jnp.bfloat16)
    return (d_gate, d_up)


def per_device(
    tokens, out_grad, gate_pre, up_pre, w_gate, w_up, w_down, mask_gate, mask_up, mask_down
):
    keep_gate = expand(mask_gate)
    keep_up = expand(mask_up)
    keep_down = expand(mask_down)
    gate_eff = w_gate * keep_gate
    up_eff = w_up * keep_up
    down_eff = w_down * keep_down
    grad_all, tok_all = (
        lax.all_gather(out_grad, "col", axis=0, tiled=True),
        lax.all_gather(tokens, "col", axis=0, tiled=True),
    )
    gate_val, up_val, sigmoid_g, silu_g = gate_arith(gate_pre, up_pre)
    hidden_part = (silu_g * up_val).astype(jnp.bfloat16)
    hidden_all = lax.all_gather(hidden_part, "row", axis=0, tiled=True)
    d_hidden = lax.psum_scatter(
        contract_last(grad_all, down_eff), "row", scatter_dimension=0, tiled=True
    )
    d_gate, d_up = gate_grads(d_hidden, gate_val, up_val, sigmoid_g, silu_g)
    dgate_all, dup_all = (
        lax.all_gather(d_gate, "row", axis=0, tiled=True),
        lax.all_gather(d_up, "row", axis=0, tiled=True),
    )
    grad_x = lax.psum_scatter(
        contract_last(dgate_all, gate_eff) + contract_last(dup_all, up_eff),
        "col",
        scatter_dimension=0,
        tiled=True,
    ).astype(jnp.bfloat16)
    grad_gate = (contract_first(tok_all, dgate_all) * keep_gate.astype(jnp.float32)).astype(
        jnp.bfloat16
    )
    grad_up = (contract_first(tok_all, dup_all) * keep_up.astype(jnp.float32)).astype(jnp.bfloat16)
    grad_down = (contract_first(hidden_all, grad_all) * keep_down.astype(jnp.float32)).astype(
        jnp.bfloat16
    )
    return (grad_x, grad_gate, grad_up, grad_down)


def solution(mesh):
    return jax.shard_map(
        per_device,
        mesh=mesh,
        in_specs=(
            P("col", "row"),
            P("col", "row"),
            P("row", "col"),
            P("row", "col"),
            P("row", "col"),
            P("row", "col"),
            P("col", "row"),
            P("row", "col"),
            P("row", "col"),
            P("col", "row"),
        ),
        out_specs=(P("col", "row"), P("row", "col"), P("row", "col"), P("col", "row")),
        check_vma=False,
    )
```

profile of v0, /device:TPU:0, one launch (start us, length us, event | category | flops | bytes accessed | tf_op | source)
XLA Modules:
  0.0 547.1 jit_solution(1231140790140074344)
XLA Ops:
  7.2 0.0 all-gather.6.cloned.1.call-start
  7.2 0.7 all-gather.6.cloned.1.call-update
  7.9 0.0 copy-start.2
  7.9 0.0 reduce-scatter.3.cloned.1.call-start
  8.0 18.7 %copy.21 = bf16[3584,2048]{0,1:T(8,128)(2,1)} copy(bf16[3584,2048]{1,0:T(8,128)(2,1)} %param.16) | data formatting | bytes 29360128 | tf_op args[6]
  26.7 0.0 copy-done.2
  26.7 0.3 broadcast_in_dim.18
  27.0 0.3 reshape.26
  27.3 14.3 %all-gather.6.cloned.1.call-done = bf16[576,2048]{1,0:T(8,128)(2,1)} async-done(((bf16[72,2048]{1,0:T(8,128)(2,1)}), bf16[576,2048]{1,0:T(8,128)(2,1)}) %all-gather.6.cloned.1.call-update) | async-done | bytes 2359312 | tf_op jit(solution)/shard_map/all_gather | solution.py:52
  41.6 6.6 %broadcast_in_dim.19 = bf16[3584,32,64]{0,2,1:T(8,128)(2,1)} broadcast(bf16[3584,32]{0,1:T(8,128)(2,1)S(1)} %reshape.26), dimensions={0,1} | broadcast | bytes 14909440 | tf_op jit(solution)/shard_map/broadcast_in_dim | solution.py:11
  48.2 0.0 copy-done.5
  48.2 16.0 %fusion.4 = f32[576,3584]{1,0:T(8,128)} fusion(bf16[576,2048]{1,0:T(8,128)(2,1)S(1)} %copy-done.5, bf16[3584,2048]{0,1:T(8,128)(2,1)} %copy.21, bf16[3584,2048]{0,1:T(8,128)(2,1)} %bitcast.34), kind=kOutput, calls=%fused_computation.9 | convolution fusion | flops 8463056896 | bytes 39976960 | tf_op jit(solution)/shard_map/dot_general | solution.py:15
  64.3 0.0 reduce-scatter.3.cloned.1.call-update
  64.3 0.0 all-gather.8.cloned.1.call-start
  64.4 142.5 %reduce-scatter.3.cloned.1.call-done = f32[144,3584]{1,0:T(8,128)} async-done(((f32[576,3584]{1,0:T(8,128)}), f32[144,3584]{1,0:T(8,128)}) %reduce-scatter.3.cloned.1.call-update) | async-done | bytes 2064400 | tf_op jit(solution)/shard_map/reduce_scatter | solution.py:58
  206.9 0.0 copy-done
  206.9 0.0 copy-done.1
  206.9 4.3 multiply_convert_fusion.1
  211.1 0.0 all-gather.8.cloned.1.call-update
  211.1 0.0 all-gather.10.cloned.1.call-start
  211.2 0.5 all-gather.10.cloned.1.call-update
  211.7 0.0 all-gather.12.cloned.1.call-start
  211.8 0.5 all-gather.12.cloned.1.call-update
  212.3 0.0 all-gather.14.cloned.1.call-start
  212.4 0.5 all-gather.14.cloned.1.call-update
  212.9 0.0 copy-start.3
  212.9 0.2 reduce-scatter.5.cloned.1.call-start
  213.1 20.4 %copy.23 = bf16[2048,3584]{0,1:T(8,128)(2,1)} copy(bf16[2048,3584]{1,0:T(8,128)(2,1)} %param.14) | data formatting | bytes 29360128 | tf_op args[4]
  233.5 0.0 copy-done.3
  233.5 0.1 copy.22
  233.6 0.3 broadcast_in_dim.20
  233.9 0.4 reshape.28
  234.3 0.0 copy-start.4
  234.4 20.3 %copy.25 = bf16[2048,3584]{0,1:T(8,128)(2,1)} copy(bf16[2048,3584]{1,0:T(8,128)(2,1)} %param.15) | data formatting | bytes 29360128 | tf_op args[5]
  254.6 0.0 copy-done.4
  254.6 0.1 copy.24
  254.7 0.3 broadcast_in_dim.22
  255.0 0.0 slice-start
  255.1 0.4 reshape.30
  255.5 0.0 slice-start.1
  255.5 0.0 slice-start.2
  255.5 0.0 slice-start.3
  255.5 15.4 %bitcast_multiply_fusion.3 = bf16[2048,3584]{0,1:T(8,128)(2,1)} fusion(bf16[2048,3584]{0,1:T(8,128)(2,1)} %copy.23, bf16[2048,56]{0,1:T(8,128)(2,1)S(1)} %reshape.28), kind=kLoop, calls=%fused_computation.6 | loop fusion | flops 7340032 | bytes 29589504 | tf_op jit(solution)/shard_map/mul | solution.py:48
  270.9 0.0 slice-done
  270.9 0.0 slice-done.1
  270.9 0.0 slice-done.2
  270.9 0.0 slice-done.3
  270.9 5.9 %bitcast_multiply_fusion.2 = bf16[2048,3584]{0,1:T(8,128)(2,1)} fusion(bf16[2048,3584]{0,1:T(8,128)(2,1)S(1)} %bitcast.37, bf16[2048,56]{0,1:T(8,128)(2,1)S(1)} %reshape.30), kind=kLoop, calls=%fused_computation.5 | loop fusion | flops 7340032 | bytes 29589504 | tf_op jit(solution)/shard_map/mul | solution.py:49
  276.8 14.8 %all-gather.8.cloned.1.call-done = bf16[576,3584]{1,0:T(8,128)(2,1)} async-done(((bf16[144,3584]{1,0:T(8,128)(2,1)}), bf16[576,3584]{1,0:T(8,128)(2,1)}) %all-gather.8.cloned.1.call-update) | async-done | bytes 4128784 | tf_op jit(solution)/shard_map/all_gather | solution.py:63
  291.7 14.6 %fusion.15 = f32[576,2048]{1,0:T(8,128)} fusion(bf16[576,3584]{1,0:T(8,128)(2,1)} %all-gather.8.cloned.1.call-done, bf16[2048,3584]{0,1:T(8,128)(2,1)} %bitcast_multiply_fusion.3), kind=kOutput, calls=%fused_computation.25 | convolution fusion | flops 8455716864 | bytes 23527424 | tf_op jit(solution)/shard_map/dot_general | solution.py:15
  306.2 65.2 %all-gather.10.cloned.1.call-done = bf16[576,3584]{1,0:T(8,128)(2,1)} async-done(((bf16[144,3584]{1,0:T(8,128)(2,1)}), bf16[576,3584]{1,0:T(8,128)(2,1)}) %all-gather.10.cloned.1.call-update) | async-done | bytes 4128784 | tf_op jit(solution)/shard_map/all_gather | solution.py:64
  371.4 15.3 %convolution_add_fusion = f32[576,2048]{1,0:T(8,128)} fusion(f32[576,2048]{1,0:T(8,128)} %fusion.15, bf16[576,3584]{1,0:T(8,128)(2,1)} %all-gather.10.cloned.1.call-done, bf16[2048,3584]{0,1:T(8,128)(2,1)} %bitcast_multiply_fusion.2), kind=kOutput, calls=%fused_computation.10 | convolution fusion | flops 8456896512 | bytes 28246016 | tf_op jit(solution)/shard_map/dot_general | solution.py:15
  386.7 0.0 reduce-scatter.5.cloned.1.call-update
  386.7 20.4 %copy.26 = bf16[3584,2048]{1,0:T(8,128)(2,1)} copy(bf16[3584,2048]{0,1:T(8,128)(2,1)} %bitcast.35) | data formatting | bytes 29360128 | tf_op jit(solution)/shard_map/reshape | solution.py:11
  407.1 17.7 %fusion.1 = bf16[2048,3584]{0,1:T(8,128)(2,1)} fusion(bf16[576,3584]{1,0:T(8,128)(2,1)} %all-gather.8.cloned.1.call-done, bf16[576,2048]{1,0:T(8,128)(2,1)} %all-gather.12.cloned.1.call-done, bf16[2048,56]{0,1:T(8,128)(2,1)S(1)} %reshape.28), kind=kOutput, calls=%fused_computation.3 | convolution fusion | flops 8477736960 | bytes 21397504 | tf_op jit(solution)/shard_map/dot_general | solution.py:21
  424.8 18.8 %copy.27 = bf16[2048,3584]{1,0:T(8,128)(2,1)} copy(bf16[2048,3584]{0,1:T(8,128)(2,1)} %fusion.1) | data formatting | bytes 29360128
  443.7 0.0 copy-done.7
  443.7 16.3 %fusion = bf16[2048,3584]{0,1:T(8,128)(2,1)} fusion(bf16[576,3584]{1,0:T(8,128)(2,1)} %all-gather.10.cloned.1.call-done, bf16[576,2048]{1,0:T(8,128)(2,1)S(1)} %copy-done.7, bf16[2048,56]{0,1:T(8,128)(2,1)S(1)} %reshape.30), kind=kOutput, calls=%fused_computation.1 | convolution fusion | flops 8477736960 | bytes 21397504 | tf_op jit(solution)/shard_map/dot_general | solution.py:21
  460.0 18.8 %copy.28 = bf16[2048,3584]{1,0:T(8,128)(2,1)} copy(bf16[2048,3584]{0,1:T(8,128)(2,1)} %fusion) | data formatting | bytes 29360128
  478.8 3.3 all-gather.14.cloned.1.call-done
  482.1 0.0 copy-done.6
  482.1 18.2 %multiply_convert_fusion = bf16[3584,2048]{1,0:T(8,128)(2,1)} fusion(bf16[3584,2048]{1,0:T(8,128)(2,1)} %copy.26, bf16[576,3584]{1,0:T(8,128)(2,1)} %all-gather.14.cloned.1.call-done, bf16[576,2048]{1,0:T(8,128)(2,1)S(1)} %copy-done.6), kind=kOutput, calls=%fused_computation.4 | convolution fusion | flops 8477736960 | bytes 35848192 | tf_op jit(solution)/shard_map/dot_general | solution.py:21
  500.3 38.1 %reduce-scatter.5.cloned.1.call-done = f32[72,2048]{1,0:T(8,128)} async-done(((f32[576,2048]{1,0:T(8,128)}), f32[72,2048]{1,0:T(8,128)}) %reduce-scatter.5.cloned.1.call-update) | async-done | bytes 589840 | tf_op jit(solution)/shard_map/reduce_scatter | solution.py:66
  538.4 1.8 convert_element_type.52
  (10 shorter events, 0.0 us)
Async XLA Ops:
  7.2 34.5 %all-gather.6.cloned.1.call-start = ((), (), s32[]{:S(2)}) async-start(), calls=%async_computation.2 | async-start | bytes 2654208 | tf_op jit(solution)/shard_map/all_gather | solution.py:52
  7.9 18.8 %copy-start.2 = (s32[56,32]{0,1:T(8,128)S(1)}, s32[56,32]{0,1:T(8,128)}, u32[]{:S(2)}) copy-start(s32[56,32]{0,1:T(8,128)} %param.19) | copy-start | bytes 21508
  7.9 198.9 %reduce-scatter.3.cloned.1.call-start = ((), (), s32[]{:S(2)}) async-start(), calls=%async_computation.3 | async-start | bytes 10321920 | tf_op jit(solution)/shard_map/reduce_scatter | solution.py:58
  41.6 6.6 %copy-start.5 = (bf16[576,2048]{1,0:T(8,128)(2,1)S(1)}, bf16[576,2048]{1,0:T(8,128)(2,1)}, u32[]{:S(2)}) copy-start(bf16[576,2048]{1,0:T(8,128)(2,1)} %all-gather.6.cloned.1.call-done) | copy-start | bytes 7077892
  64.3 142.6 %copy-start = (bf16[144,3584]{1,0:T(8,128)(2,1)S(1)}, bf16[144,3584]{1,0:T(8,128)(2,1)}, u32[]{:S(2)}) copy-start(bf16[144,3584]{1,0:T(8,128)(2,1)} %param.12) | copy-start | bytes 3096580
  64.3 142.6 %copy-start.1 = (bf16[144,3584]{1,0:T(8,128)(2,1)S(1)}, bf16[144,3584]{1,0:T(8,128)(2,1)}, u32[]{:S(2)}) copy-start(bf16[144,3584]{1,0:T(8,128)(2,1)} %param.13) | copy-start | bytes 3096580
  64.3 227.4 %all-gather.8.cloned.1.call-start = ((), (), s32[]{:S(2)}) async-start(), calls=%async_computation.4 | async-start | bytes 5160960 | tf_op jit(solution)/shard_map/all_gather | solution.py:63
  211.1 160.3 %all-gather.10.cloned.1.call-start = ((), (), s32[]{:S(2)}) async-start(), calls=%async_computation.5 | async-start | bytes 5160960 | tf_op jit(solution)/shard_map/all_gather | solution.py:64
  211.7 195.4 %all-gather.12.cloned.1.call-start = ((), (), s32[]{:S(2)}) async-start(), calls=%async_computation.7 | async-start | bytes 2654208 | tf_op jit(solution)/shard_map/all_gather | solution.py:53
  212.3 269.8 %all-gather.14.cloned.1.call-start = ((), (), s32[]{:S(2)}) async-start(), calls=%async_computation.8 | async-start | bytes 5160960 | tf_op jit(solution)/shard_map/all_gather | solution.py:57
  212.9 20.6 %copy-start.3 = (s32[32,56]{1,0:T(8,128)S(1)}, s32[32,56]{1,0:T(8,128)}, u32[]{:S(2)}) copy-start(s32[32,56]{1,0:T(8,128)} %param.17) | copy-start | bytes 21508
  212.9 325.5 %reduce-scatter.5.cloned.1.call-start = ((), (), s32[]{:S(2)}) async-start(), calls=%async_computation.6 | async-start | bytes 5308416 | tf_op jit(solution)/shard_map/reduce_scatter | solution.py:66
  234.3 20.3 %copy-start.4 = (s32[32,56]{1,0:T(8,128)S(1)}, s32[32,56]{1,0:T(8,128)}, u32[]{:S(2)}) copy-start(s32[32,56]{1,0:T(8,128)} %param.18) | copy-start | bytes 21508
  255.0 15.9 %slice-start = ((s8[14680064]{0:T(1024)(128)(4,1)}), s8[2097152]{0:T(1024)(128)(4,1)S(1)}, s32[]{:S(2)}) async-start(s8[14680064]{0:T(1024)(128)(4,1)} %bitcast.36), calls=%async_computation.9 | async-start | bytes 4194304
  255.5 15.4 %slice-start.1 = ((s8[14680064]{0:T(1024)(128)(4,1)}), s8[4194304]{0:T(1024)(128)(4,1)S(1)}, s32[]{:S(2)}) async-start(s8[14680064]{0:T(1024)(128)(4,1)} %bitcast.36), calls=%async_computation.10 | async-start | bytes 8388608
  255.5 15.4 %slice-start.2 = ((s8[14680064]{0:T(1024)(128)(4,1)}), s8[4194304]{0:T(1024)(128)(4,1)S(1)}, s32[]{:S(2)}) async-start(s8[14680064]{0:T(1024)(128)(4,1)} %bitcast.36), calls=%async_computation.11 | async-start | bytes 8388608
  255.5 15.4 %slice-start.3 = ((s8[14680064]{0:T(1024)(128)(4,1)}), s8[4194304]{0:T(1024)(128)(4,1)S(1)}, s32[]{:S(2)}) async-start(s8[14680064]{0:T(1024)(128)(4,1)} %bitcast.36), calls=%async_computation.12 | async-start | bytes 8388608
  424.8 18.8 %copy-start.7 = (bf16[576,2048]{1,0:T(8,128)(2,1)S(1)}, bf16[576,2048]{1,0:T(8,128)(2,1)}, u32[]{:S(2)}) copy-start(bf16[576,2048]{1,0:T(8,128)(2,1)} %all-gather.12.cloned.1.call-done) | copy-start | bytes 7077892
  460.0 22.1 %copy-start.6 = (bf16[576,2048]{1,0:T(8,128)(2,1)S(1)}, bf16[576,2048]{1,0:T(8,128)(2,1)}, u32[]{:S(2)}) copy-start(bf16[576,2048]{1,0:T(8,128)(2,1)} %all-gather.6.cloned.1.call-done) | copy-start | bytes 7077892
Sparse Core Ops, SparseCore 0:
  9.9 31.7 all-gather.5
  64.4 142.3 reduce-scatter.2
  211.3 80.3 all-gather.7
  293.2 78.2 all-gather.9
  373.3 27.5 all-gather.11
  402.4 79.6 all-gather.13
  486.0 52.4 reduce-scatter.4
where the time goes:
time: 550 us; the launch traced here: 547 us
  waiting for transfers between devices  281 us (51%)
  local copies, waits for them, and re-layouts  126 us (23%)
  matrix products  98.1 us (18%)
  other arithmetic  27.4 us (5%)
  between operations  14.3 us (3%)
    reduce_scatter x1, waiting for transfers between devices, per_device(): lax.psum_scatter(contract_last(grad_all, down_eff), 'row', scatter_dimens...  142 us
    unnamed x29, local copies, waits for them, and re-layouts  97 us
    all_gather x1, waiting for transfers between devices, per_device(): lax.all_gather(d_up, 'row', axis=0, tiled=True)  65.2 us
    dot_general x3, matrix products, contract_first(): lax.dot_general(left, right, (((0,), (0,)), ((), ())), preferred_element_...  52.2 us
    dot_general x3, matrix products, contract_last(): lax.dot_general(left, right, (((1,), (1,)), ((), ())), preferred_element_...  45.9 us
    reduce_scatter x1, waiting for transfers between devices, per_device(): lax.psum_scatter(contract_last(dgate_all, gate_eff) + contract_last(dup_a...  38.1 us
    reshape x4, local copies, waits for them, and re-layouts, expand(): return jnp.repeat(jnp.repeat(small, TILE, axis=0), TILE, axis=1)  21.5 us
    mul x1, other arithmetic, per_device(): gate_eff = w_gate * keep_gate  15.4 us
  transfers between devices with their start and end apart: 7, of which 6 were waited for; matrix products, arithmetic and copies ran while one was open for 41% of the time, Pallas kernels for 0%

commit v1 on v0

v1 whole, which is shorter than its diff:
```python
import functools

import jax
import jax.numpy as jnp
from jax import lax
from jax.experimental import pallas as pl
from jax.experimental.pallas import tpu as pltpu
from jax.sharding import PartitionSpec as P

TILE = 64
VMEM_LIMIT = 56 * 1024 * 1024
BF16, F32 = jnp.bfloat16, jnp.float32


def params(n_axes=1):
    return pltpu.CompilerParams(
        dimension_semantics=("arbitrary",) * n_axes, vmem_limit_bytes=VMEM_LIMIT
    )


def whole(shape):
    return pl.BlockSpec(shape, lambda j, *_: (0,) * len(shape))


def masked(block, keep):
    rows = [
        block[r * TILE : (r + 1) * TILE] * keep[r : r + 1] for r in range(keep.shape[0])
    ]
    return jnp.concatenate(rows, axis=0)


def dhidden_kernel(n_low, grad_ref, w_ref, keep_ref, low_ref, high_ref):
    w_eff = masked(w_ref[...], keep_ref[0].astype(BF16))
    out = lax.dot_general(
        grad_ref[...], w_eff, (((1,), (1,)), ((), ())), preferred_element_type=F32
    )

    @pl.when(pl.program_id(0) < n_low)
    def _():
        low_ref[...] = out

    @pl.when(pl.program_id(0) >= n_low)
    def _():
        high_ref[...] = out


def dhidden_part(grad_all, w_down, keep_down, cut, ft):
    T, D = grad_all.shape
    F = w_down.shape[0]
    return pl.pallas_call(
        functools.partial(dhidden_kernel, cut // ft),
        out_shape=(
            jax.ShapeDtypeStruct((T, cut), F32),
            jax.ShapeDtypeStruct((T, F - cut), F32),
        ),
        grid=(F // ft,),
        in_specs=[
            whole((T, D)),
            pl.BlockSpec((ft, D), lambda j: (j, 0)),
            pl.BlockSpec((1, ft // TILE, D), lambda j: (j, 0, 0)),
        ],
        out_specs=[
            pl.BlockSpec((T, ft), lambda j: (0, jnp.minimum(j, cut // ft - 1))),
            pl.BlockSpec((T, ft), lambda j: (0, jnp.maximum(j - cut // ft, 0))),
        ],
        compiler_params=params(),
        cost_estimate=pl.CostEstimate(
            flops=2 * T * D * F, bytes_accessed=2 * D * F + 4 * T * F, transcendentals=0
        ),
        name="dhidden",
    )(grad_all, w_down, keep_down)


def in_order(at_ref, buf, pieces, rows, half=0):
    for s, piece in enumerate(pieces):
        start = pl.multiple_of(at_ref[s] * rows, 16)
        buf[pl.ds(start, rows), :] = piece[half * rows : (half + 1) * rows, :]
    return buf[: buf.shape[0] - rows, :]


def gate_parts(gate, up):
    gate_val, up_val = gate.astype(F32), up.astype(F32)
    sig = jax.nn.sigmoid(gate_val)
    return gate_val, up_val, sig, gate_val * sig


def down_kernel(n, rows, at_ref, *refs):
    pairs, refs = refs[:n], refs[n:]
    grad_ref, keep_ref = refs[:2]
    gdown_ref, buf = refs[-2:]
    gate = in_order(at_ref, buf, pairs, rows, 0)
    up = in_order(at_ref, buf, pairs, rows, 1)
    _, up_val, _, silu = gate_parts(gate, up)
    hidden = (silu * up_val).astype(BF16)
    out = lax.dot_general(
        hidden, grad_ref[...], (((0,), (0,)), ((), ())), preferred_element_type=F32
    )
    gdown_ref[...] = masked(out, keep_ref[0]).astype(BF16)


def down_grad(where, pairs, grad_all, keep_down, held, at, f, n_row, ft):
    T, D = grad_all.shape
    F = keep_down.shape[0] * ft
    rows, n = pairs[0].shape[0], len(pairs)
    first = held is None
    args = [where, *pairs, grad_all, keep_down]
    here = at // ft
    return pl.pallas_call(
        functools.partial(down_kernel, n, rows // 2),
        out_shape=jax.ShapeDtypeStruct((F, D), BF16),
        grid_spec=pltpu.PrefetchScalarGridSpec(
            num_scalar_prefetch=1,
            grid=(f // ft,),
            in_specs=[pl.BlockSpec((rows, ft), lambda j, *_: (0, j))] * n
            + [whole((T, D)), pl.BlockSpec((1, ft // TILE, D), lambda j, *_: (j + here, 0, 0))]
            + ([] if first else [pl.BlockSpec(memory_space=pl.ANY)]),
            out_specs=pl.BlockSpec((ft, D), lambda j, *_: (j + here, 0)),
            scratch_shapes=[pltpu.VMEM(((n_row + 1) * rows // 2, ft), BF16)],
        ),
        input_output_aliases={} if first else {len(args): 0},
        compiler_params=params(),
        cost_estimate=pl.CostEstimate(
            flops=2 * T * D * f, bytes_accessed=2 * D * f + 14 * T * f, transcendentals=T * f
        ),
        name="grad_down",
    )(*args, *([] if first else [held]))


def input_kernel(n, rows, first, at_ref, *refs):
    pieces, pairs, rest = refs[:n], refs[n : 2 * n], refs[2 * n :]
    wg_ref, wu_ref, kg_ref, ku_ref = rest[:4]
    rest = rest[4:]
    if not first:
        sum_ref, rest = rest[0], rest[1:]
    gx_ref, dg_ref, du_ref, buf = rest

    @pl.when(pl.program_id(0) == 0)
    def _():
        d_hidden = in_order(at_ref, buf, pieces, rows).astype(F32)
        gate = in_order(at_ref, buf, pairs, rows, 0)
        up = in_order(at_ref, buf, pairs, rows, 1)
        gate_val, up_val, sig, silu = gate_parts(gate, up)
        dg_ref[...] = (d_hidden * up_val * sig * (1.0 + gate_val * (1.0 - sig))).astype(BF16)
        du_ref[...] = (d_hidden * silu).astype(BF16)

    dims = (((1,), (1,)), ((), ()))
    wg = masked(wg_ref[...], kg_ref[...].astype(BF16))
    wu = masked(wu_ref[...], ku_ref[...].astype(BF16))
    out = lax.dot_general(dg_ref[...], wg, dims, preferred_element_type=F32)
    out = out + lax.dot_general(du_ref[...], wu, dims, preferred_element_type=F32)
    gx_ref[...] = out if first else sum_ref[...] + out


def input_grad(where, pieces, pairs, w_gate, w_up, keep_gate, keep_up, total, start, at, f, n_row, dt):
    rows = pieces[0].shape[0]
    T = rows * n_row
    D = w_gate.shape[0]
    n = len(pieces)
    col, inner = (start + at) // f, at // f
    first = total is None
    weight = pl.BlockSpec((dt, f), lambda d, *_: (d, col))
    keep = pl.BlockSpec((dt // TILE, f), lambda d, *_: (d, col))
    gx = pl.BlockSpec((T, dt), lambda d, *_: (0, d))
    args = [where, *pieces, *pairs, w_gate, w_up, keep_gate, keep_up]
    return pl.pallas_call(
        functools.partial(input_kernel, n, rows, first),
        out_shape=(
            jax.ShapeDtypeStruct((T, D), F32),
            jax.ShapeDtypeStruct((T, f), BF16),
            jax.ShapeDtypeStruct((T, f), BF16),
        ),
        grid_spec=pltpu.PrefetchScalarGridSpec(
            num_scalar_prefetch=1,
            grid=(D // dt,),
            in_specs=[pl.BlockSpec((rows, f), lambda d, *_: (0, inner))] * n
            + [pl.BlockSpec((2 * rows, f), lambda d, *_: (0, inner))] * n
            + [weight, weight, keep, keep]
            + ([] if first else [gx]),
            out_specs=[gx, whole((T, f)), whole((T, f))],
            scratch_shapes=[pltpu.VMEM(((n_row + 1) * rows, f), BF16)],
        ),
        input_output_aliases={} if first else {len(args): 0},
        compiler_params=params(),
        cost_estimate=pl.CostEstimate(
            flops=4 * T * D * f, bytes_accessed=4 * D * f + 8 * T * D, transcendentals=T * f
        ),
        name="grad_x_part",
    )(*args, *([] if first else [total]))


def weight_kernel(first, tok_ref, dg_ref, du_ref, kg_ref, ku_ref, *refs):
    gg_ref, gu_ref = refs[-2:]
    tok = tok_ref[...]
    dims = (((0,), (0,)), ((), ()))
    gg = lax.dot_general(tok, dg_ref[...], dims, preferred_element_type=F32)
    gg_ref[...] = masked(gg, kg_ref[...]).astype(BF16)
    gu = lax.dot_general(tok, du_ref[...], dims, preferred_element_type=F32)
    gu_ref[...] = masked(gu, ku_ref[...]).astype(BF16)


def weight_grads(tok_all, d_gate, d_up, keep_gate, keep_up, held, at, f, dt):
    T, D = tok_all.shape
    F = keep_gate.shape[1]
    col = at // f
    first = held is None
    keep = pl.BlockSpec((dt // TILE, f), lambda d: (d, col))
    out = pl.BlockSpec((dt, f), lambda d: (d, col))
    return pl.pallas_call(
        functools.partial(weight_kernel, first),
        out_shape=(jax.ShapeDtypeStruct((D, F), BF16),) * 2,
        grid=(D // dt,),
        in_specs=[pl.BlockSpec((T, dt), lambda d: (0, d)), whole((T, f)), whole((T, f)), keep, keep]
        + ([] if first else [pl.BlockSpec(memory_space=pl.ANY)] * 2),
        out_specs=[out, out],
        input_output_aliases={} if first else {5: 0, 6: 1},
        compiler_params=params(),
        cost_estimate=pl.CostEstimate(
            flops=4 * T * D * f, bytes_accessed=4 * D * f + 2 * T * D, transcendentals=0
        ),
        name="grad_gate_up",
    )(tok_all, d_gate, d_up, keep_gate, keep_up, *([] if first else held))


class Queue:
    def __init__(self, perm):
        self.perm, self.flying = perm, [(), ()]

    def hold(self, *deps):
        self.flying[0] = (*self.flying[0], *deps)

    def issue(self, x):
        wait = self.flying.pop(0)
        if wait:
            x, *_ = lax.optimization_barrier((x, *wait))
        x = lax.ppermute(x, "row", self.perm)
        self.flying.append((x,))
        return x


class Four:
    def __init__(self, me):
        self.me = me
        self.outer = Queue([(0, 1), (1, 0), (2, 3), (3, 2)])
        self.inner = Queue([(1, 2), (2, 1), (0, 0), (3, 3)])
        self.mid = (me == 1) | (me == 2)
        self.side = me // 2
        near, far = jnp.where(self.side == 0, 2, 1), jnp.where(self.side == 0, 3, 0)
        self.where = jnp.stack(
            [
                me,
                me ^ 1,
                jnp.where(self.mid, near, 4),
                jnp.where(self.mid, far, 4),
                jnp.where(self.mid, 4, near),
                jnp.where(self.mid, 4, far),
            ]
        ).astype(jnp.int32)


class Gather:
    def __init__(self, four, piece):
        self.four, self.own = four, piece

    def swap(self):
        self.next = self.four.outer.issue(self.own)

    def cross(self):
        self.near = self.four.inner.issue(self.own)

    def cross_next(self):
        self.far = self.four.inner.issue(self.next)

    def spread(self, outwards=None):
        send = self.near if outwards is None else jnp.where(self.four.mid, self.near, outwards)
        self.near_out = self.four.outer.issue(send)

    def spread_next(self):
        self.far_out = self.four.outer.issue(self.far)

    def pieces(self):
        return [self.own, self.next, self.near, self.far, self.near_out, self.far_out]


class Reduce:
    def __init__(self, four, part):
        self.four, self.part = four, part
        self.rows = part.shape[0] // 4

    def block(self, b, count=1):
        return lax.dynamic_slice_in_dim(self.part, b * self.rows, count * self.rows, 0)

    def others(self):
        return self.block(2 - 2 * self.four.side, 2)

    def cross(self, from_end):
        send = (self.others() + from_end.astype(F32)).astype(BF16)
        self.crossed = self.four.inner.issue(send)

    def crossed_block(self, b):
        got = lax.dynamic_slice_in_dim(self.crossed, (b % 2) * self.rows, self.rows, 0)
        return jnp.where(self.four.mid, got.astype(F32), 0.0)

    def swap(self):
        other = self.four.me ^ 1
        self.swapped = self.four.outer.issue(
            (self.block(other) + self.crossed_block(other)).astype(BF16)
        )

    def result(self):
        me = self.four.me
        return (self.block(me) + self.crossed_block(me) + self.swapped.astype(F32)).astype(BF16)


def ring_gather(piece, n):
    ring = [(i, (i + 1) % n) for i in range(n)]
    pieces = [piece]
    for _ in range(1, n):
        pieces.append(lax.ppermute(pieces[-1], "row", ring))
    return pieces


def ring_reduce(part, n, me):
    ring = [(i, (i + 1) % n) for i in range(n)]
    rows = part.shape[0] // n
    total = None
    for s in range(n):
        block = lax.dynamic_slice_in_dim(part, (me + n - 1 - s) % n * rows, rows, 0)
        total = block if total is None else block + total.astype(F32)
        total = total.astype(BF16)
        if s < n - 1:
            total = lax.ppermute(total, "row", ring)
    return total


def pairs_gather(piece, n, in_turn=False):
    got = [piece]
    for k in range(1, n // 2):
        send = lax.optimization_barrier((piece, got[-1]))[0] if in_turn else piece
        got.append(lax.ppermute(send, "col", [(i, i ^ (2 * k)) for i in range(n)]))
    return jnp.stack(got)


def pair_gather(mine, n, me):
    half, rows, width = mine.shape
    core, pair = me % 2, me // 2
    other = lax.ppermute(mine, "col", [(i, i ^ 1) for i in range(n)])
    even, odd = jnp.where(core == 0, mine, other), jnp.where(core == 0, other, mine)
    both = jnp.stack([even, odd], axis=1)
    ordered = [lax.dynamic_index_in_dim(both, pair ^ k, 0, keepdims=False) for k in range(half)]
    return jnp.stack(ordered).reshape(n * rows, width)


def pair_sums(part, n, me):
    rows = part.shape[0] // n
    core = me % 2
    blocks = part.reshape(n // 2, 2, rows, part.shape[1])
    send = lax.dynamic_index_in_dim(blocks, 1 - core, 1, keepdims=False)
    keep = lax.dynamic_index_in_dim(blocks, core, 1, keepdims=False)
    return keep + lax.ppermute(send, "col", [(i, i ^ 1) for i in range(n)])


def pair_reduce(summed, n, me):
    half = n // 2
    pair = me // 2
    total = lax.dynamic_index_in_dim(summed, pair, 0, keepdims=False)
    low = summed.astype(BF16)
    got = [
        lax.ppermute(
            lax.dynamic_index_in_dim(low, pair ^ k, 0, keepdims=False),
            "col",
            [(i, i ^ (2 * k)) for i in range(n)],
        )
        for k in range(1, half)
    ]
    for g in got:
        total = total + g.astype(F32)
    return total


def lanes(mask):
    return jnp.repeat(mask.astype(F32), TILE, axis=1)


def per_device(
    n_row,
    n_col,
    tokens,
    out_grad,
    gate_pre,
    up_pre,
    w_gate,
    w_up,
    w_down,
    mask_gate,
    mask_up,
    mask_down,
):
    row, col = lax.axis_index("row"), lax.axis_index("col")
    F, D = w_down.shape
    ft = 512 if F % 512 == 0 else 256
    dt = min(512, D)
    keep_gate, keep_up, keep_down = lanes(mask_gate), lanes(mask_up), lanes(mask_down)
    keep_down = keep_down.reshape(F // ft, ft // TILE, D)

    n_tiles = F // ft
    cut = (n_tiles + 1) // 2 * ft
    spans = ((0, cut), (cut, F - cut))
    own = [
        jnp.concatenate([gate_pre[:, a : a + f], up_pre[:, a : a + f]], axis=0) for a, f in spans
    ]

    def chunked(which):
        start, width = spans[which]
        return [(start, at, min(2 * ft, width - at)) for at in range(0, width, 2 * ft)]

    def use(chunk, pieces, pairs, total):
        start, at, f = chunk
        total, d_gate, d_up = input_grad(
            where, pieces, pairs, w_gate, w_up, keep_gate, keep_up, total, start, at, f, n_row, dt
        )
        return total, (d_gate, d_up, start + at, f)

    def weights(job, held):
        d_gate, d_up, at, f = job
        return weight_grads(tok_all, d_gate, d_up, keep_gate, keep_up, held, at, f, dt)

    def down(which, pairs, grad_down):
        start, width = spans[which]
        return down_grad(
            where, pairs, grad_all, keep_down, grad_down, start, width, n_row, ft
        )

    if n_row != 4:
        where = jnp.stack([(row - s) % n_row for s in range(n_row)]).astype(jnp.int32)
        grad_all = pair_gather(pairs_gather(out_grad, n_col), n_col, col)
        tok_all = pair_gather(pairs_gather(tokens, n_col), n_col, col)
        total = held = grad_down = None
        for which, part in enumerate(dhidden_part(grad_all, w_down, keep_down, cut, ft)):
            pairs = ring_gather(own[which], n_row)
            pieces = ring_gather(ring_reduce(part, n_row, row), n_row)
            for chunk in chunked(which):
                total, job = use(chunk, pieces, pairs, total)
                held = weights(job, held)
            grad_down = down(which, pairs, grad_down)
        grad_x = pair_reduce(pair_sums(total, n_col, col), n_col, col).astype(BF16)
        return (grad_x, held[0], held[1], grad_down)

    def after(x, *deps):
        return lax.optimization_barrier((x, *deps))[0]

    four = Four(row)
    where = four.where
    outer, inner = four.outer, four.inner
    a, b = Gather(four, own[0]), Gather(four, own[1])
    b.swap()
    a.cross()
    mine = pairs_gather(out_grad, n_col)
    grad_all = pair_gather(after(mine, b.next, a.near, keep_down), n_col, col)
    a.swap()
    b.cross()
    low, high = dhidden_part(grad_all, w_down, keep_down, cut, ft)
    sum_a, sum_b = Reduce(four, low), Reduce(four, high)
    inner.hold(high)
    a.cross_next()
    a.spread(sum_a.others().astype(BF16))
    tok_mine = pairs_gather(after(tokens, a.far), n_col, True)
    b.spread(sum_b.others().astype(BF16))
    sum_a.cross(a.near_out)
    a.spread_next()
    sum_b.cross(b.near_out)
    outer.hold(a.far_out)
    sum_a.swap()
    b.cross_next()
    grad_down = down(0, a.pieces(), None)
    sum_b.swap()
    tok_all = pair_gather(tok_mine, n_col, col)
    h_a = Gather(four, sum_a.result())
    inner.hold(grad_down)
    h_a.cross()
    h_a.swap()
    outer.hold(tok_all)
    h_a.spread()
    h_a.cross_next()
    h_b = Gather(four, sum_b.result())
    h_b.cross()
    h_a.spread_next()
    h_b.swap()
    b.spread_next()
    h_b.cross_next()
    total = held = None
    first, second = chunked(0), chunked(1)
    jobs = []
    later = [h_b.spread, h_b.spread_next]
    for c in first:
        total, job = use(c, h_a.pieces(), a.pieces(), total)
        jobs.append(job)
        outer.hold(total)
        if later:
            later.pop(0)()
    for step in later:
        step()
    for job in jobs:
        held = weights(job, held)
    total = after(total, held[0])
    jobs = []
    for c in second:
        total, job = use(c, h_b.pieces(), b.pieces(), total)
        jobs.append(job)
    summed = pair_sums(total, n_col, col)
    held = weights(jobs[0], held)
    grad_x = pair_reduce(summed, n_col, col).astype(BF16)
    for job in jobs[1:]:
        held = weights((after(job[0], summed), *job[1:]), held)
    pieces = b.pieces()
    pieces[0] = after(pieces[0], summed)
    grad_down = down(1, pieces, grad_down)
    return (grad_x, held[0], held[1], grad_down)


def solution(mesh):
    return jax.shard_map(
        functools.partial(per_device, mesh.shape["row"], mesh.shape["col"]),
        mesh=mesh,
        in_specs=(
            P("col", "row"),
            P("col", "row"),
            P("row", "col"),
            P("row", "col"),
            P("row", "col"),
            P("row", "col"),
            P("col", "row"),
            P("row", "col"),
            P("row", "col"),
            P("col", "row"),
        ),
        out_specs=(P("col", "row"), P("row", "col"), P("row", "col"), P("col", "row")),
        check_vma=False,
    )
```

time: 550 us -> 346 us (0.63)
  waiting for transfers between devices: 281 us -> 71.8 us
  Pallas kernels: 0 us -> 135 us
  local copies, waits for them, and re-layouts: 126 us -> 20.9 us
  matrix products: 98.1 us -> 0 us
  starting transfers between devices: 0.45 us -> 86.9 us
  between operations: 14.3 us -> 1.2 us
    reduce_scatter x2 -> x0, waiting for transfers between devices: 181 us -> none  [the longest x1 142 us: per_device(): lax.psum_scatter(contract_last(grad_all, down_eff), 'row', scatter_dimens...]
    pallas_call x0 -> x11, Pallas kernels: none -> 135 us  [the longest x4 57.4 us: input_grad(): pl.pallas_call(functools.partial(input_kernel, n, rows, first), out_shape...]
    dot_general x6 -> x0, matrix products: 98.1 us -> none  [the longest x3 52.2 us: contract_first(): lax.dot_general(left, right, (((0,), (0,)), ((), ())), preferred_element_...]
    all_gather x5 -> x0, waiting for transfers between devices: 97.7 us -> none  [the longest x1 65.2 us: per_device(): lax.all_gather(d_up, 'row', axis=0, tiled=True)]
    unnamed x29 -> x68, local copies, waits for them, and re-layouts: 97 us -> 4.1 us
    ppermute x0 -> x36, starting transfers between devices: none -> 86.9 us  [the longest x24 75.2 us: issue(): x = lax.ppermute(x, 'row', self.perm)]
    ppermute x0 -> x36, waiting for transfers between devices: none -> 71.8 us  [the longest x24 64.4 us: issue(): x = lax.ppermute(x, 'row', self.perm)]
    mul x2 -> x0, other arithmetic: 21.3 us -> none  [the longest x1 15.4 us: per_device(): gate_eff = w_gate * keep_gate]
  transfers between devices with their start and end apart: 7 -> 36, of which waited for: 6 -> 10; matrix products, arithmetic and copies ran while one was open for 41% -> 10% of each run, Pallas kernels for 0% -> 31%
where the time goes in v1:
time: 346 us; the launch traced here: 343 us
  Pallas kernels  135 us (39%)
  starting transfers between devices  86.9 us (25%)
  waiting for transfers between devices  71.8 us (21%)
  other arithmetic  27.3 us (8%)
  local copies, waits for them, and re-layouts  20.9 us (6%)
    ppermute x24, starting transfers between devices, issue(): x = lax.ppermute(x, 'row', self.perm)  75.2 us
    ppermute x24, waiting for transfers between devices, issue(): x = lax.ppermute(x, 'row', self.perm)  64.4 us
    pallas_call x4, Pallas kernels, input_grad(): pl.pallas_call(functools.partial(input_kernel, n, rows, first), out_shape...  57.4 us
    pallas_call x4, Pallas kernels, weight_grads(): pl.pallas_call(functools.partial(weight_kernel, first), out_shape=(jax.Sh...  37.6 us
    pallas_call x2, Pallas kernels, down_grad(): pl.pallas_call(functools.partial(down_kernel, n, rows // 2), out_shape=ja...  23.8 us
    pallas_call x1, Pallas kernels, dhidden_part(): pl.pallas_call(functools.partial(dhidden_kernel, cut // ft), out_shape=(j...  15.8 us
    ppermute x6, starting transfers between devices, pairs_gather(): got.append(lax.ppermute(send, 'col', [(i, i ^ 2 * k) for i in range(n)]))  8.06 us
    ppermute x6, waiting for transfers between devices, pairs_gather(): got.append(lax.ppermute(send, 'col', [(i, i ^ 2 * k) for i in range(n)]))  7.41 us
  transfers between devices with their start and end apart: 36, of which 10 were waited for; matrix products, arithmetic and copies ran while one was open for 10% of the time, Pallas kernels for 31%

profile of v1, /device:TPU:0, one launch (start us, length us, event | category | flops | bytes accessed | tf_op | source)
XLA Modules:
  0.0 342.8 jit_solution(10740876059440894520)
XLA Ops:
  0.7 1.0 slice-done.2
  3.4 1.0 pad_maximum_fusion.5.refs_6_.refs_0_
  4.4 5.3 %collective-permute-start.3 = (bf16[288,1536]{1,0:T(8,128)(2,1)}, bf16[288,1536]{1,0:T(8,128)(2,1)S(1)}, u32[]{:S(2)}, u32[]{:S(2)}) collective-permute-start(bf16[288,1536]{1,0:T(8,128)(2,1)} %pad_maximum_fusion.5.refs_6_.refs_0_), channel_id=1, source_target_pairs={{0,8},{8,0},{16,24},{24,16},{1,9},{9,1},{17,25},{25,17},{2,10},{10... | collective-permute-start | bytes 2654216 | tf_op jit(solution)/shard_map/ppermute | solution.py:235
  9.7 1.5 collective-permute-start
  11.2 1.5 collective-permute-start.1
  13.8 2.0 broadcast_in_dim.19
  15.8 2.3 reshape_reshape.3.keep_ref.refs_7_
  18.1 1.6 collective-permute-done
  19.7 5.8 %collective-permute-done.1 = bf16[72,2048]{1,0:T(8,128)(2,1)} collective-permute-done((bf16[72,2048]{1,0:T(8,128)(2,1)S(1)}, bf16[72,2048]{1,0:T(8,128)(2,1)}, u32[]{:S(2)}, u32[]{:S(2)}) %collective-permute-start.1) | collective-permute-done | bytes 294944 | tf_op jit(solution)/shard_map/ppermute | solution.py:339
  25.5 2.3 pad_maximum_fusion.2
  27.8 1.4 collective-permute-done.3.refs_7_.refs_1_
  29.3 8.3 %collective-permute-start.6 = (bf16[288,1536]{1,0:T(8,128)(2,1)}, bf16[288,1536]{1,0:T(8,128)(2,1)}, u32[]{:S(2)}, u32[]{:S(2)}) collective-permute-start(bf16[288,1536]{1,0:T(8,128)(2,1)} %pad_maximum_fusion.5.refs_6_.refs_0_), channel_id=1, source_target_pairs={{8,16},{16,8},{0,0},{24,24},{9,17},{17,9},{1,1},{25,25},{10,18},{1... | collective-permute-start | bytes 2654216 | tf_op jit(solution)/shard_map/ppermute | solution.py:235
  38.3 1.8 select_bitcast_fusion.2
  40.7 1.6 copy.25
  42.2 15.8 %dhidden.1 = (f32[576,2048]{1,0:T(8,128)}, f32[576,1536]{1,0:T(8,128)}) custom-call(bf16[576,2048]{1,0:T(8,128)(2,1)} %bitcast.52, bf16[3584,2048]{1,0:T(8,128)(2,1)} %w_ref.1, f32[7,8,2048]{2,1,0:T(8,128)} %reshape_reshape.3.keep_ref.refs_7_), custom_call_target="tpu_custom_call" | custom-call | flops 8455716864 | bytes 22937600 | tf_op jit(solution)/shard_map/dhidden/pallas_call | solution.py:50
  58.1 2.1 fusion
  60.2 1.3 collective-permute-start.11
  61.6 4.9 %collective-permute-done.7.refs_1_.refs_7_ = bf16[288,2048]{1,0:T(8,128)(2,1)} collective-permute-done((bf16[288,2048]{1,0:T(8,128)(2,1)S(1)}, bf16[288,2048]{1,0:T(8,128)(2,1)}, u32[]{:S(2)}, u32[]{:S(2)}) %collective-permute-start.7) | collective-permute-done | bytes 1179680 | tf_op jit(solution)/shard_map/ppermute | solution.py:235
  66.4 1.9 collective-permute-start.9
  68.4 1.7 fusion.1
  70.1 1.6 collective-permute-start.8
  71.6 20.0 %collective-permute-done.11.refs_4_.refs_10_ = bf16[288,2048]{1,0:T(8,128)(2,1)S(1)} collective-permute-done((bf16[288,2048]{1,0:T(8,128)(2,1)S(1)}, bf16[288,2048]{1,0:T(8,128)(2,1)S(1)}, u32[]{:S(2)}, u32[]{:S(2)}) %collective-permute-start.11) | collective-permute-done | bytes 1179680 | tf_op jit(solution)/shard_map/ppermute | solution.py:235
  91.6 1.4 add_convert_fusion
  93.0 10.4 %collective-permute-start.14 = (bf16[288,2048]{1,0:T(8,128)(2,1)}, bf16[288,2048]{1,0:T(8,128)(2,1)}, u32[]{:S(2)}, u32[]{:S(2)}) collective-permute-start(bf16[288,2048]{1,0:T(8,128)(2,1)} %add_convert_fusion), channel_id=1, source_target_pairs={{8,16},{16,8},{0,0},{24,24},{9,17},{17,9},{1,1},{25,25},{10,18},{1... | collective-permute-start | bytes 3538952 | tf_op jit(solution)/shard_map/ppermute | solution.py:235
  103.4 1.6 collective-permute-start.17
  105.0 5.6 %collective-permute-done.8.refs_10_.refs_4_ = bf16[288,1536]{1,0:T(8,128)(2,1)S(1)} collective-permute-done((bf16[288,1536]{1,0:T(8,128)(2,1)S(1)}, bf16[288,1536]{1,0:T(8,128)(2,1)S(1)}, u32[]{:S(2)}, u32[]{:S(2)}) %collective-permute-start.8) | collective-permute-done | bytes 884768 | tf_op jit(solution)/shard_map/ppermute | solution.py:235
  110.6 1.2 add_convert_fusion.1
  111.8 1.6 collective-permute-start.18
  113.4 8.2 %collective-permute-start.10 = (bf16[288,1536]{1,0:T(8,128)(2,1)}, bf16[288,1536]{1,0:T(8,128)(2,1)}, u32[]{:S(2)}, u32[]{:S(2)}) collective-permute-start(bf16[288,1536]{1,0:T(8,128)(2,1)} %add_convert_fusion.1), channel_id=1, source_target_pairs={{8,16},{16,8},{0,0},{24,24},{9,17},{17,9},{1,1},{25,25},{10,18},{1... | collective-permute-start | bytes 2654216 | tf_op jit(solution)/shard_map/ppermute | solution.py:235
  121.6 1.4 collective-permute-start.19
  123.0 2.4 add_convert_fusion.3
  125.4 10.0 %collective-permute-done.12.refs_5_.refs_11_ = bf16[288,2048]{1,0:T(8,128)(2,1)S(1)} collective-permute-done((bf16[288,2048]{1,0:T(8,128)(2,1)S(1)}, bf16[288,2048]{1,0:T(8,128)(2,1)S(1)}, u32[]{:S(2)}, u32[]{:S(2)}) %collective-permute-start.12) | collective-permute-done | bytes 1179680 | tf_op jit(solution)/shard_map/ppermute | solution.py:235
  136.7 2.2 pad_maximum_fusion.4
  139.6 2.2 add_convert_fusion.5
  142.5 4.2 %collective-permute-start.13 = (bf16[144,1536]{1,0:T(8,128)(2,1)}, bf16[144,1536]{1,0:T(8,128)(2,1)}, u32[]{:S(2)}, u32[]{:S(2)}) collective-permute-start(bf16[144,1536]{1,0:T(8,128)(2,1)} %add_convert_fusion.5), channel_id=1, source_target_pairs={{0,8},{8,0},{16,24},{24,16},{1,9},{9,1},{17,25},{25,17},{2,10},{10... | collective-permute-start | bytes 1327112 | tf_op jit(solution)/shard_map/ppermute | solution.py:235
  146.7 5.3 %collective-permute-done.15 = bf16[144,2048]{1,0:T(8,128)(2,1)} collective-permute-done((bf16[144,2048]{1,0:T(8,128)(2,1)}, bf16[144,2048]{1,0:T(8,128)(2,1)}, u32[]{:S(2)}, u32[]{:S(2)}) %collective-permute-start.15) | collective-permute-done | bytes 589856 | tf_op jit(solution)/shard_map/ppermute | solution.py:235
  152.0 1.8 add_convert_fusion.2.refs_0_
  154.5 13.0 %grad_down.2.refs_8_ = bf16[3584,2048]{1,0:T(8,128)(2,1)} custom-call(s32[6]{0:T(128)} %stack.89.at_ref, bf16[288,2048]{1,0:T(8,128)(2,1)} %copy-done, bf16[288,2048]{1,0:T(8,128)(2,1)} %collective-permute-done.7.refs_1_.refs_7_, bf16[288,2048]{1,0:T(8,128)(2,1)} %copy-done.2, bf16[288,2048]{1,0:T(8,128)(2,1)} %copy-done.4, bf16[288,2048]{1,0:T(8,128)(2,1)} %copy-done.1, ...), custom_call_target="tpu_custom_call" | custom-call | flops 4831838208 | bytes 24903680 | tf_op jit(solution)/shard_map/grad_down/pallas_call | solution.py:108
  168.2 1.5 select_bitcast_fusion
  169.7 3.0 collective-permute-done.24.refs_1_
  172.7 1.5 collective-permute-start.26
  174.7 1.8 copy.26
  176.5 10.6 %collective-permute-start.21 = (bf16[144,2048]{1,0:T(8,128)(2,1)S(1)}, bf16[144,2048]{1,0:T(8,128)(2,1)S(1)}, u32[]{:S(2)}, u32[]{:S(2)}) collective-permute-start(bf16[144,2048]{1,0:T(8,128)(2,1)S(1)} %collective-permute-done.16.refs_2_), channel_id=1, source_target_pairs={{0,8},{8,0},{16,24},{24,16},{1,9},{9,1},{17,25},{25,17},{2,10},{10... | collective-permute-start | bytes 1769480 | tf_op jit(solution)/shard_map/ppermute | solution.py:235
  187.1 8.9 %collective-permute-start.28 = (bf16[144,2048]{1,0:T(8,128)(2,1)}, bf16[144,2048]{1,0:T(8,128)(2,1)S(1)}, u32[]{:S(2)}, u32[]{:S(2)}) collective-permute-start(bf16[144,2048]{1,0:T(8,128)(2,1)} %collective-permute-done.26.refs_3_), channel_id=1, source_target_pairs={{0,8},{8,0},{16,24},{24,16},{1,9},{9,1},{17,25},{25,17},{2,10},{10... | collective-permute-start | bytes 1769480 | tf_op jit(solution)/shard_map/ppermute | solution.py:235
  196.1 1.6 add_convert_fusion.4.refs_0_
  198.6 1.1 collective-permute-start.22
  200.0 1.0 reshape.25.refs_14_.kg_ref
  201.3 1.0 reshape.26.refs_15_.ku_ref
  203.0 14.1 %collective-permute-done.22.refs_1_ = bf16[144,1536]{1,0:T(8,128)(2,1)S(1)} collective-permute-done((bf16[144,1536]{1,0:T(8,128)(2,1)S(1)}, bf16[144,1536]{1,0:T(8,128)(2,1)S(1)}, u32[]{:S(2)}, u32[]{:S(2)}) %collective-permute-start.22) | collective-permute-done | bytes 442400 | tf_op jit(solution)/shard_map/ppermute | solution.py:235
  218.8 14.9 %grad_x_part.4 = (f32[576,2048]{1,0:T(8,128)}, bf16[576,1024]{1,0:T(8,128)(2,1)}, bf16[576,1024]{1,0:T(8,128)(2,1)}) custom-call(s32[6]{0:T(128)} %stack.89.at_ref, bf16[144,2048]{1,0:T(8,128)(2,1)} %copy-done.12, bf16[144,2048]{1,0:T(8,128)(2,1)} %copy-done.14, bf16[144,2048]{1,0:T(8,128)(2,1)} %copy-done.15, ...), custom_call_target="tpu_custom_call" | custom-call | flops 4831838208 | bytes 17825792 | tf_op jit(solution)/shard_map/grad_x_part/pallas_call | solution.py:165
  233.7 4.2 %collective-permute-start.30 = (bf16[288,1536]{1,0:T(8,128)(2,1)S(1)}, bf16[288,1536]{1,0:T(8,128)(2,1)S(1)}, u32[]{:S(2)}, u32[]{:S(2)}) collective-permute-start(bf16[288,1536]{1,0:T(8,128)(2,1)S(1)} %collective-permute-done.25.refs_9_.refs_3_), channel_id=1, source_target_pairs={{0,8},{8,0},{16,24},{24,16},{1,9},{9,1},{17,25},{25,17},{2,10},{10... | collective-permute-start | bytes 2654216 | tf_op jit(solution)/shard_map/ppermute | solution.py:235
  238.0 10.2 %grad_gate_up.4 = (bf16[2048,3584]{1,0:T(8,128)(2,1)}, bf16[2048,3584]{1,0:T(8,128)(2,1)}) custom-call(bf16[576,2048]{1,0:T(8,128)(2,1)} %bitcast.48, bf16[576,1024]{1,0:T(8,128)(2,1)} %get-tuple-element.85.dg_ref, bf16[576,1024]{1,0:T(8,128)(2,1)} %get-tuple-element.86.du_ref, f32[32,3584]{1,0:T(8,128)} %reshape.25.refs_14_.kg_ref, ...), custom_call_target="tpu_custom_call" | custom-call | flops 4831838208 | bytes 10747904 | tf_op jit(solution)/shard_map/grad_gate_up/pallas_call | solution.py:208
  248.3 15.7 %grad_x_part.5 = (f32[576,2048]{1,0:T(8,128)}, bf16[576,1024]{1,0:T(8,128)(2,1)}, bf16[576,1024]{1,0:T(8,128)(2,1)}) custom-call(s32[6]{0:T(128)} %stack.89.at_ref, bf16[144,2048]{1,0:T(8,128)(2,1)} %copy-done.12, bf16[144,2048]{1,0:T(8,128)(2,1)} %copy-done.14, bf16[144,2048]{1,0:T(8,128)(2,1)} %copy-done.15, ...), custom_call_target="tpu_custom_call", output_to_operand_aliasing={{0}: (17, {})} | custom-call | flops 4831838208 | bytes 17825792 | tf_op jit(solution)/shard_map/grad_x_part/pallas_call | solution.py:165
  264.0 2.0 collective-permute-start.31
  266.0 10.2 %grad_gate_up.5 = (bf16[2048,3584]{1,0:T(8,128)(2,1)}, bf16[2048,3584]{1,0:T(8,128)(2,1)}) custom-call(bf16[576,2048]{1,0:T(8,128)(2,1)} %bitcast.49, bf16[576,1024]{1,0:T(8,128)(2,1)} %get-tuple-element.83.dg_ref, bf16[576,1024]{1,0:T(8,128)(2,1)} %get-tuple-element.84.du_ref, ...), custom_call_target="tpu_custom_call", output_to_operand_aliasing={{0}: (5, {}), {1}: (6, {})} | custom-call | flops 4831838208 | bytes 10747904 | tf_op jit(solution)/shard_map/grad_gate_up/pallas_call | solution.py:208
  277.8 16.1 %grad_x_part.6 = (f32[576,2048]{1,0:T(8,128)}, bf16[576,1024]{1,0:T(8,128)(2,1)}, bf16[576,1024]{1,0:T(8,128)(2,1)}) custom-call(s32[6]{0:T(128)} %stack.89.at_ref, bf16[144,1536]{1,0:T(8,128)(2,1)} %copy-done.13, bf16[144,1536]{1,0:T(8,128)(2,1)} %copy-done.18, bf16[144,1536]{1,0:T(8,128)(2,1)} %copy-done.19, ...), custom_call_target="tpu_custom_call", output_to_operand_aliasing={{0}: (17, {})} | custom-call | flops 4831838208 | bytes 17825792 | tf_op jit(solution)/shard_map/grad_x_part/pallas_call | solution.py:165
  293.9 10.8 %grad_x_part.7 = (f32[576,2048]{1,0:T(8,128)}, bf16[576,512]{1,0:T(8,128)(2,1)}, bf16[576,512]{1,0:T(8,128)(2,1)}) custom-call(s32[6]{0:T(128)} %stack.89.at_ref, bf16[144,1536]{1,0:T(8,128)(2,1)} %copy-done.13, bf16[144,1536]{1,0:T(8,128)(2,1)} %copy-done.18, bf16[144,1536]{1,0:T(8,128)(2,1)} %copy-done.19, ...), custom_call_target="tpu_custom_call", output_to_operand_aliasing={{0}: (17, {})} | custom-call | flops 2415919104 | bytes 13631488 | tf_op jit(solution)/shard_map/grad_x_part/pallas_call | solution.py:165
  304.7 3.4 dynamic-slice_bitcast_fusion
  308.1 10.4 %grad_gate_up.6 = (bf16[2048,3584]{1,0:T(8,128)(2,1)}, bf16[2048,3584]{1,0:T(8,128)(2,1)}) custom-call(bf16[576,2048]{1,0:T(8,128)(2,1)} %bitcast.50, bf16[576,1024]{1,0:T(8,128)(2,1)} %get-tuple-element.96.dg_ref, bf16[576,1024]{1,0:T(8,128)(2,1)} %get-tuple-element.97.du_ref, ...), custom_call_target="tpu_custom_call", output_to_operand_aliasing={{0}: (5, {}), {1}: (6, {})} | custom-call | flops 4831838208 | bytes 10747904 | tf_op jit(solution)/shard_map/grad_gate_up/pallas_call | solution.py:208
  318.5 2.2 fusion.13
  320.9 1.6 collective-permute-start.33
  322.4 1.5 collective-permute-start.34
  324.4 6.7 %grad_gate_up.7 = (bf16[2048,3584]{1,0:T(8,128)(2,1)}, bf16[2048,3584]{1,0:T(8,128)(2,1)}) custom-call(bf16[576,2048]{1,0:T(8,128)(2,1)} %bitcast.51, bf16[576,512]{1,0:T(8,128)(2,1)} %get-tuple-element.94.dg_ref, bf16[576,512]{1,0:T(8,128)(2,1)} %get-tuple-element.95.du_ref, ...), custom_call_target="tpu_custom_call", output_to_operand_aliasing={{0}: (5, {}), {1}: (6, {})} | custom-call | flops 2415919104 | bytes 6553600 | tf_op jit(solution)/shard_map/grad_gate_up/pallas_call | solution.py:208
  331.1 10.8 %grad_down.3 = bf16[3584,2048]{1,0:T(8,128)(2,1)} custom-call(s32[6]{0:T(128)} %stack.89.at_ref, bf16[288,1536]{1,0:T(8,128)(2,1)} %pad_maximum_fusion.5.refs_6_.refs_0_, bf16[288,1536]{1,0:T(8,128)(2,1)} %copy-done.6, bf16[288,1536]{1,0:T(8,128)(2,1)} %collective-permute-done.6.refs_8_.refs_2_, ...), custom_call_target="tpu_custom_call", output_to_operand_aliasing={{}: (9, {})} | custom-call | flops 3623878656 | bytes 18677760 | tf_op jit(solution)/shard_map/grad_down/pallas_call | solution.py:108
  (131 shorter events, 15.6 us)
Async XLA Ops:
  1.9 1.5 slice-start.5
  2.0 35.6 %copy-start = (bf16[288,2048]{1,0:T(8,128)(2,1)}, bf16[288,2048]{1,0:T(8,128)(2,1)S(1)}, u32[]{:S(2)}) copy-start(bf16[288,2048]{1,0:T(8,128)(2,1)S(1)} %pad_maximum_fusion.3.refs_0_.refs_6_) | copy-start | bytes 3538948
  2.0 7.7 %copy-start.28 = (bf16[72,2048]{1,0:T(8,128)(2,1)S(1)}, bf16[72,2048]{1,0:T(8,128)(2,1)}, u32[]{:S(2)}) copy-start(bf16[72,2048]{1,0:T(8,128)(2,1)} %param.11) | copy-start | bytes 884740
  2.0 11.2 %copy-start.29 = (s32[56,32]{0,1:T(8,128)S(1)}, s32[56,32]{0,1:T(8,128)}, u32[]{:S(2)}) copy-start(s32[56,32]{0,1:T(8,128)} %param.19) | copy-start | bytes 21508
  2.0 27.2 %collective-permute-start.4 = (bf16[288,2048]{1,0:T(8,128)(2,1)S(1)}, bf16[288,2048]{1,0:T(8,128)(2,1)S(1)}, u32[]{:S(2)}, u32[]{:S(2)}) collective-permute-start(bf16[288,2048]{1,0:T(8,128)(2,1)S(1)} %pad_maximum_fusion.3.refs_0_.refs_6_), channel_id=1, source_target_pairs={{8,16},{16,8},{0,0},{24,24},{9,17},{17,9},{1,1},{25,25},{10,18},{1... | collective-permute-start | bytes 3538952 | tf_op jit(solution)/shard_map/ppermute | solution.py:235
  4.4 24.9 %collective-permute-start.3 = (bf16[288,1536]{1,0:T(8,128)(2,1)}, bf16[288,1536]{1,0:T(8,128)(2,1)S(1)}, u32[]{:S(2)}, u32[]{:S(2)}) collective-permute-start(bf16[288,1536]{1,0:T(8,128)(2,1)} %pad_maximum_fusion.5.refs_6_.refs_0_), channel_id=1, source_target_pairs={{0,8},{8,0},{16,24},{24,16},{1,9},{9,1},{17,25},{25,17},{2,10},{10... | collective-permute-start | bytes 2654216 | tf_op jit(solution)/shard_map/ppermute | solution.py:235
  9.7 10.1 %collective-permute-start = (bf16[72,2048]{1,0:T(8,128)(2,1)S(1)}, bf16[72,2048]{1,0:T(8,128)(2,1)}, u32[]{:S(2)}, u32[]{:S(2)}) collective-permute-start(bf16[72,2048]{1,0:T(8,128)(2,1)S(1)} %copy-done.28), channel_id=1, source_target_pairs={{0,2},{1,3},{2,0},{3,1},{4,6},{5,7},{6,4},{7,5},{8,10},{9,11},{10,... | collective-permute-start | bytes 884744 | tf_op jit(solution)/shard_map/ppermute | solution.py:339
  11.2 14.3 %collective-permute-start.1 = (bf16[72,2048]{1,0:T(8,128)(2,1)S(1)}, bf16[72,2048]{1,0:T(8,128)(2,1)}, u32[]{:S(2)}, u32[]{:S(2)}) collective-permute-start(bf16[72,2048]{1,0:T(8,128)(2,1)S(1)} %copy-done.28), channel_id=1, source_target_pairs={{0,4},{1,5},{2,6},{3,7},{4,0},{5,1},{6,2},{7,3},{8,12},{9,13},{10,... | collective-permute-start | bytes 884744 | tf_op jit(solution)/shard_map/ppermute | solution.py:339
  12.7 12.8 %collective-permute-start.2 = (bf16[72,2048]{1,0:T(8,128)(2,1)S(1)}, bf16[72,2048]{1,0:T(8,128)(2,1)}, u32[]{:S(2)}, u32[]{:S(2)}) collective-permute-start(bf16[72,2048]{1,0:T(8,128)(2,1)S(1)} %copy-done.28), channel_id=1, source_target_pairs={{0,6},{1,7},{2,4},{3,5},{4,2},{5,3},{6,0},{7,1},{8,14},{9,15},{10,... | collective-permute-start | bytes 884744 | tf_op jit(solution)/shard_map/ppermute | solution.py:339
  29.2 10.9 %copy-start.6 = (bf16[288,1536]{1,0:T(8,128)(2,1)}, bf16[288,1536]{1,0:T(8,128)(2,1)S(1)}, u32[]{:S(2)}) copy-start(bf16[288,1536]{1,0:T(8,128)(2,1)S(1)} %collective-permute-done.3.refs_7_.refs_1_) | copy-start | bytes 2654212
  29.2 28.8 %copy-start.2 = (bf16[288,2048]{1,0:T(8,128)(2,1)}, bf16[288,2048]{1,0:T(8,128)(2,1)S(1)}, u32[]{:S(2)}) copy-start(bf16[288,2048]{1,0:T(8,128)(2,1)S(1)} %collective-permute-done.4.refs_2_.refs_8_) | copy-start | bytes 3538948
  29.2 9.1 %collective-permute-start.5 = (bf16[4,72,2048]{2,1,0:T(8,128)(2,1)}, bf16[4,72,2048]{2,1,0:T(8,128)(2,1)}, u32[]{:S(2)}, u32[]{:S(2)}) collective-permute-start(bf16[4,72,2048]{2,1,0:T(8,128)(2,1)} %pad_maximum_fusion.2), channel_id=1, source_target_pairs={{0,1},{1,0},{2,3},{3,2},{4,5},{5,4},{6,7},{7,6},{8,9},{9,8},{10,11... | collective-permute-start | bytes 3538952 | tf_op jit(solution)/shard_map/ppermute | solution.py:346
  29.3 39.0 %collective-permute-start.6 = (bf16[288,1536]{1,0:T(8,128)(2,1)}, bf16[288,1536]{1,0:T(8,128)(2,1)}, u32[]{:S(2)}, u32[]{:S(2)}) collective-permute-start(bf16[288,1536]{1,0:T(8,128)(2,1)} %pad_maximum_fusion.5.refs_6_.refs_0_), channel_id=1, source_target_pairs={{8,16},{16,8},{0,0},{24,24},{9,17},{17,9},{1,1},{25,25},{10,18},{1... | collective-permute-start | bytes 2654216 | tf_op jit(solution)/shard_map/ppermute | solution.py:235
  37.6 28.9 %collective-permute-start.7 = (bf16[288,2048]{1,0:T(8,128)(2,1)S(1)}, bf16[288,2048]{1,0:T(8,128)(2,1)}, u32[]{:S(2)}, u32[]{:S(2)}) collective-permute-start(bf16[288,2048]{1,0:T(8,128)(2,1)S(1)} %pad_maximum_fusion.3.refs_0_.refs_6_), channel_id=1, source_target_pairs={{0,8},{8,0},{16,24},{24,16},{1,9},{9,1},{17,25},{25,17},{2,10},{10... | collective-permute-start | bytes 3538952 | tf_op jit(solution)/shard_map/ppermute | solution.py:235
  58.1 33.6 %copy-start.10 = (f32[576,2048]{1,0:T(8,128)S(1)}, f32[576,2048]{1,0:T(8,128)}, u32[]{:S(2)}) copy-start(f32[576,2048]{1,0:T(8,128)} %get-tuple-element.59) | copy-start | bytes 14155780
  60.2 31.4 %collective-permute-start.11 = (bf16[288,2048]{1,0:T(8,128)(2,1)S(1)}, bf16[288,2048]{1,0:T(8,128)(2,1)S(1)}, u32[]{:S(2)}, u32[]{:S(2)}) collective-permute-start(bf16[288,2048]{1,0:T(8,128)(2,1)S(1)} %fusion), channel_id=1, source_target_pairs={{0,8},{8,0},{16,24},{24,16},{1,9},{9,1},{17,25},{25,17},{2,10},{10... | collective-permute-start | bytes 3538952 | tf_op jit(solution)/shard_map/ppermute | solution.py:235
  66.4 37.0 %collective-permute-start.9 = (bf16[288,2048]{1,0:T(8,128)(2,1)}, bf16[288,2048]{1,0:T(8,128)(2,1)S(1)}, u32[]{:S(2)}, u32[]{:S(2)}) collective-permute-start(bf16[288,2048]{1,0:T(8,128)(2,1)} %collective-permute-done.7.refs_1_.refs_7_), channel_id=1, source_target_pairs={{8,16},{16,8},{0,0},{24,24},{9,17},{17,9},{1,1},{25,25},{10,18},{1... | collective-permute-start | bytes 3538952 | tf_op jit(solution)/shard_map/ppermute | solution.py:235
  70.1 33.4 %copy-start.23 = (bf16[72,2048]{1,0:T(8,128)(2,1)S(1)}, bf16[72,2048]{1,0:T(8,128)(2,1)}, u32[]{:S(2)}) copy-start(bf16[72,2048]{1,0:T(8,128)(2,1)} %param.10) | copy-start | bytes 884740
  70.1 40.5 %copy-start.11 = (f32[576,1536]{1,0:T(8,128)S(1)}, f32[576,1536]{1,0:T(8,128)}, u32[]{:S(2)}) copy-start(f32[576,1536]{1,0:T(8,128)} %get-tuple-element.55) | copy-start | bytes 10616836
  70.1 40.5 %collective-permute-start.8 = (bf16[288,1536]{1,0:T(8,128)(2,1)S(1)}, bf16[288,1536]{1,0:T(8,128)(2,1)S(1)}, u32[]{:S(2)}, u32[]{:S(2)}) collective-permute-start(bf16[288,1536]{1,0:T(8,128)(2,1)S(1)} %fusion.1), channel_id=1, source_target_pairs={{0,8},{8,0},{16,24},{24,16},{1,9},{9,1},{17,25},{25,17},{2,10},{10... | collective-permute-start | bytes 2654216 | tf_op jit(solution)/shard_map/ppermute | solution.py:235
  93.0 30.0 %collective-permute-start.14 = (bf16[288,2048]{1,0:T(8,128)(2,1)}, bf16[288,2048]{1,0:T(8,128)(2,1)}, u32[]{:S(2)}, u32[]{:S(2)}) collective-permute-start(bf16[288,2048]{1,0:T(8,128)(2,1)} %add_convert_fusion), channel_id=1, source_target_pairs={{8,16},{16,8},{0,0},{24,24},{9,17},{17,9},{1,1},{25,25},{10,18},{1... | collective-permute-start | bytes 3538952 | tf_op jit(solution)/shard_map/ppermute | solution.py:235
  103.4 8.3 %copy-start.4 = (bf16[288,2048]{1,0:T(8,128)(2,1)}, bf16[288,2048]{1,0:T(8,128)(2,1)S(1)}, u32[]{:S(2)}) copy-start(bf16[288,2048]{1,0:T(8,128)(2,1)S(1)} %collective-permute-done.9.refs_3_.refs_9_) | copy-start | bytes 3538948
  103.4 32.0 %collective-permute-start.12 = (bf16[288,2048]{1,0:T(8,128)(2,1)S(1)}, bf16[288,2048]{1,0:T(8,128)(2,1)S(1)}, u32[]{:S(2)}, u32[]{:S(2)}) collective-permute-start(bf16[288,2048]{1,0:T(8,128)(2,1)S(1)} %collective-permute-done.9.refs_3_.refs_9_), channel_id=1, source_target_pairs={{0,8},{8,0},{16,24},{24,16},{1,9},{9,1},{17,25},{25,17},{2,10},{10... | collective-permute-start | bytes 3538952 | tf_op jit(solution)/shard_map/ppermute | solution.py:235
  103.4 8.3 %collective-permute-start.17 = (bf16[72,2048]{1,0:T(8,128)(2,1)S(1)}, bf16[72,2048]{1,0:T(8,128)(2,1)S(1)}, u32[]{:S(2)}, u32[]{:S(2)}) collective-permute-start(bf16[72,2048]{1,0:T(8,128)(2,1)S(1)} %copy-done.23), channel_id=1, source_target_pairs={{0,2},{1,3},{2,0},{3,1},{4,6},{5,7},{6,4},{7,5},{8,10},{9,11},{10,... | collective-permute-start | bytes 884744 | tf_op jit(solution)/shard_map/ppermute | solution.py:339
  111.8 9.8 %collective-permute-start.18 = (bf16[72,2048]{1,0:T(8,128)(2,1)S(1)}, bf16[72,2048]{1,0:T(8,128)(2,1)S(1)}, u32[]{:S(2)}, u32[]{:S(2)}) collective-permute-start(bf16[72,2048]{1,0:T(8,128)(2,1)S(1)} %copy-done.23), channel_id=1, source_target_pairs={{0,4},{1,5},{2,6},{3,7},{4,0},{5,1},{6,2},{7,3},{8,12},{9,13},{10,... | collective-permute-start | bytes 884744 | tf_op jit(solution)/shard_map/ppermute | solution.py:339
  113.4 26.2 %collective-permute-start.10 = (bf16[288,1536]{1,0:T(8,128)(2,1)}, bf16[288,1536]{1,0:T(8,128)(2,1)}, u32[]{:S(2)}, u32[]{:S(2)}) collective-permute-start(bf16[288,1536]{1,0:T(8,128)(2,1)} %add_convert_fusion.1), channel_id=1, source_target_pairs={{8,16},{16,8},{0,0},{24,24},{9,17},{17,9},{1,1},{25,25},{10,18},{1... | collective-permute-start | bytes 2654216 | tf_op jit(solution)/shard_map/ppermute | solution.py:235
  121.6 14.4 %copy-start.24 = (bf16[72,2048]{1,0:T(8,128)(2,1)}, bf16[72,2048]{1,0:T(8,128)(2,1)S(1)}, u32[]{:S(2)}) copy-start(bf16[72,2048]{1,0:T(8,128)(2,1)S(1)} %collective-permute-done.18) | copy-start | bytes 884740
  121.6 14.3 %collective-permute-start.19 = (bf16[72,2048]{1,0:T(8,128)(2,1)S(1)}, bf16[72,2048]{1,0:T(8,128)(2,1)S(1)}, u32[]{:S(2)}, u32[]{:S(2)}) collective-permute-start(bf16[72,2048]{1,0:T(8,128)(2,1)S(1)} %copy-done.23), channel_id=1, source_target_pairs={{0,6},{1,7},{2,4},{3,5},{4,2},{5,3},{6,0},{7,1},{8,14},{9,15},{10,... | collective-permute-start | bytes 884744 | tf_op jit(solution)/shard_map/ppermute | solution.py:339
  135.5 6.3 %copy-start.5 = (bf16[288,2048]{1,0:T(8,128)(2,1)}, bf16[288,2048]{1,0:T(8,128)(2,1)S(1)}, u32[]{:S(2)}) copy-start(bf16[288,2048]{1,0:T(8,128)(2,1)S(1)} %collective-permute-done.12.refs_5_.refs_11_) | copy-start | bytes 3538948
  135.5 16.5 %collective-permute-start.15 = (bf16[144,2048]{1,0:T(8,128)(2,1)}, bf16[144,2048]{1,0:T(8,128)(2,1)}, u32[]{:S(2)}, u32[]{:S(2)}) collective-permute-start(bf16[144,2048]{1,0:T(8,128)(2,1)} %add_convert_fusion.3), channel_id=1, source_target_pairs={{0,8},{8,0},{16,24},{24,16},{1,9},{9,1},{17,25},{25,17},{2,10},{10... | collective-permute-start | bytes 1769480 | tf_op jit(solution)/shard_map/ppermute | solution.py:235
  136.7 5.1 %copy-start.7 = (bf16[288,1536]{1,0:T(8,128)(2,1)S(1)}, bf16[288,1536]{1,0:T(8,128)(2,1)}, u32[]{:S(2)}) copy-start(bf16[288,1536]{1,0:T(8,128)(2,1)} %copy-done.6) | copy-start | bytes 2654212
  138.9 29.3 %collective-permute-start.20 = (bf16[4,72,2048]{2,1,0:T(8,128)(2,1)}, bf16[4,72,2048]{2,1,0:T(8,128)(2,1)}, u32[]{:S(2)}, u32[]{:S(2)}) collective-permute-start(bf16[4,72,2048]{2,1,0:T(8,128)(2,1)} %pad_maximum_fusion.4), channel_id=1, source_target_pairs={{0,1},{1,0},{2,3},{3,2},{4,5},{5,4},{6,7},{7,6},{8,9},{9,8},{10,11... | collective-permute-start | bytes 3538952 | tf_op jit(solution)/shard_map/ppermute | solution.py:346
  141.8 28.0 %collective-permute-start.25 = (bf16[288,1536]{1,0:T(8,128)(2,1)S(1)}, bf16[288,1536]{1,0:T(8,128)(2,1)S(1)}, u32[]{:S(2)}, u32[]{:S(2)}) collective-permute-start(bf16[288,1536]{1,0:T(8,128)(2,1)S(1)} %copy-done.7), channel_id=1, source_target_pairs={{8,16},{16,8},{0,0},{24,24},{9,17},{17,9},{1,1},{25,25},{10,18},{1... | collective-permute-start | bytes 2654216 | tf_op jit(solution)/shard_map/ppermute | solution.py:235
  142.5 34.0 %collective-permute-start.13 = (bf16[144,1536]{1,0:T(8,128)(2,1)}, bf16[144,1536]{1,0:T(8,128)(2,1)}, u32[]{:S(2)}, u32[]{:S(2)}) collective-permute-start(bf16[144,1536]{1,0:T(8,128)(2,1)} %add_convert_fusion.5), channel_id=1, source_target_pairs={{0,8},{8,0},{16,24},{24,16},{1,9},{9,1},{17,25},{25,17},{2,10},{10... | collective-permute-start | bytes 1327112 | tf_op jit(solution)/shard_map/ppermute | solution.py:235
  153.8 13.6 %copy-start.12 = (bf16[144,2048]{1,0:T(8,128)(2,1)}, bf16[144,2048]{1,0:T(8,128)(2,1)S(1)}, u32[]{:S(2)}) copy-start(bf16[144,2048]{1,0:T(8,128)(2,1)S(1)} %add_convert_fusion.2.refs_0_) | copy-start | bytes 1769476
  153.8 14.3 %copy-start.25 = (bf16[72,2048]{1,0:T(8,128)(2,1)S(1)}, bf16[72,2048]{1,0:T(8,128)(2,1)}, u32[]{:S(2)}) copy-start(bf16[72,2048]{1,0:T(8,128)(2,1)} %copy-done.24) | copy-start | bytes 884740
  153.9 14.3 %copy-start.27 = (bf16[72,2048]{1,0:T(8,128)(2,1)S(1)}, bf16[72,2048]{1,0:T(8,128)(2,1)}, u32[]{:S(2)}) copy-start(bf16[72,2048]{1,0:T(8,128)(2,1)} %copy-done.26) | copy-start | bytes 884740
  153.9 18.9 %collective-permute-start.24 = (bf16[144,2048]{1,0:T(8,128)(2,1)S(1)}, bf16[144,2048]{1,0:T(8,128)(2,1)S(1)}, u32[]{:S(2)}, u32[]{:S(2)}) collective-permute-start(bf16[144,2048]{1,0:T(8,128)(2,1)S(1)} %add_convert_fusion.2.refs_0_), channel_id=1, source_target_pairs={{0,8},{8,0},{16,24},{24,16},{1,9},{9,1},{17,25},{25,17},{2,10},{10... | collective-permute-start | bytes 1769480 | tf_op jit(solution)/shard_map/ppermute | solution.py:235
  167.5 9.0 %collective-permute-start.16 = (bf16[144,2048]{1,0:T(8,128)(2,1)S(1)}, bf16[144,2048]{1,0:T(8,128)(2,1)S(1)}, u32[]{:S(2)}, u32[]{:S(2)}) collective-permute-start(bf16[144,2048]{1,0:T(8,128)(2,1)S(1)} %add_convert_fusion.2.refs_0_), channel_id=1, source_target_pairs={{8,16},{16,8},{0,0},{24,24},{9,17},{17,9},{1,1},{25,25},{10,18},{1... | collective-permute-start | bytes 1769480 | tf_op jit(solution)/shard_map/ppermute | solution.py:235
  169.7 64.0 %copy-start.8 = (bf16[288,1536]{1,0:T(8,128)(2,1)}, bf16[288,1536]{1,0:T(8,128)(2,1)S(1)}, u32[]{:S(2)}) copy-start(bf16[288,1536]{1,0:T(8,128)(2,1)S(1)} %collective-permute-done.25.refs_9_.refs_3_) | copy-start | bytes 2654212
  172.7 1.7 copy-start.14
  172.7 14.4 %collective-permute-start.26 = (bf16[144,2048]{1,0:T(8,128)(2,1)S(1)}, bf16[144,2048]{1,0:T(8,128)(2,1)}, u32[]{:S(2)}, u32[]{:S(2)}) collective-permute-start(bf16[144,2048]{1,0:T(8,128)(2,1)S(1)} %collective-permute-done.24.refs_1_), channel_id=1, source_target_pairs={{8,16},{16,8},{0,0},{24,24},{9,17},{17,9},{1,1},{25,25},{10,18},{1... | collective-permute-start | bytes 1769480 | tf_op jit(solution)/shard_map/ppermute | solution.py:235
  176.5 23.2 %copy-start.30 = (s32[32,56]{1,0:T(8,128)S(1)}, s32[32,56]{1,0:T(8,128)}, u32[]{:S(2)}) copy-start(s32[32,56]{1,0:T(8,128)} %param.17) | copy-start | bytes 21508
  176.5 21.2 %copy-start.15 = (bf16[144,2048]{1,0:T(8,128)(2,1)}, bf16[144,2048]{1,0:T(8,128)(2,1)S(1)}, u32[]{:S(2)}) copy-start(bf16[144,2048]{1,0:T(8,128)(2,1)S(1)} %collective-permute-done.16.refs_2_) | copy-start | bytes 1769476
  176.5 24.5 %copy-start.31 = (s32[32,56]{1,0:T(8,128)S(1)}, s32[32,56]{1,0:T(8,128)}, u32[]{:S(2)}) copy-start(s32[32,56]{1,0:T(8,128)} %param.18) | copy-start | bytes 21508
  176.5 21.1 %collective-permute-start.21 = (bf16[144,2048]{1,0:T(8,128)(2,1)S(1)}, bf16[144,2048]{1,0:T(8,128)(2,1)S(1)}, u32[]{:S(2)}, u32[]{:S(2)}) collective-permute-start(bf16[144,2048]{1,0:T(8,128)(2,1)S(1)} %collective-permute-done.16.refs_2_), channel_id=1, source_target_pairs={{0,8},{8,0},{16,24},{24,16},{1,9},{9,1},{17,25},{25,17},{2,10},{10... | collective-permute-start | bytes 1769480 | tf_op jit(solution)/shard_map/ppermute | solution.py:235
  187.1 30.8 %collective-permute-start.28 = (bf16[144,2048]{1,0:T(8,128)(2,1)}, bf16[144,2048]{1,0:T(8,128)(2,1)S(1)}, u32[]{:S(2)}, u32[]{:S(2)}) collective-permute-start(bf16[144,2048]{1,0:T(8,128)(2,1)} %collective-permute-done.26.refs_3_), channel_id=1, source_target_pairs={{0,8},{8,0},{16,24},{24,16},{1,9},{9,1},{17,25},{25,17},{2,10},{10... | collective-permute-start | bytes 1769480 | tf_op jit(solution)/shard_map/ppermute | solution.py:235
  197.7 4.7 %copy-start.13 = (bf16[144,1536]{1,0:T(8,128)(2,1)}, bf16[144,1536]{1,0:T(8,128)(2,1)S(1)}, u32[]{:S(2)}) copy-start(bf16[144,1536]{1,0:T(8,128)(2,1)S(1)} %add_convert_fusion.4.refs_0_) | copy-start | bytes 1327108
  198.6 18.5 %collective-permute-start.22 = (bf16[144,1536]{1,0:T(8,128)(2,1)S(1)}, bf16[144,1536]{1,0:T(8,128)(2,1)S(1)}, u32[]{:S(2)}, u32[]{:S(2)}) collective-permute-start(bf16[144,1536]{1,0:T(8,128)(2,1)S(1)} %add_convert_fusion.4.refs_0_), channel_id=1, source_target_pairs={{0,8},{8,0},{16,24},{24,16},{1,9},{9,1},{17,25},{25,17},{2,10},{10... | collective-permute-start | bytes 1327112 | tf_op jit(solution)/shard_map/ppermute | solution.py:235
  202.3 31.4 %collective-permute-start.23 = (bf16[144,1536]{1,0:T(8,128)(2,1)S(1)}, bf16[144,1536]{1,0:T(8,128)(2,1)S(1)}, u32[]{:S(2)}, u32[]{:S(2)}) collective-permute-start(bf16[144,1536]{1,0:T(8,128)(2,1)S(1)} %add_convert_fusion.4.refs_0_), channel_id=1, source_target_pairs={{8,16},{16,8},{0,0},{24,24},{9,17},{17,9},{1,1},{25,25},{10,18},{1... | collective-permute-start | bytes 1327112 | tf_op jit(solution)/shard_map/ppermute | solution.py:235
  217.1 16.6 %copy-start.18 = (bf16[144,1536]{1,0:T(8,128)(2,1)}, bf16[144,1536]{1,0:T(8,128)(2,1)S(1)}, u32[]{:S(2)}) copy-start(bf16[144,1536]{1,0:T(8,128)(2,1)S(1)} %collective-permute-done.22.refs_1_) | copy-start | bytes 1327108
  217.1 46.8 %collective-permute-start.27 = (bf16[144,1536]{1,0:T(8,128)(2,1)S(1)}, bf16[144,1536]{1,0:T(8,128)(2,1)S(1)}, u32[]{:S(2)}, u32[]{:S(2)}) collective-permute-start(bf16[144,1536]{1,0:T(8,128)(2,1)S(1)} %collective-permute-done.22.refs_1_), channel_id=1, source_target_pairs={{8,16},{16,8},{0,0},{24,24},{9,17},{17,9},{1,1},{25,25},{10,18},{1... | collective-permute-start | bytes 1327112 | tf_op jit(solution)/shard_map/ppermute | solution.py:235
  233.7 14.5 %copy-start.19 = (bf16[144,1536]{1,0:T(8,128)(2,1)}, bf16[144,1536]{1,0:T(8,128)(2,1)S(1)}, u32[]{:S(2)}) copy-start(bf16[144,1536]{1,0:T(8,128)(2,1)S(1)} %collective-permute-done.23.refs_2_) | copy-start | bytes 1327108
  233.7 30.2 %collective-permute-start.30 = (bf16[288,1536]{1,0:T(8,128)(2,1)S(1)}, bf16[288,1536]{1,0:T(8,128)(2,1)S(1)}, u32[]{:S(2)}, u32[]{:S(2)}) collective-permute-start(bf16[288,1536]{1,0:T(8,128)(2,1)S(1)} %collective-permute-done.25.refs_9_.refs_3_), channel_id=1, source_target_pairs={{0,8},{8,0},{16,24},{24,16},{1,9},{9,1},{17,25},{25,17},{2,10},{10... | collective-permute-start | bytes 2654216 | tf_op jit(solution)/shard_map/ppermute | solution.py:235
  237.9 38.3 %collective-permute-start.29 = (bf16[144,1536]{1,0:T(8,128)(2,1)S(1)}, bf16[144,1536]{1,0:T(8,128)(2,1)S(1)}, u32[]{:S(2)}, u32[]{:S(2)}) collective-permute-start(bf16[144,1536]{1,0:T(8,128)(2,1)S(1)} %collective-permute-done.23.refs_2_), channel_id=1, source_target_pairs={{0,8},{8,0},{16,24},{24,16},{1,9},{9,1},{17,25},{25,17},{2,10},{10... | collective-permute-start | bytes 1327112 | tf_op jit(solution)/shard_map/ppermute | solution.py:235
  264.0 12.3 %copy-start.20 = (bf16[144,1536]{1,0:T(8,128)(2,1)}, bf16[144,1536]{1,0:T(8,128)(2,1)S(1)}, u32[]{:S(2)}) copy-start(bf16[144,1536]{1,0:T(8,128)(2,1)S(1)} %collective-permute-done.27.refs_3_) | copy-start | bytes 1327108
  264.0 12.3 %copy-start.9 = (bf16[288,1536]{1,0:T(8,128)(2,1)}, bf16[288,1536]{1,0:T(8,128)(2,1)S(1)}, u32[]{:S(2)}) copy-start(bf16[288,1536]{1,0:T(8,128)(2,1)S(1)} %collective-permute-done.30.refs_11_.refs_5_) | copy-start | bytes 2654212
  264.0 12.3 %collective-permute-start.31 = (bf16[144,1536]{1,0:T(8,128)(2,1)S(1)}, bf16[144,1536]{1,0:T(8,128)(2,1)S(1)}, u32[]{:S(2)}, u32[]{:S(2)}) collective-permute-start(bf16[144,1536]{1,0:T(8,128)(2,1)S(1)} %collective-permute-done.27.refs_3_), channel_id=1, source_target_pairs={{0,8},{8,0},{16,24},{24,16},{1,9},{9,1},{17,25},{25,17},{2,10},{10... | collective-permute-start | bytes 1327112 | tf_op jit(solution)/shard_map/ppermute | solution.py:235
  304.7 13.8 %slice-start = ((s8[4718592]{0:T(1024)(128)(4,1)}), s8[524288]{0:T(1024)(128)(4,1)S(1)}, s32[]{:S(2)}) async-start(s8[4718592]{0:T(1024)(128)(4,1)} %bitcast.45), calls=%async_computation | async-start | bytes 1048576
  308.1 10.4 %collective-permute-start.32 = (f32[4,72,2048]{2,1,0:T(8,128)}, f32[4,72,2048]{2,1,0:T(8,128)}, u32[]{:S(2)}, u32[]{:S(2)}) collective-permute-start(f32[4,72,2048]{2,1,0:T(8,128)} %dynamic-slice_bitcast_fusion), channel_id=1, source_target_pairs={{0,1},{1,0},{2,3},{3,2},{4,5},{5,4},{6,7},{7,6},{8,9},{9,8},{10,11... | collective-permute-start | bytes 7077896 | tf_op jit(solution)/shard_map/ppermute | solution.py:359
  308.1 10.4 %slice-start.1 = ((s8[4718592]{0:T(1024)(128)(4,1)}), s8[4194304]{0:T(1024)(128)(4,1)S(1)}, s32[]{:S(2)}) async-start(s8[4718592]{0:T(1024)(128)(4,1)} %bitcast.45), calls=%async_computation.1 | async-start | bytes 8388608
  320.9 21.0 %collective-permute-start.33 = (bf16[72,2048]{1,0:T(8,128)(2,1)S(1)}, bf16[72,2048]{1,0:T(8,128)(2,1)S(1)}, u32[]{:S(2)}, u32[]{:S(2)}) collective-permute-start(bf16[72,2048]{1,0:T(8,128)(2,1)S(1)} %get-tuple-element.118), channel_id=1, source_target_pairs={{0,2},{1,3},{2,0},{3,1},{4,6},{5,7},{6,4},{7,5},{8,10},{9,11},{10,... | collective-permute-start | bytes 884744 | tf_op jit(solution)/shard_map/ppermute | solution.py:368
  322.4 19.5 %collective-permute-start.34 = (bf16[72,2048]{1,0:T(8,128)(2,1)S(1)}, bf16[72,2048]{1,0:T(8,128)(2,1)S(1)}, u32[]{:S(2)}, u32[]{:S(2)}) collective-permute-start(bf16[72,2048]{1,0:T(8,128)(2,1)S(1)} %get-tuple-element.120), channel_id=1, source_target_pairs={{0,4},{1,5},{2,6},{3,7},{4,0},{5,1},{6,2},{7,3},{8,12},{9,13},{10,... | collective-permute-start | bytes 884744 | tf_op jit(solution)/shard_map/ppermute | solution.py:368
  323.9 18.0 %collective-permute-start.35 = (bf16[72,2048]{1,0:T(8,128)(2,1)S(1)}, bf16[72,2048]{1,0:T(8,128)(2,1)S(1)}, u32[]{:S(2)}, u32[]{:S(2)}) collective-permute-start(bf16[72,2048]{1,0:T(8,128)(2,1)S(1)} %get-tuple-element.119), channel_id=1, source_target_pairs={{0,6},{1,7},{2,4},{3,5},{4,2},{5,3},{6,0},{7,1},{8,14},{9,15},{10,... | collective-permute-start | bytes 884744 | tf_op jit(solution)/shard_map/ppermute | solution.py:368
  (10 other events, 10.0 us)

commit v2 on v1

--- a/solution.py
+++ b/solution.py
@@ -29,43 +29,32 @@
     return jnp.concatenate(rows, axis=0)
 
 
-def dhidden_kernel(n_low, grad_ref, w_ref, keep_ref, low_ref, high_ref):
+def dhidden_kernel(grad_ref, w_ref, keep_ref, out_ref):
     w_eff = masked(w_ref[...], keep_ref[0].astype(BF16))
-    out = lax.dot_general(
+    out_ref[...] = lax.dot_general(
         grad_ref[...], w_eff, (((1,), (1,)), ((), ())), preferred_element_type=F32
     )
 
-    @pl.when(pl.program_id(0) < n_low)
-    def _():
-        low_ref[...] = out
-
-    @pl.when(pl.program_id(0) >= n_low)
-    def _():
-        high_ref[...] = out
-
-
-def dhidden_part(grad_all, w_down, keep_down, cut, ft):
+
+def dhidden_part(grad_all, w_down, keep_down, span, ft):
     T, D = grad_all.shape
-    F = w_down.shape[0]
+    start, width = span
+    here = start // ft
     return pl.pallas_call(
-        functools.partial(dhidden_kernel, cut // ft),
-        out_shape=(
-            jax.ShapeDtypeStruct((T, cut), F32),
-            jax.ShapeDtypeStruct((T, F - cut), F32),
-        ),
-        grid=(F // ft,),
+        dhidden_kernel,
+        out_shape=jax.ShapeDtypeStruct((T, width), F32),
+        grid=(width // ft,),
         in_specs=[
             whole((T, D)),
-            pl.BlockSpec((ft, D), lambda j: (j, 0)),
-            pl.BlockSpec((1, ft // TILE, D), lambda j: (j, 0, 0)),
+            pl.BlockSpec((ft, D), lambda j: (j + here, 0)),
+            pl.BlockSpec((1, ft // TILE, D), lambda j: (j + here, 0, 0)),
         ],
-        out_specs=[
-            pl.BlockSpec((T, ft), lambda j: (0, jnp.minimum(j, cut // ft - 1))),
-            pl.BlockSpec((T, ft), lambda j: (0, jnp.maximum(j - cut // ft, 0))),
-        ],
+        out_specs=pl.BlockSpec((T, ft), lambda j: (0, j)),
         compiler_params=params(),
         cost_estimate=pl.CostEstimate(
-            flops=2 * T * D * F, bytes_accessed=2 * D * F + 4 * T * F, transcendentals=0
+            flops=2 * T * D * width,
+            bytes_accessed=2 * D * width + 4 * T * width,
+            transcendentals=0,
         ),
         name="dhidden",
     )(grad_all, w_down, keep_down)
@@ -132,7 +121,8 @@
     rest = rest[4:]
     if not first:
         sum_ref, rest = rest[0], rest[1:]
-    gx_ref, dg_ref, du_ref, buf = rest
+    gx_ref, dg_ref, du_ref, buf, dg_all, du_all = rest
+    c = pl.program_id(1)
 
     @pl.when(pl.program_id(0) == 0)
     def _():
@@ -140,55 +130,74 @@
         gate = in_order(at_ref, buf, pairs, rows, 0)
         up = in_order(at_ref, buf, pairs, rows, 1)
         gate_val, up_val, sig, silu = gate_parts(gate, up)
-        dg_ref[...] = (d_hidden * up_val * sig * (1.0 + gate_val * (1.0 - sig))).astype(BF16)
-        du_ref[...] = (d_hidden * silu).astype(BF16)
+        d_gate = (d_hidden * up_val * sig * (1.0 + gate_val * (1.0 - sig))).astype(BF16)
+        d_up = (d_hidden * silu).astype(BF16)
+        dg_ref[...] = d_gate
+        du_ref[...] = d_up
+        dg_all[c] = d_gate
+        du_all[c] = d_up
 
     dims = (((1,), (1,)), ((), ()))
     wg = masked(wg_ref[...], kg_ref[...].astype(BF16))
     wu = masked(wu_ref[...], ku_ref[...].astype(BF16))
-    out = lax.dot_general(dg_ref[...], wg, dims, preferred_element_type=F32)
-    out = out + lax.dot_general(du_ref[...], wu, dims, preferred_element_type=F32)
-    gx_ref[...] = out if first else sum_ref[...] + out
-
-
-def input_grad(where, pieces, pairs, w_gate, w_up, keep_gate, keep_up, total, start, at, f, n_row, dt):
-    rows = pieces[0].shape[0]
+    out = lax.dot_general(dg_all[c], wg, dims, preferred_element_type=F32)
+    out = out + lax.dot_general(du_all[c], wu, dims, preferred_element_type=F32)
+
+    @pl.when(c == 0)
+    def _():
+        gx_ref[...] = out if first else sum_ref[...] + out
+
+    @pl.when(c > 0)
+    def _():
+        gx_ref[...] += out
+
+
+def input_grad(where, pieces, pairs, w_gate, w_up, keep_gate, keep_up, total, span, n_row, ft, dt):
+    rows, n = pieces[0].shape[0], len(pieces)
     T = rows * n_row
     D = w_gate.shape[0]
-    n = len(pieces)
-    col, inner = (start + at) // f, at // f
+    start, width = span
+    here, chunks = start // ft, width // ft
     first = total is None
-    weight = pl.BlockSpec((dt, f), lambda d, *_: (d, col))
-    keep = pl.BlockSpec((dt // TILE, f), lambda d, *_: (d, col))
-    gx = pl.BlockSpec((T, dt), lambda d, *_: (0, d))
+
+    def once(d, c):
+        return jnp.where(d == 0, c, chunks - 1)
+
+    piece = pl.BlockSpec((rows, ft), lambda d, c, *_: (0, once(d, c)))
+    pair = pl.BlockSpec((2 * rows, ft), lambda d, c, *_: (0, once(d, c)))
+    tall = pl.BlockSpec((T, ft), lambda d, c, *_: (0, once(d, c)))
+    weight = pl.BlockSpec((dt, ft), lambda d, c, *_: (d, c + here))
+    keep = pl.BlockSpec((dt // TILE, ft), lambda d, c, *_: (d, c + here))
+    gx = pl.BlockSpec((T, dt), lambda d, c, *_: (0, d))
     args = [where, *pieces, *pairs, w_gate, w_up, keep_gate, keep_up]
     return pl.pallas_call(
         functools.partial(input_kernel, n, rows, first),
         out_shape=(
             jax.ShapeDtypeStruct((T, D), F32),
-            jax.ShapeDtypeStruct((T, f), BF16),
-            jax.ShapeDtypeStruct((T, f), BF16),
+            jax.ShapeDtypeStruct((T, width), BF16),
+            jax.ShapeDtypeStruct((T, width), BF16),
         ),
         grid_spec=pltpu.PrefetchScalarGridSpec(
             num_scalar_prefetch=1,
-            grid=(D // dt,),
-            in_specs=[pl.BlockSpec((rows, f), lambda d, *_: (0, inner))] * n
-            + [pl.BlockSpec((2 * rows, f), lambda d, *_: (0, inner))] * n
-            + [weight, weight, keep, keep]
-            + ([] if first else [gx]),
-            out_specs=[gx, whole((T, f)), whole((T, f))],
-            scratch_shapes=[pltpu.VMEM(((n_row + 1) * rows, f), BF16)],
+            grid=(D // dt, chunks),
+            in_specs=[piece] * n + [pair] * n + [weight, weight, keep, keep] + ([] if first else [gx]),
+            out_specs=[gx, tall, tall],
+            scratch_shapes=[
+                pltpu.VMEM(((n_row + 1) * rows, ft), BF16),
+                pltpu.VMEM((chunks, T, ft), BF16),
+                pltpu.VMEM((chunks, T, ft), BF16),
+            ],
         ),
         input_output_aliases={} if first else {len(args): 0},
-        compiler_params=params(),
+        compiler_params=params(2),
         cost_estimate=pl.CostEstimate(
-            flops=4 * T * D * f, bytes_accessed=4 * D * f + 8 * T * D, transcendentals=T * f
+            flops=4 * T * D * width, bytes_accessed=4 * D * width + 8 * T * D, transcendentals=T * width
         ),
         name="grad_x_part",
     )(*args, *([] if first else [total]))
 
 
-def weight_kernel(first, tok_ref, dg_ref, du_ref, kg_ref, ku_ref, *refs):
+def weight_kernel(tok_ref, dg_ref, du_ref, kg_ref, ku_ref, *refs):
     gg_ref, gu_ref = refs[-2:]
     tok = tok_ref[...]
     dims = (((0,), (0,)), ((), ()))
@@ -198,27 +207,28 @@
     gu_ref[...] = masked(gu, ku_ref[...]).astype(BF16)
 
 
-def weight_grads(tok_all, d_gate, d_up, keep_gate, keep_up, held, at, f, dt):
+def weight_grads(tok_all, d_gate, d_up, keep_gate, keep_up, held, span, part, ft):
     T, D = tok_all.shape
     F = keep_gate.shape[1]
-    col = at // f
-    first = held is None
-    keep = pl.BlockSpec((dt // TILE, f), lambda d: (d, col))
-    out = pl.BlockSpec((dt, f), lambda d: (d, col))
+    at, width = part[0] // ft, part[1]
+    here = span[0] // ft + at
+    keep = pl.BlockSpec((D // TILE, ft), lambda c: (0, c + here))
+    out = pl.BlockSpec((D, ft), lambda c: (0, c + here))
+    tall = pl.BlockSpec((T, ft), lambda c: (0, c + at))
     return pl.pallas_call(
-        functools.partial(weight_kernel, first),
+        weight_kernel,
         out_shape=(jax.ShapeDtypeStruct((D, F), BF16),) * 2,
-        grid=(D // dt,),
-        in_specs=[pl.BlockSpec((T, dt), lambda d: (0, d)), whole((T, f)), whole((T, f)), keep, keep]
-        + ([] if first else [pl.BlockSpec(memory_space=pl.ANY)] * 2),
+        grid=(width // ft,),
+        in_specs=[whole((T, D)), tall, tall, keep, keep]
+        + ([] if held is None else [pl.BlockSpec(memory_space=pl.ANY)] * 2),
         out_specs=[out, out],
-        input_output_aliases={} if first else {5: 0, 6: 1},
+        input_output_aliases={} if held is None else {5: 0, 6: 1},
         compiler_params=params(),
         cost_estimate=pl.CostEstimate(
-            flops=4 * T * D * f, bytes_accessed=4 * D * f + 2 * T * D, transcendentals=0
+            flops=4 * T * D * width, bytes_accessed=4 * D * width + 2 * T * D, transcendentals=0
         ),
         name="grad_gate_up",
-    )(tok_all, d_gate, d_up, keep_gate, keep_up, *([] if first else held))
+    )(tok_all, d_gate, d_up, keep_gate, keep_up, *([] if held is None else held))
 
 
 class Queue:
@@ -241,7 +251,7 @@
     def __init__(self, me):
         self.me = me
         self.outer = Queue([(0, 1), (1, 0), (2, 3), (3, 2)])
-        self.inner = Queue([(1, 2), (2, 1), (0, 0), (3, 3)])
+        self.inner = Queue([(1, 2), (2, 1)])
         self.mid = (me == 1) | (me == 2)
         self.side = me // 2
         near, far = jnp.where(self.side == 0, 2, 1), jnp.where(self.side == 0, 3, 0)
@@ -398,7 +408,7 @@
     row, col = lax.axis_index("row"), lax.axis_index("col")
     F, D = w_down.shape
     ft = 512 if F % 512 == 0 else 256
-    dt = min(512, D)
+    dt = min(1024, D)
     keep_gate, keep_up, keep_down = lanes(mask_gate), lanes(mask_up), lanes(mask_down)
     keep_down = keep_down.reshape(F // ft, ft // TILE, D)
 
@@ -409,20 +419,15 @@
         jnp.concatenate([gate_pre[:, a : a + f], up_pre[:, a : a + f]], axis=0) for a, f in spans
     ]
 
-    def chunked(which):
-        start, width = spans[which]
-        return [(start, at, min(2 * ft, width - at)) for at in range(0, width, 2 * ft)]
-
-    def use(chunk, pieces, pairs, total):
-        start, at, f = chunk
-        total, d_gate, d_up = input_grad(
-            where, pieces, pairs, w_gate, w_up, keep_gate, keep_up, total, start, at, f, n_row, dt
+    def use(which, pieces, pairs, total):
+        return input_grad(
+            where, pieces, pairs, w_gate, w_up, keep_gate, keep_up, total, spans[which], n_row, ft, dt
         )
-        return total, (d_gate, d_up, start + at, f)
-
-    def weights(job, held):
-        d_gate, d_up, at, f = job
-        return weight_grads(tok_all, d_gate, d_up, keep_gate, keep_up, held, at, f, dt)
+
+    def weights(which, d_gate, d_up, held, part=None):
+        span = spans[which]
+        part = part or (0, span[1])
+        return weight_grads(tok_all, d_gate, d_up, keep_gate, keep_up, held, span, part, ft)
 
     def down(which, pairs, grad_down):
         start, width = spans[which]
@@ -435,12 +440,12 @@
         grad_all = pair_gather(pairs_gather(out_grad, n_col), n_col, col)
         tok_all = pair_gather(pairs_gather(tokens, n_col), n_col, col)
         total = held = grad_down = None
-        for which, part in enumerate(dhidden_part(grad_all, w_down, keep_down, cut, ft)):
+        for which, span in enumerate(spans):
+            part = dhidden_part(grad_all, w_down, keep_down, span, ft)
             pairs = ring_gather(own[which], n_row)
             pieces = ring_gather(ring_reduce(part, n_row, row), n_row)
-            for chunk in chunked(which):
-                total, job = use(chunk, pieces, pairs, total)
-                held = weights(job, held)
+            total, d_gate, d_up = use(which, pieces, pairs, total)
+            held = weights(which, d_gate, d_up, held)
             grad_down = down(which, pairs, grad_down)
         grad_x = pair_reduce(pair_sums(total, n_col, col), n_col, col).astype(BF16)
         return (grad_x, held[0], held[1], grad_down)
@@ -452,68 +457,63 @@
     where = four.where
     outer, inner = four.outer, four.inner
     a, b = Gather(four, own[0]), Gather(four, own[1])
-    b.swap()
+    a.swap()
     a.cross()
     mine = pairs_gather(out_grad, n_col)
-    grad_all = pair_gather(after(mine, b.next, a.near, keep_down), n_col, col)
-    a.swap()
+    grad_all = pair_gather(after(mine, a.next, a.near, keep_down), n_col, col)
+    b.swap()
     b.cross()
-    low, high = dhidden_part(grad_all, w_down, keep_down, cut, ft)
-    sum_a, sum_b = Reduce(four, low), Reduce(four, high)
-    inner.hold(high)
+    low = dhidden_part(grad_all, w_down, keep_down, spans[0], ft)
+    sum_a = Reduce(four, low)
+    outwards = sum_a.others().astype(BF16)
+    outer.hold(b.next, b.near)
+    a.spread(outwards)
+    sum_b = Reduce(four, dhidden_part(grad_all, w_down, keep_down, spans[1], ft))
+    inner.hold(outwards)
     a.cross_next()
-    a.spread(sum_a.others().astype(BF16))
     tok_mine = pairs_gather(after(tokens, a.far), n_col, True)
-    b.spread(sum_b.others().astype(BF16))
+    b_outwards = sum_b.others().astype(BF16)
+    b.spread(b_outwards)
+    inner.hold(b_outwards)
     sum_a.cross(a.near_out)
+    outer.hold(b.near_out)
     a.spread_next()
+    b.cross_next()
     sum_b.cross(b.near_out)
-    outer.hold(a.far_out)
+    outer.hold(a.far_out, b.far)
     sum_a.swap()
-    b.cross_next()
-    grad_down = down(0, a.pieces(), None)
-    sum_b.swap()
     tok_all = pair_gather(tok_mine, n_col, col)
     h_a = Gather(four, sum_a.result())
-    inner.hold(grad_down)
     h_a.cross()
     h_a.swap()
-    outer.hold(tok_all)
+    sum_b.swap()
+    grad_down = down(0, a.pieces(), None)
+    inner.hold(grad_down, h_a.near)
     h_a.spread()
     h_a.cross_next()
     h_b = Gather(four, sum_b.result())
     h_b.cross()
+    outer.hold(h_a.near_out)
     h_a.spread_next()
+    outer.hold(tok_all)
     h_b.swap()
     b.spread_next()
+    total, d_gate, d_up = use(0, h_a.pieces(), a.pieces(), None)
+    inner.hold(total)
     h_b.cross_next()
-    total = held = None
-    first, second = chunked(0), chunked(1)
-    jobs = []
-    later = [h_b.spread, h_b.spread_next]
-    for c in first:
-        total, job = use(c, h_a.pieces(), a.pieces(), total)
-        jobs.append(job)
-        outer.hold(total)
-        if later:
-            later.pop(0)()
-    for step in later:
-        step()
-    for job in jobs:
-        held = weights(job, held)
+    outer.hold(total)
+    h_b.spread()
+    half = cut // ft // 2 * ft
+    held = weights(0, d_gate, d_up, None, (0, half))
+    outer.hold(held[0])
+    h_b.spread_next()
+    held = weights(0, d_gate, d_up, held, (half, cut - half))
     total = after(total, held[0])
-    jobs = []
-    for c in second:
-        total, job = use(c, h_b.pieces(), b.pieces(), total)
-        jobs.append(job)
+    total, d_gate, d_up = use(1, h_b.pieces(), b.pieces(), total)
     summed = pair_sums(total, n_col, col)
-    held = weights(jobs[0], held)
+    grad_down = down(1, b.pieces(), grad_down)
     grad_x = pair_reduce(summed, n_col, col).astype(BF16)
-    for job in jobs[1:]:
-        held = weights((after(job[0], summed), *job[1:]), held)
-    pieces = b.pieces()
-    pieces[0] = after(pieces[0], summed)
-    grad_down = down(1, pieces, grad_down)
+    held = weights(1, after(d_gate, summed), d_up, held)
     return (grad_x, held[0], held[1], grad_down)
 
 

time: 346 us -> 322 us (0.931)
  starting transfers between devices: 86.9 us -> 67.4 us
  waiting for transfers between devices: 71.8 us -> 80.9 us
  Pallas kernels: 135 us -> 126 us
  other arithmetic: 27.3 us -> 22.8 us
    ppermute x24, starting transfers between devices: 75.2 us -> 54.7 us  [issue(): x = lax.ppermute(x, 'row', self.perm)]
    pallas_call x4 -> x2, Pallas kernels: 57.4 us -> 47 us  [input_grad(): pl.pallas_call(functools.partial(input_kernel, n, rows, first), out_shape...]
    ppermute x6, waiting for transfers between devices: 7.41 us -> 17.2 us  [pairs_gather(): got.append(lax.ppermute(send, 'col', [(i, i ^ 2 * k) for i in range(n)]))]
  transfers between devices with their start and end apart: 36 -> 36, of which waited for: 10 -> 11; matrix products, arithmetic and copies ran while one was open for 10% -> 11% of each run, Pallas kernels for 31% -> 32%
where the time goes in v2:
time: 322 us; the launch traced here: 321 us
  Pallas kernels  126 us (39%)
  waiting for transfers between devices  80.9 us (25%)
  starting transfers between devices  67.4 us (21%)
  local copies, waits for them, and re-layouts  23.1 us (7%)
  other arithmetic  22.8 us (7%)
    ppermute x24, waiting for transfers between devices, issue(): x = lax.ppermute(x, 'row', self.perm)  63.7 us
    ppermute x24, starting transfers between devices, issue(): x = lax.ppermute(x, 'row', self.perm)  54.7 us
    pallas_call x2, Pallas kernels, input_grad(): pl.pallas_call(functools.partial(input_kernel, n, rows, first), out_shape...  47 us
    pallas_call x3, Pallas kernels, weight_grads(): pl.pallas_call(weight_kernel, out_shape=(jax.ShapeDtypeStruct((D, F), BF1...  35.8 us
    pallas_call x2, Pallas kernels, down_grad(): pl.pallas_call(functools.partial(down_kernel, n, rows // 2), out_shape=ja...  24.3 us
    pallas_call x2, Pallas kernels, dhidden_part(): pl.pallas_call(dhidden_kernel, out_shape=jax.ShapeDtypeStruct((T, width),...  18.7 us
    ppermute x6, waiting for transfers between devices, pairs_gather(): got.append(lax.ppermute(send, 'col', [(i, i ^ 2 * k) for i in range(n)]))  17.2 us
    ppermute x6, starting transfers between devices, pairs_gather(): got.append(lax.ppermute(send, 'col', [(i, i ^ 2 * k) for i in range(n)]))  9.01 us
  transfers between devices with their start and end apart: 36, of which 11 were waited for; matrix products, arithmetic and copies ran while one was open for 11% of the time, Pallas kernels for 32%

profile of v2, /device:TPU:0, one launch (start us, length us, event | category | flops | bytes accessed | tf_op | source)
XLA Modules:
  0.0 321.2 jit_solution(6683071135386251770)
XLA Ops:
  0.7 1.0 slice-done.4
  2.0 3.1 collective-permute-start.3
  5.8 1.6 collective-permute-start
  7.4 1.5 collective-permute-start.1
  10.1 2.0 broadcast_in_dim.19
  12.1 2.3 reshape_reshape.3.keep_ref.refs_7_
  14.3 1.8 collective-permute-done
  16.1 6.1 %collective-permute-done.1 = bf16[72,2048]{1,0:T(8,128)(2,1)} collective-permute-done((bf16[72,2048]{1,0:T(8,128)(2,1)}, bf16[72,2048]{1,0:T(8,128)(2,1)}, u32[]{:S(2)}, u32[]{:S(2)}) %collective-permute-start.1) | collective-permute-done | bytes 294944 | tf_op jit(solution)/shard_map/ppermute | solution.py:349
  22.2 2.5 pad_maximum_fusion.2
  24.7 6.4 %collective-permute-done.3.refs_1_.refs_7_ = bf16[288,2048]{1,0:T(8,128)(2,1)S(1)} collective-permute-done((bf16[288,2048]{1,0:T(8,128)(2,1)S(1)}, bf16[288,2048]{1,0:T(8,128)(2,1)S(1)}, u32[]{:S(2)}, u32[]{:S(2)}) %collective-permute-start.3) | collective-permute-done | bytes 1179680 | tf_op jit(solution)/shard_map/ppermute | solution.py:245
  32.9 6.8 %collective-permute-start.7 = (bf16[288,1536]{1,0:T(8,128)(2,1)S(1)}, bf16[288,1536]{1,0:T(8,128)(2,1)}, u32[]{:S(2)}, u32[]{:S(2)}) collective-permute-start(bf16[288,1536]{1,0:T(8,128)(2,1)S(1)} %pad_maximum_fusion.5.refs_6_.refs_0_), channel_id=1, source_target_pairs={{0,8},{8,0},{16,24},{24,16},{1,9},{9,1},{17,25},{25,17},{2,10},{10... | collective-permute-start | bytes 2654216 | tf_op jit(solution)/shard_map/ppermute | solution.py:245
  39.7 1.8 select_bitcast_fusion.2
  42.0 1.6 copy.21
  43.6 9.8 %dhidden.3 = f32[576,2048]{1,0:T(8,128)} custom-call(bf16[576,2048]{1,0:T(8,128)(2,1)} %bitcast.44, bf16[3584,2048]{1,0:T(8,128)(2,1)} %w_ref.3, f32[7,8,2048]{2,1,0:T(8,128)} %reshape_reshape.3.keep_ref.refs_7_), custom_call_target="tpu_custom_call" | custom-call | flops 4831838208 | bytes 13107200 | tf_op jit(solution)/shard_map/dhidden/pallas_call | solution.py:43
  53.4 3.2 broadcast_select_fusion
  57.5 2.3 collective-permute-done.7.refs_7_.refs_1_
  59.8 1.7 collective-permute-start.9
  62.3 8.9 %dhidden.2 = f32[576,1536]{1,0:T(8,128)} custom-call(bf16[576,2048]{1,0:T(8,128)(2,1)} %bitcast.45, bf16[3584,2048]{1,0:T(8,128)(2,1)} %w_ref.3, f32[7,8,2048]{2,1,0:T(8,128)} %reshape_reshape.3.keep_ref.refs_7_), custom_call_target="tpu_custom_call" | custom-call | flops 3623878656 | bytes 9830400 | tf_op jit(solution)/shard_map/dhidden/pallas_call | solution.py:43
  71.1 1.7 broadcast_select_fusion.1
  72.9 2.4 collective-permute-start.8
  75.3 13.6 %collective-permute-done.9.refs_4_.refs_10_ = bf16[288,2048]{1,0:T(8,128)(2,1)S(1)} collective-permute-done((bf16[288,2048]{1,0:T(8,128)(2,1)}, bf16[288,2048]{1,0:T(8,128)(2,1)S(1)}, u32[]{:S(2)}, u32[]{:S(2)}) %collective-permute-start.9) | collective-permute-done | bytes 1179680 | tf_op jit(solution)/shard_map/ppermute | solution.py:245
  88.9 1.4 add_convert_fusion
  90.3 1.7 collective-permute-start.10
  91.9 14.6 %collective-permute-done.8.refs_10_.refs_4_ = bf16[288,1536]{1,0:T(8,128)(2,1)S(1)} collective-permute-done((bf16[288,1536]{1,0:T(8,128)(2,1)S(1)}, bf16[288,1536]{1,0:T(8,128)(2,1)S(1)}, u32[]{:S(2)}, u32[]{:S(2)}) %collective-permute-start.8) | collective-permute-done | bytes 884768 | tf_op jit(solution)/shard_map/ppermute | solution.py:245
  106.5 1.5 collective-permute-start.13
  108.0 1.5 collective-permute-start.20
  109.5 1.6 collective-permute-start.14
  111.1 4.1 %collective-permute-done.20 = bf16[72,2048]{1,0:T(8,128)(2,1)S(1)} collective-permute-done((bf16[72,2048]{1,0:T(8,128)(2,1)S(1)}, bf16[72,2048]{1,0:T(8,128)(2,1)S(1)}, u32[]{:S(2)}, u32[]{:S(2)}) %collective-permute-start.20) | collective-permute-done | bytes 294944 | tf_op jit(solution)/shard_map/ppermute | solution.py:349
  115.2 1.5 collective-permute-start.21
  116.7 5.2 %collective-permute-done.21 = bf16[72,2048]{1,0:T(8,128)(2,1)S(1)} collective-permute-done((bf16[72,2048]{1,0:T(8,128)(2,1)S(1)}, bf16[72,2048]{1,0:T(8,128)(2,1)S(1)}, u32[]{:S(2)}, u32[]{:S(2)}) %collective-permute-start.21) | collective-permute-done | bytes 294944 | tf_op jit(solution)/shard_map/ppermute | solution.py:349
  122.7 2.4 collective-permute-start.22
  125.1 1.2 broadcast_in_dim.22
  126.4 2.2 reshape.25.refs_14_.kg_ref
  128.6 1.2 broadcast_in_dim.23
  129.8 2.2 reshape.26.refs_15_.ku_ref
  132.7 1.7 add_convert_fusion.3
  134.4 3.7 %collective-permute-start.15 = (bf16[144,2048]{1,0:T(8,128)(2,1)S(1)}, bf16[144,2048]{1,0:T(8,128)(2,1)S(1)}, u32[]{:S(2)}, u32[]{:S(2)}) collective-permute-start(bf16[144,2048]{1,0:T(8,128)(2,1)S(1)} %add_convert_fusion.3), channel_id=1, source_target_pairs={{0,8},{8,0},{16,24},{24,16},{1,9},{9,1},{17,25},{25,17},{2,10},{10... | collective-permute-start | bytes 1769480 | tf_op jit(solution)/shard_map/ppermute | solution.py:245
  138.1 2.2 pad_maximum_fusion.4
  140.3 1.1 add_convert_fusion.1
  142.1 5.5 %collective-permute-done.15 = bf16[144,2048]{1,0:T(8,128)(2,1)S(1)} collective-permute-done((bf16[144,2048]{1,0:T(8,128)(2,1)S(1)}, bf16[144,2048]{1,0:T(8,128)(2,1)S(1)}, u32[]{:S(2)}, u32[]{:S(2)}) %collective-permute-start.15) | collective-permute-done | bytes 589856 | tf_op jit(solution)/shard_map/ppermute | solution.py:245
  147.7 1.7 add_convert_fusion.2.refs_0_
  149.3 1.8 collective-permute-start.18
  151.2 1.5 collective-permute-start.17
  152.6 13.0 %grad_down.2.refs_8_ = bf16[3584,2048]{1,0:T(8,128)(2,1)} custom-call(s32[6]{0:T(128)} %stack.89.at_ref, bf16[288,2048]{1,0:T(8,128)(2,1)} %copy-done.2, bf16[288,2048]{1,0:T(8,128)(2,1)} %copy-done.8, bf16[288,2048]{1,0:T(8,128)(2,1)} %copy-done.3, bf16[288,2048]{1,0:T(8,128)(2,1)} %copy-done.9, bf16[288,2048]{1,0:T(8,128)(2,1)} %copy-done.1, ...), custom_call_target="tpu_custom_call" | custom-call | flops 4831838208 | bytes 24903680 | tf_op jit(solution)/shard_map/grad_down/pallas_call | solution.py:97
  165.8 3.3 %collective-permute-start.16 = (bf16[144,1536]{1,0:T(8,128)(2,1)S(1)}, bf16[144,1536]{1,0:T(8,128)(2,1)S(1)}, u32[]{:S(2)}, u32[]{:S(2)}) collective-permute-start(bf16[144,1536]{1,0:T(8,128)(2,1)S(1)} %add_convert_fusion.5), channel_id=1, source_target_pairs={{0,8},{8,0},{16,24},{24,16},{1,9},{9,1},{17,25},{25,17},{2,10},{10... | collective-permute-start | bytes 1327112 | tf_op jit(solution)/shard_map/ppermute | solution.py:245
  169.9 12.5 %collective-permute-start.19 = (bf16[144,2048]{1,0:T(8,128)(2,1)}, bf16[144,2048]{1,0:T(8,128)(2,1)S(1)}, u32[]{:S(2)}, u32[]{:S(2)}) collective-permute-start(bf16[144,2048]{1,0:T(8,128)(2,1)} %collective-permute-done.17.refs_2_), channel_id=1, source_target_pairs={{0,8},{8,0},{16,24},{24,16},{1,9},{9,1},{17,25},{25,17},{2,10},{10... | collective-permute-start | bytes 1769480 | tf_op jit(solution)/shard_map/ppermute | solution.py:245
  182.4 1.2 select_bitcast_fusion
  183.9 11.7 %collective-permute-done.19.refs_4_ = bf16[144,2048]{1,0:T(8,128)(2,1)S(1)} collective-permute-done((bf16[144,2048]{1,0:T(8,128)(2,1)}, bf16[144,2048]{1,0:T(8,128)(2,1)S(1)}, u32[]{:S(2)}, u32[]{:S(2)}) %collective-permute-start.19) | collective-permute-done | bytes 589856 | tf_op jit(solution)/shard_map/ppermute | solution.py:245
  195.6 1.7 collective-permute-start.27
  197.6 1.6 copy.22
  200.1 2.1 collective-permute-start.24
  202.2 9.6 %collective-permute-done.27.refs_5_ = bf16[144,2048]{1,0:T(8,128)(2,1)S(1)} collective-permute-done((bf16[144,2048]{1,0:T(8,128)(2,1)S(1)}, bf16[144,2048]{1,0:T(8,128)(2,1)S(1)}, u32[]{:S(2)}, u32[]{:S(2)}) %collective-permute-start.27) | collective-permute-done | bytes 589856 | tf_op jit(solution)/shard_map/ppermute | solution.py:245
  211.8 1.7 collective-permute-start.30
  213.6 25.5 %grad_x_part.2 = (f32[576,2048]{1,0:T(8,128)}, bf16[576,2048]{1,0:T(8,128)(2,1)}, bf16[576,2048]{1,0:T(8,128)(2,1)}) custom-call(s32[6]{0:T(128)} %stack.89.at_ref, bf16[144,2048]{1,0:T(8,128)(2,1)} %copy-done.12, bf16[144,2048]{1,0:T(8,128)(2,1)} %copy-done.19, bf16[144,2048]{1,0:T(8,128)(2,1)} %collective-permute-done.17.refs_2_, ...), custom_call_target="tpu_custom_call" | custom-call | flops 9663676416 | bytes 26214400 | tf_op jit(solution)/shard_map/grad_x_part/pallas_call | solution.py:173
  239.9 2.4 collective-permute-start.29
  242.2 10.8 %grad_gate_up.3 = (bf16[2048,3584]{1,0:T(8,128)(2,1)}, bf16[2048,3584]{1,0:T(8,128)(2,1)}) custom-call(bf16[576,2048]{1,0:T(8,128)(2,1)} %bitcast.50, bf16[576,2048]{1,0:T(8,128)(2,1)} %get-tuple-element.68.dg_ref, bf16[576,2048]{1,0:T(8,128)(2,1)} %get-tuple-element.69.du_ref, f32[32,3584]{1,0:T(8,128)} %reshape.25.refs_14_.kg_ref, ...), custom_call_target="tpu_custom_call" | custom-call | flops 4831838208 | bytes 10747904 | tf_op jit(solution)/shard_map/grad_gate_up/pallas_call | solution.py:218
  253.2 10.9 %grad_gate_up.4 = (bf16[2048,3584]{1,0:T(8,128)(2,1)}, bf16[2048,3584]{1,0:T(8,128)(2,1)}) custom-call(bf16[576,2048]{1,0:T(8,128)(2,1)} %bitcast.51, bf16[576,2048]{1,0:T(8,128)(2,1)} %get-tuple-element.68.dg_ref, bf16[576,2048]{1,0:T(8,128)(2,1)} %get-tuple-element.69.du_ref, ...), custom_call_target="tpu_custom_call", output_to_operand_aliasing={{0}: (5, {}), {1}: (6, {})} | custom-call | flops 4831838208 | bytes 10747904 | tf_op jit(solution)/shard_map/grad_gate_up/pallas_call | solution.py:218
  265.7 21.4 %grad_x_part.3 = (f32[576,2048]{1,0:T(8,128)}, bf16[576,1536]{1,0:T(8,128)(2,1)}, bf16[576,1536]{1,0:T(8,128)(2,1)}) custom-call(s32[6]{0:T(128)} %stack.89.at_ref, bf16[144,1536]{1,0:T(8,128)(2,1)} %copy-done.13, bf16[144,1536]{1,0:T(8,128)(2,1)} %copy-done.24, bf16[144,1536]{1,0:T(8,128)(2,1)} %copy-done.23, ...), custom_call_target="tpu_custom_call", output_to_operand_aliasing={{0}: (17, {})} | custom-call | flops 7247757312 | bytes 22020096 | tf_op jit(solution)/shard_map/grad_x_part/pallas_call | solution.py:173
  287.1 1.9 dynamic-slice_bitcast_fusion
  289.1 11.3 %grad_down.3 = bf16[3584,2048]{1,0:T(8,128)(2,1)} custom-call(s32[6]{0:T(128)} %stack.89.at_ref, bf16[288,1536]{1,0:T(8,128)(2,1)} %copy-done.4, bf16[288,1536]{1,0:T(8,128)(2,1)} %collective-permute-done.7.refs_7_.refs_1_, bf16[288,1536]{1,0:T(8,128)(2,1)} %copy-done.5, ...), custom_call_target="tpu_custom_call", output_to_operand_aliasing={{}: (9, {})} | custom-call | flops 3623878656 | bytes 18677760 | tf_op jit(solution)/shard_map/grad_down/pallas_call | solution.py:97
  300.5 2.1 fusion.11
  302.7 1.5 collective-permute-start.33
  304.2 1.5 collective-permute-start.34
  306.2 14.1 %grad_gate_up.5 = (bf16[2048,3584]{1,0:T(8,128)(2,1)}, bf16[2048,3584]{1,0:T(8,128)(2,1)}) custom-call(bf16[576,2048]{1,0:T(8,128)(2,1)} %bitcast.52, bf16[576,1536]{1,0:T(8,128)(2,1)} %get-tuple-element.77.dg_ref, bf16[576,1536]{1,0:T(8,128)(2,1)} %get-tuple-element.78.du_ref, ...), custom_call_target="tpu_custom_call", output_to_operand_aliasing={{0}: (5, {}), {1}: (6, {})} | custom-call | flops 7247757312 | bytes 14942208 | tf_op jit(solution)/shard_map/grad_gate_up/pallas_call | solution.py:218
  (132 shorter events, 14.6 us)
Async XLA Ops:
  0.7 8.7 %copy-start.28 = (s32[56,32]{0,1:T(8,128)S(1)}, s32[56,32]{0,1:T(8,128)}, u32[]{:S(2)}) copy-start(s32[56,32]{0,1:T(8,128)} %param.19) | copy-start | bytes 21508
  2.0 22.7 %copy-start.2 = (bf16[288,2048]{1,0:T(8,128)(2,1)}, bf16[288,2048]{1,0:T(8,128)(2,1)S(1)}, u32[]{:S(2)}) copy-start(bf16[288,2048]{1,0:T(8,128)(2,1)S(1)} %pad_maximum_fusion.3.refs_0_.refs_6_) | copy-start | bytes 3538948
  2.0 29.1 %collective-permute-start.3 = (bf16[288,2048]{1,0:T(8,128)(2,1)S(1)}, bf16[288,2048]{1,0:T(8,128)(2,1)S(1)}, u32[]{:S(2)}, u32[]{:S(2)}) collective-permute-start(bf16[288,2048]{1,0:T(8,128)(2,1)S(1)} %pad_maximum_fusion.3.refs_0_.refs_6_), channel_id=1, source_target_pairs={{0,8},{8,0},{16,24},{24,16},{1,9},{9,1},{17,25},{25,17},{2,10},{10... | collective-permute-start | bytes 3538952 | tf_op jit(solution)/shard_map/ppermute | solution.py:245
  5.1 26.0 %collective-permute-start.4 = (bf16[288,2048]{1,0:T(8,128)(2,1)S(1)}, bf16[288,2048]{1,0:T(8,128)(2,1)S(1)}, u32[]{:S(2)}, u32[]{:S(2)}) collective-permute-start(bf16[288,2048]{1,0:T(8,128)(2,1)S(1)} %pad_maximum_fusion.3.refs_0_.refs_6_), channel_id=1, source_target_pairs={{8,16},{16,8},{9,17},{17,9},{10,18},{18,10},{11,19},{19,11},{12,20... | collective-permute-start | bytes 3538952 | tf_op jit(solution)/shard_map/ppermute | solution.py:245
  5.8 10.3 %collective-permute-start = (bf16[72,2048]{1,0:T(8,128)(2,1)}, bf16[72,2048]{1,0:T(8,128)(2,1)}, u32[]{:S(2)}, u32[]{:S(2)}) collective-permute-start(bf16[72,2048]{1,0:T(8,128)(2,1)} %param.11), channel_id=1, source_target_pairs={{0,2},{1,3},{2,0},{3,1},{4,6},{5,7},{6,4},{7,5},{8,10},{9,11},{10,... | collective-permute-start | bytes 884744 | tf_op jit(solution)/shard_map/ppermute | solution.py:349
  7.4 14.8 %collective-permute-start.1 = (bf16[72,2048]{1,0:T(8,128)(2,1)}, bf16[72,2048]{1,0:T(8,128)(2,1)}, u32[]{:S(2)}, u32[]{:S(2)}) collective-permute-start(bf16[72,2048]{1,0:T(8,128)(2,1)} %param.11), channel_id=1, source_target_pairs={{0,4},{1,5},{2,6},{3,7},{4,0},{5,1},{6,2},{7,3},{8,12},{9,13},{10,... | collective-permute-start | bytes 884744 | tf_op jit(solution)/shard_map/ppermute | solution.py:349
  8.9 13.3 %collective-permute-start.2 = (bf16[72,2048]{1,0:T(8,128)(2,1)}, bf16[72,2048]{1,0:T(8,128)(2,1)}, u32[]{:S(2)}, u32[]{:S(2)}) collective-permute-start(bf16[72,2048]{1,0:T(8,128)(2,1)} %param.11), channel_id=1, source_target_pairs={{0,6},{1,7},{2,4},{3,5},{4,2},{5,3},{6,0},{7,1},{8,14},{9,15},{10,... | collective-permute-start | bytes 884744 | tf_op jit(solution)/shard_map/ppermute | solution.py:349
  22.2 9.9 %slice-start.5 = ((bf16[144,3584]{1,0:T(8,128)(2,1)}), bf16[144,1536]{1,0:T(8,128)(2,1)S(1)}, s32[]{:S(2)}) async-start(bf16[144,3584]{1,0:T(8,128)(2,1)} %param.12), calls=%async_computation.5 | async-start | bytes 884736 | tf_op jit(solution)/shard_map/slice | solution.py:419
  22.2 9.9 %slice-start.7 = ((bf16[144,3584]{1,0:T(8,128)(2,1)}), bf16[144,1536]{1,0:T(8,128)(2,1)S(1)}, s32[]{:S(2)}) async-start(bf16[144,3584]{1,0:T(8,128)(2,1)} %param.13), calls=%async_computation.7 | async-start | bytes 884736 | tf_op jit(solution)/shard_map/slice | solution.py:419
  31.1 22.3 %copy-start.3 = (bf16[288,2048]{1,0:T(8,128)(2,1)}, bf16[288,2048]{1,0:T(8,128)(2,1)S(1)}, u32[]{:S(2)}) copy-start(bf16[288,2048]{1,0:T(8,128)(2,1)S(1)} %collective-permute-done.4.refs_2_.refs_8_) | copy-start | bytes 3538948
  31.1 8.6 %collective-permute-start.5 = (bf16[4,72,2048]{2,1,0:T(8,128)(2,1)}, bf16[4,72,2048]{2,1,0:T(8,128)(2,1)}, u32[]{:S(2)}, u32[]{:S(2)}) collective-permute-start(bf16[4,72,2048]{2,1,0:T(8,128)(2,1)} %pad_maximum_fusion.2), channel_id=1, source_target_pairs={{0,1},{1,0},{2,3},{3,2},{4,5},{5,4},{6,7},{7,6},{8,9},{9,8},{10,11... | collective-permute-start | bytes 3538952 | tf_op jit(solution)/shard_map/ppermute | solution.py:356
  32.2 9.3 %copy-start.4 = (bf16[288,1536]{1,0:T(8,128)(2,1)}, bf16[288,1536]{1,0:T(8,128)(2,1)S(1)}, u32[]{:S(2)}) copy-start(bf16[288,1536]{1,0:T(8,128)(2,1)S(1)} %pad_maximum_fusion.5.refs_6_.refs_0_) | copy-start | bytes 2654212
  32.2 24.4 %collective-permute-start.6 = (bf16[288,1536]{1,0:T(8,128)(2,1)S(1)}, bf16[288,1536]{1,0:T(8,128)(2,1)S(1)}, u32[]{:S(2)}, u32[]{:S(2)}) collective-permute-start(bf16[288,1536]{1,0:T(8,128)(2,1)S(1)} %pad_maximum_fusion.5.refs_6_.refs_0_), channel_id=1, source_target_pairs={{8,16},{16,8},{9,17},{17,9},{10,18},{18,10},{11,19},{19,11},{12,20... | collective-permute-start | bytes 2654216 | tf_op jit(solution)/shard_map/ppermute | solution.py:245
  32.9 26.9 %collective-permute-start.7 = (bf16[288,1536]{1,0:T(8,128)(2,1)S(1)}, bf16[288,1536]{1,0:T(8,128)(2,1)}, u32[]{:S(2)}, u32[]{:S(2)}) collective-permute-start(bf16[288,1536]{1,0:T(8,128)(2,1)S(1)} %pad_maximum_fusion.5.refs_6_.refs_0_), channel_id=1, source_target_pairs={{0,8},{8,0},{16,24},{24,16},{1,9},{9,1},{17,25},{25,17},{2,10},{10... | collective-permute-start | bytes 2654216 | tf_op jit(solution)/shard_map/ppermute | solution.py:245
  53.4 35.5 %slice-start = ((s8[4718592]{0:T(1024)(128)(4,1)}), s8[4194304]{0:T(1024)(128)(4,1)S(1)}, s32[]{:S(2)}) async-start(s8[4718592]{0:T(1024)(128)(4,1)} %bitcast.48), calls=%async_computation | async-start | bytes 8388608
  56.5 32.3 %slice-start.1 = ((s8[4718592]{0:T(1024)(128)(4,1)}), s8[524288]{0:T(1024)(128)(4,1)S(1)}, s32[]{:S(2)}) async-start(s8[4718592]{0:T(1024)(128)(4,1)} %bitcast.48), calls=%async_computation.1 | async-start | bytes 1048576
  59.8 11.4 %copy-start.6 = (bf16[288,1536]{1,0:T(8,128)(2,1)S(1)}, bf16[288,1536]{1,0:T(8,128)(2,1)}, u32[]{:S(2)}) copy-start(bf16[288,1536]{1,0:T(8,128)(2,1)} %copy-done.5) | copy-start | bytes 2654212
  59.8 29.1 %collective-permute-start.9 = (bf16[288,2048]{1,0:T(8,128)(2,1)}, bf16[288,2048]{1,0:T(8,128)(2,1)S(1)}, u32[]{:S(2)}, u32[]{:S(2)}) collective-permute-start(bf16[288,2048]{1,0:T(8,128)(2,1)} %broadcast_select_fusion), channel_id=1, source_target_pairs={{0,8},{8,0},{16,24},{24,16},{1,9},{9,1},{17,25},{25,17},{2,10},{10... | collective-permute-start | bytes 3538952 | tf_op jit(solution)/shard_map/ppermute | solution.py:245
  61.5 45.0 %collective-permute-start.12 = (bf16[288,2048]{1,0:T(8,128)(2,1)}, bf16[288,2048]{1,0:T(8,128)(2,1)S(1)}, u32[]{:S(2)}, u32[]{:S(2)}) collective-permute-start(bf16[288,2048]{1,0:T(8,128)(2,1)} %copy-done.8), channel_id=1, source_target_pairs={{8,16},{16,8},{9,17},{17,9},{10,18},{18,10},{11,19},{19,11},{12,20... | collective-permute-start | bytes 3538952 | tf_op jit(solution)/shard_map/ppermute | solution.py:245
  72.8 35.2 %copy-start.14 = (bf16[72,2048]{1,0:T(8,128)(2,1)S(1)}, bf16[72,2048]{1,0:T(8,128)(2,1)}, u32[]{:S(2)}) copy-start(bf16[72,2048]{1,0:T(8,128)(2,1)} %param.10) | copy-start | bytes 884740
  72.8 52.3 %copy-start.29 = (s32[32,56]{1,0:T(8,128)S(1)}, s32[32,56]{1,0:T(8,128)}, u32[]{:S(2)}) copy-start(s32[32,56]{1,0:T(8,128)} %param.17) | copy-start | bytes 21508
  72.9 33.7 %collective-permute-start.8 = (bf16[288,1536]{1,0:T(8,128)(2,1)S(1)}, bf16[288,1536]{1,0:T(8,128)(2,1)S(1)}, u32[]{:S(2)}, u32[]{:S(2)}) collective-permute-start(bf16[288,1536]{1,0:T(8,128)(2,1)S(1)} %broadcast_select_fusion.1), channel_id=1, source_target_pairs={{0,8},{8,0},{16,24},{24,16},{1,9},{9,1},{17,25},{25,17},{2,10},{10... | collective-permute-start | bytes 2654216 | tf_op jit(solution)/shard_map/ppermute | solution.py:245
  90.3 42.4 %collective-permute-start.10 = (bf16[288,2048]{1,0:T(8,128)(2,1)}, bf16[288,2048]{1,0:T(8,128)(2,1)}, u32[]{:S(2)}, u32[]{:S(2)}) collective-permute-start(bf16[288,2048]{1,0:T(8,128)(2,1)} %add_convert_fusion), channel_id=1, source_target_pairs={{8,16},{16,8},{9,17},{17,9},{10,18},{18,10},{11,19},{19,11},{12,20... | collective-permute-start | bytes 3538952 | tf_op jit(solution)/shard_map/ppermute | solution.py:245
  106.5 33.7 %copy-start.7 = (bf16[288,1536]{1,0:T(8,128)(2,1)}, bf16[288,1536]{1,0:T(8,128)(2,1)S(1)}, u32[]{:S(2)}) copy-start(bf16[288,1536]{1,0:T(8,128)(2,1)S(1)} %collective-permute-done.8.refs_10_.refs_4_) | copy-start | bytes 2654212
  106.5 25.5 %copy-start.9 = (bf16[288,2048]{1,0:T(8,128)(2,1)}, bf16[288,2048]{1,0:T(8,128)(2,1)S(1)}, u32[]{:S(2)}) copy-start(bf16[288,2048]{1,0:T(8,128)(2,1)S(1)} %collective-permute-done.12.refs_3_.refs_9_) | copy-start | bytes 3538948
  106.5 27.9 %collective-permute-start.13 = (bf16[288,2048]{1,0:T(8,128)(2,1)S(1)}, bf16[288,2048]{1,0:T(8,128)(2,1)S(1)}, u32[]{:S(2)}, u32[]{:S(2)}) collective-permute-start(bf16[288,2048]{1,0:T(8,128)(2,1)S(1)} %collective-permute-done.12.refs_3_.refs_9_), channel_id=1, source_target_pairs={{0,8},{8,0},{16,24},{24,16},{1,9},{9,1},{17,25},{25,17},{2,10},{10... | collective-permute-start | bytes 3538952 | tf_op jit(solution)/shard_map/ppermute | solution.py:245
  108.0 7.2 %collective-permute-start.20 = (bf16[72,2048]{1,0:T(8,128)(2,1)S(1)}, bf16[72,2048]{1,0:T(8,128)(2,1)S(1)}, u32[]{:S(2)}, u32[]{:S(2)}) collective-permute-start(bf16[72,2048]{1,0:T(8,128)(2,1)S(1)} %copy-done.14), channel_id=1, source_target_pairs={{0,2},{1,3},{2,0},{3,1},{4,6},{5,7},{6,4},{7,5},{8,10},{9,11},{10,... | collective-permute-start | bytes 884744 | tf_op jit(solution)/shard_map/ppermute | solution.py:349
  109.5 24.9 %collective-permute-start.14 = (bf16[288,1536]{1,0:T(8,128)(2,1)}, bf16[288,1536]{1,0:T(8,128)(2,1)}, u32[]{:S(2)}, u32[]{:S(2)}) collective-permute-start(bf16[288,1536]{1,0:T(8,128)(2,1)} %collective-permute-done.7.refs_7_.refs_1_), channel_id=1, source_target_pairs={{8,16},{16,8},{9,17},{17,9},{10,18},{18,10},{11,19},{19,11},{12,20... | collective-permute-start | bytes 2654216 | tf_op jit(solution)/shard_map/ppermute | solution.py:245
  115.2 6.7 %copy-start.15 = (bf16[72,2048]{1,0:T(8,128)(2,1)}, bf16[72,2048]{1,0:T(8,128)(2,1)S(1)}, u32[]{:S(2)}) copy-start(bf16[72,2048]{1,0:T(8,128)(2,1)S(1)} %collective-permute-done.20) | copy-start | bytes 884740
  115.2 6.7 %collective-permute-start.21 = (bf16[72,2048]{1,0:T(8,128)(2,1)S(1)}, bf16[72,2048]{1,0:T(8,128)(2,1)S(1)}, u32[]{:S(2)}, u32[]{:S(2)}) collective-permute-start(bf16[72,2048]{1,0:T(8,128)(2,1)S(1)} %copy-done.14), channel_id=1, source_target_pairs={{0,4},{1,5},{2,6},{3,7},{4,0},{5,1},{6,2},{7,3},{8,12},{9,13},{10,... | collective-permute-start | bytes 884744 | tf_op jit(solution)/shard_map/ppermute | solution.py:349
  122.7 15.4 %collective-permute-start.22 = (bf16[72,2048]{1,0:T(8,128)(2,1)S(1)}, bf16[72,2048]{1,0:T(8,128)(2,1)}, u32[]{:S(2)}, u32[]{:S(2)}) collective-permute-start(bf16[72,2048]{1,0:T(8,128)(2,1)S(1)} %copy-done.14), channel_id=1, source_target_pairs={{0,6},{1,7},{2,4},{3,5},{4,2},{5,3},{6,0},{7,1},{8,14},{9,15},{10,... | collective-permute-start | bytes 884744 | tf_op jit(solution)/shard_map/ppermute | solution.py:349
  132.7 5.4 %copy-start.16 = (bf16[72,2048]{1,0:T(8,128)(2,1)S(1)}, bf16[72,2048]{1,0:T(8,128)(2,1)}, u32[]{:S(2)}) copy-start(bf16[72,2048]{1,0:T(8,128)(2,1)} %copy-done.15) | copy-start | bytes 884740
  132.7 5.4 %copy-start.18 = (bf16[72,2048]{1,0:T(8,128)(2,1)S(1)}, bf16[72,2048]{1,0:T(8,128)(2,1)}, u32[]{:S(2)}) copy-start(bf16[72,2048]{1,0:T(8,128)(2,1)} %copy-done.17) | copy-start | bytes 884740
  132.7 7.6 %copy-start = (f32[576,1536]{1,0:T(8,128)S(1)}, f32[576,1536]{1,0:T(8,128)}, u32[]{:S(2)}) copy-start(f32[576,1536]{1,0:T(8,128)} %dhidden.2) | copy-start | bytes 10616836
  134.4 7.0 %copy-start.10 = (bf16[288,2048]{1,0:T(8,128)(2,1)}, bf16[288,2048]{1,0:T(8,128)(2,1)S(1)}, u32[]{:S(2)}) copy-start(bf16[288,2048]{1,0:T(8,128)(2,1)S(1)} %collective-permute-done.13.refs_5_.refs_11_) | copy-start | bytes 3538948
  134.4 13.2 %collective-permute-start.15 = (bf16[144,2048]{1,0:T(8,128)(2,1)S(1)}, bf16[144,2048]{1,0:T(8,128)(2,1)S(1)}, u32[]{:S(2)}, u32[]{:S(2)}) collective-permute-start(bf16[144,2048]{1,0:T(8,128)(2,1)S(1)} %add_convert_fusion.3), channel_id=1, source_target_pairs={{0,8},{8,0},{16,24},{24,16},{1,9},{9,1},{17,25},{25,17},{2,10},{10... | collective-permute-start | bytes 1769480 | tf_op jit(solution)/shard_map/ppermute | solution.py:245
  140.3 42.2 %collective-permute-start.23 = (bf16[4,72,2048]{2,1,0:T(8,128)(2,1)}, bf16[4,72,2048]{2,1,0:T(8,128)(2,1)S(1)}, u32[]{:S(2)}, u32[]{:S(2)}) collective-permute-start(bf16[4,72,2048]{2,1,0:T(8,128)(2,1)} %pad_maximum_fusion.4), channel_id=1, source_target_pairs={{0,1},{1,0},{2,3},{3,2},{4,5},{5,4},{6,7},{7,6},{8,9},{9,8},{10,11... | collective-permute-start | bytes 3538952 | tf_op jit(solution)/shard_map/ppermute | solution.py:356
  141.4 24.2 %collective-permute-start.11 = (bf16[288,1536]{1,0:T(8,128)(2,1)}, bf16[288,1536]{1,0:T(8,128)(2,1)S(1)}, u32[]{:S(2)}, u32[]{:S(2)}) collective-permute-start(bf16[288,1536]{1,0:T(8,128)(2,1)} %add_convert_fusion.1), channel_id=1, source_target_pairs={{8,16},{16,8},{9,17},{17,9},{10,18},{18,10},{11,19},{19,11},{12,20... | collective-permute-start | bytes 2654216 | tf_op jit(solution)/shard_map/ppermute | solution.py:245
  149.3 16.3 %copy-start.12 = (bf16[144,2048]{1,0:T(8,128)(2,1)}, bf16[144,2048]{1,0:T(8,128)(2,1)S(1)}, u32[]{:S(2)}) copy-start(bf16[144,2048]{1,0:T(8,128)(2,1)S(1)} %add_convert_fusion.2.refs_0_) | copy-start | bytes 1769476
  149.3 19.7 %collective-permute-start.18 = (bf16[144,2048]{1,0:T(8,128)(2,1)S(1)}, bf16[144,2048]{1,0:T(8,128)(2,1)S(1)}, u32[]{:S(2)}, u32[]{:S(2)}) collective-permute-start(bf16[144,2048]{1,0:T(8,128)(2,1)S(1)} %add_convert_fusion.2.refs_0_), channel_id=1, source_target_pairs={{0,8},{8,0},{16,24},{24,16},{1,9},{9,1},{17,25},{25,17},{2,10},{10... | collective-permute-start | bytes 1769480 | tf_op jit(solution)/shard_map/ppermute | solution.py:245
  151.2 17.9 %collective-permute-start.17 = (bf16[144,2048]{1,0:T(8,128)(2,1)S(1)}, bf16[144,2048]{1,0:T(8,128)(2,1)}, u32[]{:S(2)}, u32[]{:S(2)}) collective-permute-start(bf16[144,2048]{1,0:T(8,128)(2,1)S(1)} %add_convert_fusion.2.refs_0_), channel_id=1, source_target_pairs={{8,16},{16,8},{9,17},{17,9},{10,18},{18,10},{11,19},{19,11},{12,20... | collective-permute-start | bytes 1769480 | tf_op jit(solution)/shard_map/ppermute | solution.py:245
  165.8 18.1 %collective-permute-start.16 = (bf16[144,1536]{1,0:T(8,128)(2,1)S(1)}, bf16[144,1536]{1,0:T(8,128)(2,1)S(1)}, u32[]{:S(2)}, u32[]{:S(2)}) collective-permute-start(bf16[144,1536]{1,0:T(8,128)(2,1)S(1)} %add_convert_fusion.5), channel_id=1, source_target_pairs={{0,8},{8,0},{16,24},{24,16},{1,9},{9,1},{17,25},{25,17},{2,10},{10... | collective-permute-start | bytes 1327112 | tf_op jit(solution)/shard_map/ppermute | solution.py:245
  169.0 14.6 %copy-start.19 = (bf16[144,2048]{1,0:T(8,128)(2,1)}, bf16[144,2048]{1,0:T(8,128)(2,1)S(1)}, u32[]{:S(2)}) copy-start(bf16[144,2048]{1,0:T(8,128)(2,1)S(1)} %collective-permute-done.18.refs_1_) | copy-start | bytes 1769476
  169.0 14.8 %collective-permute-start.26 = (bf16[144,2048]{1,0:T(8,128)(2,1)S(1)}, bf16[144,2048]{1,0:T(8,128)(2,1)S(1)}, u32[]{:S(2)}, u32[]{:S(2)}) collective-permute-start(bf16[144,2048]{1,0:T(8,128)(2,1)S(1)} %collective-permute-done.18.refs_1_), channel_id=1, source_target_pairs={{8,16},{16,8},{9,17},{17,9},{10,18},{18,10},{11,19},{19,11},{12,20... | collective-permute-start | bytes 1769480 | tf_op jit(solution)/shard_map/ppermute | solution.py:245
  169.9 25.6 %collective-permute-start.19 = (bf16[144,2048]{1,0:T(8,128)(2,1)}, bf16[144,2048]{1,0:T(8,128)(2,1)S(1)}, u32[]{:S(2)}, u32[]{:S(2)}) collective-permute-start(bf16[144,2048]{1,0:T(8,128)(2,1)} %collective-permute-done.17.refs_2_), channel_id=1, source_target_pairs={{0,8},{8,0},{16,24},{24,16},{1,9},{9,1},{17,25},{25,17},{2,10},{10... | collective-permute-start | bytes 1769480 | tf_op jit(solution)/shard_map/ppermute | solution.py:245
  183.9 13.7 %copy-start.20 = (bf16[144,2048]{1,0:T(8,128)(2,1)}, bf16[144,2048]{1,0:T(8,128)(2,1)S(1)}, u32[]{:S(2)}) copy-start(bf16[144,2048]{1,0:T(8,128)(2,1)S(1)} %collective-permute-done.26.refs_3_) | copy-start | bytes 1769476
  195.6 16.3 %collective-permute-start.27 = (bf16[144,2048]{1,0:T(8,128)(2,1)S(1)}, bf16[144,2048]{1,0:T(8,128)(2,1)S(1)}, u32[]{:S(2)}, u32[]{:S(2)}) collective-permute-start(bf16[144,2048]{1,0:T(8,128)(2,1)S(1)} %collective-permute-done.26.refs_3_), channel_id=1, source_target_pairs={{0,8},{8,0},{16,24},{24,16},{1,9},{9,1},{17,25},{25,17},{2,10},{10... | collective-permute-start | bytes 1769480 | tf_op jit(solution)/shard_map/ppermute | solution.py:245
  199.4 39.7 %copy-start.13 = (bf16[144,1536]{1,0:T(8,128)(2,1)}, bf16[144,1536]{1,0:T(8,128)(2,1)S(1)}, u32[]{:S(2)}) copy-start(bf16[144,1536]{1,0:T(8,128)(2,1)S(1)} %add_convert_fusion.4.refs_0_) | copy-start | bytes 1327108
  199.4 40.4 %collective-permute-start.25 = (bf16[144,1536]{1,0:T(8,128)(2,1)S(1)}, bf16[144,1536]{1,0:T(8,128)(2,1)S(1)}, u32[]{:S(2)}, u32[]{:S(2)}) collective-permute-start(bf16[144,1536]{1,0:T(8,128)(2,1)S(1)} %add_convert_fusion.4.refs_0_), channel_id=1, source_target_pairs={{8,16},{16,8},{9,17},{17,9},{10,18},{18,10},{11,19},{19,11},{12,20... | collective-permute-start | bytes 1327112 | tf_op jit(solution)/shard_map/ppermute | solution.py:245
  200.1 39.0 %collective-permute-start.24 = (bf16[144,1536]{1,0:T(8,128)(2,1)S(1)}, bf16[144,1536]{1,0:T(8,128)(2,1)S(1)}, u32[]{:S(2)}, u32[]{:S(2)}) collective-permute-start(bf16[144,1536]{1,0:T(8,128)(2,1)S(1)} %add_convert_fusion.4.refs_0_), channel_id=1, source_target_pairs={{0,8},{8,0},{16,24},{24,16},{1,9},{9,1},{17,25},{25,17},{2,10},{10... | collective-permute-start | bytes 1327112 | tf_op jit(solution)/shard_map/ppermute | solution.py:245
  211.8 41.2 %collective-permute-start.30 = (bf16[288,1536]{1,0:T(8,128)(2,1)}, bf16[288,1536]{1,0:T(8,128)(2,1)S(1)}, u32[]{:S(2)}, u32[]{:S(2)}) collective-permute-start(bf16[288,1536]{1,0:T(8,128)(2,1)} %collective-permute-done.14.refs_9_.refs_3_), channel_id=1, source_target_pairs={{0,8},{8,0},{16,24},{24,16},{1,9},{9,1},{17,25},{25,17},{2,10},{10... | collective-permute-start | bytes 2654216 | tf_op jit(solution)/shard_map/ppermute | solution.py:245
  239.1 13.9 %copy-start.24 = (bf16[144,1536]{1,0:T(8,128)(2,1)}, bf16[144,1536]{1,0:T(8,128)(2,1)S(1)}, u32[]{:S(2)}) copy-start(bf16[144,1536]{1,0:T(8,128)(2,1)S(1)} %collective-permute-done.24.refs_1_) | copy-start | bytes 1327108
  239.1 13.9 %collective-permute-start.28 = (bf16[144,1536]{1,0:T(8,128)(2,1)S(1)}, bf16[144,1536]{1,0:T(8,128)(2,1)S(1)}, u32[]{:S(2)}, u32[]{:S(2)}) collective-permute-start(bf16[144,1536]{1,0:T(8,128)(2,1)S(1)} %collective-permute-done.24.refs_1_), channel_id=1, source_target_pairs={{8,16},{16,8},{9,17},{17,9},{10,18},{18,10},{11,19},{19,11},{12,20... | collective-permute-start | bytes 1327112 | tf_op jit(solution)/shard_map/ppermute | solution.py:245
  239.8 13.2 %copy-start.23 = (bf16[144,1536]{1,0:T(8,128)(2,1)}, bf16[144,1536]{1,0:T(8,128)(2,1)S(1)}, u32[]{:S(2)}) copy-start(bf16[144,1536]{1,0:T(8,128)(2,1)S(1)} %collective-permute-done.25.refs_2_) | copy-start | bytes 1327108
  239.9 24.2 %collective-permute-start.29 = (bf16[144,1536]{1,0:T(8,128)(2,1)S(1)}, bf16[144,1536]{1,0:T(8,128)(2,1)S(1)}, u32[]{:S(2)}, u32[]{:S(2)}) collective-permute-start(bf16[144,1536]{1,0:T(8,128)(2,1)S(1)} %collective-permute-done.25.refs_2_), channel_id=1, source_target_pairs={{0,8},{8,0},{16,24},{24,16},{1,9},{9,1},{17,25},{25,17},{2,10},{10... | collective-permute-start | bytes 1327112 | tf_op jit(solution)/shard_map/ppermute | solution.py:245
  253.0 11.1 %copy-start.25 = (bf16[144,1536]{1,0:T(8,128)(2,1)}, bf16[144,1536]{1,0:T(8,128)(2,1)S(1)}, u32[]{:S(2)}) copy-start(bf16[144,1536]{1,0:T(8,128)(2,1)S(1)} %collective-permute-done.28.refs_3_) | copy-start | bytes 1327108
  253.1 11.0 %copy-start.11 = (bf16[288,1536]{1,0:T(8,128)(2,1)}, bf16[288,1536]{1,0:T(8,128)(2,1)S(1)}, u32[]{:S(2)}) copy-start(bf16[288,1536]{1,0:T(8,128)(2,1)S(1)} %collective-permute-done.30.refs_11_.refs_5_) | copy-start | bytes 2654212
  253.1 11.1 %collective-permute-start.31 = (bf16[144,1536]{1,0:T(8,128)(2,1)S(1)}, bf16[144,1536]{1,0:T(8,128)(2,1)S(1)}, u32[]{:S(2)}, u32[]{:S(2)}) collective-permute-start(bf16[144,1536]{1,0:T(8,128)(2,1)S(1)} %collective-permute-done.28.refs_3_), channel_id=1, source_target_pairs={{0,8},{8,0},{16,24},{24,16},{1,9},{9,1},{17,25},{25,17},{2,10},{10... | collective-permute-start | bytes 1327112 | tf_op jit(solution)/shard_map/ppermute | solution.py:245
  287.1 13.3 %slice-start.2 = ((s8[4718592]{0:T(1024)(128)(4,1)}), s8[524288]{0:T(1024)(128)(4,1)S(1)}, s32[]{:S(2)}) async-start(s8[4718592]{0:T(1024)(128)(4,1)} %bitcast.54), calls=%async_computation.2 | async-start | bytes 1048576
  289.0 11.4 %collective-permute-start.32 = (f32[4,72,2048]{2,1,0:T(8,128)S(1)}, f32[4,72,2048]{2,1,0:T(8,128)}, u32[]{:S(2)}, u32[]{:S(2)}) collective-permute-start(f32[4,72,2048]{2,1,0:T(8,128)S(1)} %dynamic-slice_bitcast_fusion), channel_id=1, source_target_pairs={{0,1},{1,0},{2,3},{3,2},{4,5},{5,4},{6,7},{7,6},{8,9},{9,8},{10,11... | collective-permute-start | bytes 7077896 | tf_op jit(solution)/shard_map/ppermute | solution.py:369
  289.1 11.3 %slice-start.3 = ((s8[4718592]{0:T(1024)(128)(4,1)}), s8[4194304]{0:T(1024)(128)(4,1)S(1)}, s32[]{:S(2)}) async-start(s8[4718592]{0:T(1024)(128)(4,1)} %bitcast.54), calls=%async_computation.3 | async-start | bytes 8388608
  302.7 17.7 %collective-permute-start.33 = (bf16[72,2048]{1,0:T(8,128)(2,1)S(1)}, bf16[72,2048]{1,0:T(8,128)(2,1)S(1)}, u32[]{:S(2)}, u32[]{:S(2)}) collective-permute-start(bf16[72,2048]{1,0:T(8,128)(2,1)S(1)} %get-tuple-element.100), channel_id=1, source_target_pairs={{0,2},{1,3},{2,0},{3,1},{4,6},{5,7},{6,4},{7,5},{8,10},{9,11},{10,... | collective-permute-start | bytes 884744 | tf_op jit(solution)/shard_map/ppermute | solution.py:378
  304.2 16.2 %collective-permute-start.34 = (bf16[72,2048]{1,0:T(8,128)(2,1)S(1)}, bf16[72,2048]{1,0:T(8,128)(2,1)S(1)}, u32[]{:S(2)}, u32[]{:S(2)}) collective-permute-start(bf16[72,2048]{1,0:T(8,128)(2,1)S(1)} %get-tuple-element.102), channel_id=1, source_target_pairs={{0,4},{1,5},{2,6},{3,7},{4,0},{5,1},{6,2},{7,3},{8,12},{9,13},{10,... | collective-permute-start | bytes 884744 | tf_op jit(solution)/shard_map/ppermute | solution.py:378
  305.7 14.6 %collective-permute-start.35 = (bf16[72,2048]{1,0:T(8,128)(2,1)S(1)}, bf16[72,2048]{1,0:T(8,128)(2,1)S(1)}, u32[]{:S(2)}, u32[]{:S(2)}) collective-permute-start(bf16[72,2048]{1,0:T(8,128)(2,1)S(1)} %get-tuple-element.101), channel_id=1, source_target_pairs={{0,6},{1,7},{2,4},{3,5},{4,2},{5,3},{6,0},{7,1},{8,14},{9,15},{10,... | collective-permute-start | bytes 884744 | tf_op jit(solution)/shard_map/ppermute | solution.py:378
  (11 other events, 15.2 us)

commit v3 on v2

--- a/solution.py
+++ b/solution.py
@@ -73,13 +73,17 @@
     return gate_val, up_val, sig, gate_val * sig
 
 
-def down_kernel(n, rows, at_ref, *refs):
+def down_kernel(n, rows, factors, at_ref, *refs):
     pairs, refs = refs[:n], refs[n:]
     grad_ref, keep_ref = refs[:2]
-    gdown_ref, buf = refs[-2:]
+    buf, outs = refs[-1], refs[:-1]
+    gdown_ref = outs[-3] if factors else outs[-1]
     gate = in_order(at_ref, buf, pairs, rows, 0)
     up = in_order(at_ref, buf, pairs, rows, 1)
-    _, up_val, _, silu = gate_parts(gate, up)
+    gate_val, up_val, sig, silu = gate_parts(gate, up)
+    if factors:
+        outs[-2][...] = up_val * sig * (1.0 + gate_val * (1.0 - sig))
+        outs[-1][...] = silu
     hidden = (silu * up_val).astype(BF16)
     out = lax.dot_general(
         hidden, grad_ref[...], (((0,), (0,)), ((), ())), preferred_element_type=F32
@@ -87,7 +91,7 @@
     gdown_ref[...] = masked(out, keep_ref[0]).astype(BF16)
 
 
-def down_grad(where, pairs, grad_all, keep_down, held, at, f, n_row, ft):
+def down_grad(where, pairs, grad_all, keep_down, held, at, f, n_row, ft, factors=False):
     T, D = grad_all.shape
     F = keep_down.shape[0] * ft
     rows, n = pairs[0].shape[0], len(pairs)
@@ -95,15 +99,17 @@
     args = [where, *pairs, grad_all, keep_down]
     here = at // ft
     return pl.pallas_call(
-        functools.partial(down_kernel, n, rows // 2),
-        out_shape=jax.ShapeDtypeStruct((F, D), BF16),
+        functools.partial(down_kernel, n, rows // 2, factors),
+        out_shape=[jax.ShapeDtypeStruct((F, D), BF16)]
+        + ([jax.ShapeDtypeStruct((T, f), F32)] * 2 if factors else []),
         grid_spec=pltpu.PrefetchScalarGridSpec(
             num_scalar_prefetch=1,
             grid=(f // ft,),
             in_specs=[pl.BlockSpec((rows, ft), lambda j, *_: (0, j))] * n
             + [whole((T, D)), pl.BlockSpec((1, ft // TILE, D), lambda j, *_: (j + here, 0, 0))]
             + ([] if first else [pl.BlockSpec(memory_space=pl.ANY)]),
-            out_specs=pl.BlockSpec((ft, D), lambda j, *_: (j + here, 0)),
+            out_specs=[pl.BlockSpec((ft, D), lambda j, *_: (j + here, 0))]
+            + ([pl.BlockSpec((T, ft), lambda j, *_: (0, j))] * 2 if factors else []),
             scratch_shapes=[pltpu.VMEM(((n_row + 1) * rows // 2, ft), BF16)],
         ),
         input_output_aliases={} if first else {len(args): 0},
@@ -115,23 +121,29 @@
     )(*args, *([] if first else [held]))
 
 
-def input_kernel(n, rows, first, at_ref, *refs):
-    pieces, pairs, rest = refs[:n], refs[n : 2 * n], refs[2 * n :]
+def input_kernel(n, rows, n_pair, first, last, at_ref, *refs):
+    pieces, refs = refs[:n], refs[n:]
+    pairs, rest = refs[:n_pair], refs[n_pair:]
     wg_ref, wu_ref, kg_ref, ku_ref = rest[:4]
     rest = rest[4:]
     if not first:
         sum_ref, rest = rest[0], rest[1:]
-    gx_ref, dg_ref, du_ref, buf, dg_all, du_all = rest
+    gx_ref, dg_ref, du_ref = rest[:3]
+    buf, dg_all, du_all = rest[-3:]
     c = pl.program_id(1)
 
     @pl.when(pl.program_id(0) == 0)
     def _():
         d_hidden = in_order(at_ref, buf, pieces, rows).astype(F32)
-        gate = in_order(at_ref, buf, pairs, rows, 0)
-        up = in_order(at_ref, buf, pairs, rows, 1)
-        gate_val, up_val, sig, silu = gate_parts(gate, up)
-        d_gate = (d_hidden * up_val * sig * (1.0 + gate_val * (1.0 - sig))).astype(BF16)
-        d_up = (d_hidden * silu).astype(BF16)
+        if n_pair == 2:
+            d_gate = (d_hidden * pairs[0][...]).astype(BF16)
+            d_up = (d_hidden * pairs[1][...]).astype(BF16)
+        else:
+            gate = in_order(at_ref, buf, pairs, rows, 0)
+            up = in_order(at_ref, buf, pairs, rows, 1)
+            gate_val, up_val, sig, silu = gate_parts(gate, up)
+            d_gate = (d_hidden * up_val * sig * (1.0 + gate_val * (1.0 - sig))).astype(BF16)
+            d_up = (d_hidden * silu).astype(BF16)
         dg_ref[...] = d_gate
         du_ref[...] = d_up
         dg_all[c] = d_gate
@@ -151,8 +163,18 @@
     def _():
         gx_ref[...] += out
 
-
-def input_grad(where, pieces, pairs, w_gate, w_up, keep_gate, keep_up, total, span, n_row, ft, dt):
+    if last:
+
+        @pl.when(c == pl.num_programs(1) - 1)
+        def _():
+            send_ref = rest[3]
+            per = last
+            for p in range(send_ref.shape[0] // per):
+                start = pl.multiple_of((2 * p + 1 - at_ref[n]) * per, 8)
+                send_ref[p * per : (p + 1) * per, :] = gx_ref[pl.ds(start, per), :]
+
+
+def input_grad(where, pieces, pairs, w_gate, w_up, keep_gate, keep_up, total, span, last, n_row, ft, dt):
     rows, n = pieces[0].shape[0], len(pieces)
     T = rows * n_row
     D = w_gate.shape[0]
@@ -164,24 +186,29 @@
         return jnp.where(d == 0, c, chunks - 1)
 
     piece = pl.BlockSpec((rows, ft), lambda d, c, *_: (0, once(d, c)))
-    pair = pl.BlockSpec((2 * rows, ft), lambda d, c, *_: (0, once(d, c)))
+    pair = pl.BlockSpec((pairs[0].shape[0], ft), lambda d, c, *_: (0, once(d, c)))
     tall = pl.BlockSpec((T, ft), lambda d, c, *_: (0, once(d, c)))
     weight = pl.BlockSpec((dt, ft), lambda d, c, *_: (d, c + here))
     keep = pl.BlockSpec((dt // TILE, ft), lambda d, c, *_: (d, c + here))
     gx = pl.BlockSpec((T, dt), lambda d, c, *_: (0, d))
     args = [where, *pieces, *pairs, w_gate, w_up, keep_gate, keep_up]
     return pl.pallas_call(
-        functools.partial(input_kernel, n, rows, first),
-        out_shape=(
+        functools.partial(input_kernel, n, rows, len(pairs), first, last),
+        out_shape=[
             jax.ShapeDtypeStruct((T, D), F32),
             jax.ShapeDtypeStruct((T, width), BF16),
             jax.ShapeDtypeStruct((T, width), BF16),
-        ),
+        ]
+        + ([jax.ShapeDtypeStruct((T // 2, D), F32)] if last else []),
         grid_spec=pltpu.PrefetchScalarGridSpec(
             num_scalar_prefetch=1,
             grid=(D // dt, chunks),
-            in_specs=[piece] * n + [pair] * n + [weight, weight, keep, keep] + ([] if first else [gx]),
-            out_specs=[gx, tall, tall],
+            in_specs=[piece] * n
+            + [pair] * len(pairs)
+            + [weight, weight, keep, keep]
+            + ([] if first else [gx]),
+            out_specs=[gx, tall, tall]
+            + ([pl.BlockSpec((T // 2, dt), lambda d, c, *_: (0, d))] if last else []),
             scratch_shapes=[
                 pltpu.VMEM(((n_row + 1) * rows, ft), BF16),
                 pltpu.VMEM((chunks, T, ft), BF16),
@@ -360,11 +387,11 @@
     return jnp.stack(ordered).reshape(n * rows, width)
 
 
-def pair_sums(part, n, me):
+def pair_sums(part, send, n, me):
     rows = part.shape[0] // n
     core = me % 2
     blocks = part.reshape(n // 2, 2, rows, part.shape[1])
-    send = lax.dynamic_index_in_dim(blocks, 1 - core, 1, keepdims=False)
+    send = send.reshape(n // 2, rows, part.shape[1])
     keep = lax.dynamic_index_in_dim(blocks, core, 1, keepdims=False)
     return keep + lax.ppermute(send, "col", [(i, i ^ 1) for i in range(n)])
 
@@ -408,7 +435,7 @@
     row, col = lax.axis_index("row"), lax.axis_index("col")
     F, D = w_down.shape
     ft = 512 if F % 512 == 0 else 256
-    dt = min(1024, D)
+    dt = min(2048, D)
     keep_gate, keep_up, keep_down = lanes(mask_gate), lanes(mask_up), lanes(mask_down)
     keep_down = keep_down.reshape(F // ft, ft // TILE, D)
 
@@ -420,8 +447,9 @@
     ]
 
     def use(which, pieces, pairs, total):
+        last = grad_all.shape[0] // n_col if which else 0
         return input_grad(
-            where, pieces, pairs, w_gate, w_up, keep_gate, keep_up, total, spans[which], n_row, ft, dt
+            where, pieces, pairs, w_gate, w_up, keep_gate, keep_up, total, spans[which], last, n_row, ft, dt
         )
 
     def weights(which, d_gate, d_up, held, part=None):
@@ -429,14 +457,14 @@
         part = part or (0, span[1])
         return weight_grads(tok_all, d_gate, d_up, keep_gate, keep_up, held, span, part, ft)
 
-    def down(which, pairs, grad_down):
+    def down(which, pairs, grad_down, factors=False):
         start, width = spans[which]
         return down_grad(
-            where, pairs, grad_all, keep_down, grad_down, start, width, n_row, ft
+            where, pairs, grad_all, keep_down, grad_down, start, width, n_row, ft, factors
         )
 
     if n_row != 4:
-        where = jnp.stack([(row - s) % n_row for s in range(n_row)]).astype(jnp.int32)
+        where = jnp.stack([(row - s) % n_row for s in range(n_row)] + [col % 2]).astype(jnp.int32)
         grad_all = pair_gather(pairs_gather(out_grad, n_col), n_col, col)
         tok_all = pair_gather(pairs_gather(tokens, n_col), n_col, col)
         total = held = grad_down = None
@@ -444,23 +472,23 @@
             part = dhidden_part(grad_all, w_down, keep_down, span, ft)
             pairs = ring_gather(own[which], n_row)
             pieces = ring_gather(ring_reduce(part, n_row, row), n_row)
-            total, d_gate, d_up = use(which, pieces, pairs, total)
+            total, d_gate, d_up, *send = use(which, pieces, pairs, total)
             held = weights(which, d_gate, d_up, held)
-            grad_down = down(which, pairs, grad_down)
-        grad_x = pair_reduce(pair_sums(total, n_col, col), n_col, col).astype(BF16)
+            (grad_down,) = down(which, pairs, grad_down)
+        grad_x = pair_reduce(pair_sums(total, send[0], n_col, col), n_col, col).astype(BF16)
         return (grad_x, held[0], held[1], grad_down)
 
     def after(x, *deps):
         return lax.optimization_barrier((x, *deps))[0]
 
     four = Four(row)
-    where = four.where
+    where = jnp.append(four.where, (col % 2).astype(jnp.int32))
     outer, inner = four.outer, four.inner
     a, b = Gather(four, own[0]), Gather(four, own[1])
     a.swap()
     a.cross()
     mine = pairs_gather(out_grad, n_col)
-    grad_all = pair_gather(after(mine, a.next, a.near, keep_down), n_col, col)
+    grad_all = pair_gather(after(mine, a.next, a.near, keep_down, keep_gate, keep_up), n_col, col)
     b.swap()
     b.cross()
     low = dhidden_part(grad_all, w_down, keep_down, spans[0], ft)
@@ -487,7 +515,7 @@
     h_a.cross()
     h_a.swap()
     sum_b.swap()
-    grad_down = down(0, a.pieces(), None)
+    grad_down, *factors = down(0, a.pieces(), None, True)
     inner.hold(grad_down, h_a.near)
     h_a.spread()
     h_a.cross_next()
@@ -498,7 +526,7 @@
     outer.hold(tok_all)
     h_b.swap()
     b.spread_next()
-    total, d_gate, d_up = use(0, h_a.pieces(), a.pieces(), None)
+    total, d_gate, d_up = use(0, h_a.pieces(), factors, None)
     inner.hold(total)
     h_b.cross_next()
     outer.hold(total)
@@ -509,9 +537,9 @@
     h_b.spread_next()
     held = weights(0, d_gate, d_up, held, (half, cut - half))
     total = after(total, held[0])
-    total, d_gate, d_up = use(1, h_b.pieces(), b.pieces(), total)
-    summed = pair_sums(total, n_col, col)
-    grad_down = down(1, b.pieces(), grad_down)
+    total, d_gate, d_up, send = use(1, h_b.pieces(), b.pieces(), total)
+    summed = pair_sums(total, send, n_col, col)
+    (grad_down,) = down(1, b.pieces(), grad_down)
     grad_x = pair_reduce(summed, n_col, col).astype(BF16)
     held = weights(1, after(d_gate, summed), d_up, held)
     return (grad_x, held[0], held[1], grad_down)

time: 322 us -> 315 us (0.978)
  local copies, waits for them, and re-layouts: 23.1 us -> 13.2 us
  waiting for transfers between devices: 80.9 us -> 90.7 us
  Pallas kernels: 126 us -> 119 us
    ppermute x24, waiting for transfers between devices: 63.7 us -> 72.3 us  [issue(): x = lax.ppermute(x, 'row', self.perm)]
    pallas_call x4, Pallas kernels: 71.3 us -> 64.5 us  [the longest x2 38.8 us: input_grad(): pl.pallas_call(functools.partial(input_kernel, n, rows, len(pairs), first...]
    broadcast_in_dim x3, local copies, waits for them, and re-layouts: 4.46 us -> 0.89 us  [lanes(): return jnp.repeat(mask.astype(F32), TILE, axis=1)]
  transfers between devices with their start and end apart: 36 -> 36, of which waited for: 11 -> 12; matrix products, arithmetic and copies ran while one was open for 11% -> 8% of each run, Pallas kernels for 32% -> 32%
where the time goes in v3:
time: 315 us; the launch traced here: 314 us
  Pallas kernels  119 us (38%)
  waiting for transfers between devices  90.7 us (29%)
  starting transfers between devices  68.3 us (22%)
  other arithmetic  21.7 us (7%)
  local copies, waits for them, and re-layouts  13.2 us (4%)
    ppermute x24, waiting for transfers between devices, issue(): x = lax.ppermute(x, 'row', self.perm)  72.3 us
    ppermute x24, starting transfers between devices, issue(): x = lax.ppermute(x, 'row', self.perm)  55.7 us
    pallas_call x2, Pallas kernels, input_grad(): pl.pallas_call(functools.partial(input_kernel, n, rows, len(pairs), first...  38.8 us
    pallas_call x3, Pallas kernels, weight_grads(): pl.pallas_call(weight_kernel, out_shape=(jax.ShapeDtypeStruct((D, F), BF1...  35.8 us
    pallas_call x2, Pallas kernels, down_grad(): pl.pallas_call(functools.partial(down_kernel, n, rows // 2, factors), out...  25.6 us
    pallas_call x2, Pallas kernels, dhidden_part(): pl.pallas_call(dhidden_kernel, out_shape=jax.ShapeDtypeStruct((T, width),...  18.7 us
    ppermute x6, waiting for transfers between devices, pairs_gather(): got.append(lax.ppermute(send, 'col', [(i, i ^ 2 * k) for i in range(n)]))  18.4 us
    ppermute x6, starting transfers between devices, pairs_gather(): got.append(lax.ppermute(send, 'col', [(i, i ^ 2 * k) for i in range(n)]))  8.95 us
  transfers between devices with their start and end apart: 36, of which 12 were waited for; matrix products, arithmetic and copies ran while one was open for 8% of the time, Pallas kernels for 32%

profile of v3, /device:TPU:0, one launch (start us, length us, event | category | flops | bytes accessed | tf_op | source)
XLA Modules:
  0.0 314.0 jit_solution(7563043641506238803)
XLA Ops:
  0.7 1.0 slice-done.2
  1.9 1.1 pad_maximum_fusion.3.refs_0_
  3.0 3.0 collective-permute-start.3
  6.0 1.7 collective-permute-start.4
  7.7 2.4 collective-permute-start.2
  11.5 1.0 reshape.31.refs_10_.kg_ref.refs_14_
  12.8 1.0 reshape.32.refs_11_.ku_ref.refs_15_
  14.3 1.1 reshape_reshape.3.keep_ref.refs_7_
  15.3 3.2 %collective-permute-done.2 = bf16[72,2048]{1,0:T(8,128)(2,1)S(1)} collective-permute-done((bf16[72,2048]{1,0:T(8,128)(2,1)S(1)}, bf16[72,2048]{1,0:T(8,128)(2,1)S(1)}, u32[]{:S(2)}, u32[]{:S(2)}) %collective-permute-start.2) | collective-permute-done | bytes 294944 | tf_op jit(solution)/shard_map/ppermute | solution.py:376
  18.6 4.9 %collective-permute-done = bf16[72,2048]{1,0:T(8,128)(2,1)S(1)} collective-permute-done((bf16[72,2048]{1,0:T(8,128)(2,1)S(1)}, bf16[72,2048]{1,0:T(8,128)(2,1)S(1)}, u32[]{:S(2)}, u32[]{:S(2)}) %collective-permute-start) | collective-permute-done | bytes 294944 | tf_op jit(solution)/shard_map/ppermute | solution.py:376
  24.3 1.3 pad_maximum_fusion.2
  25.6 6.7 %collective-permute-done.3.refs_1_ = bf16[288,2048]{1,0:T(8,128)(2,1)} collective-permute-done((bf16[288,2048]{1,0:T(8,128)(2,1)}, bf16[288,2048]{1,0:T(8,128)(2,1)}, u32[]{:S(2)}, u32[]{:S(2)}) %collective-permute-start.3) | collective-permute-done | bytes 1179680 | tf_op jit(solution)/shard_map/ppermute | solution.py:272
  33.1 7.7 %collective-permute-start.7 = (bf16[288,1536]{1,0:T(8,128)(2,1)S(1)}, bf16[288,1536]{1,0:T(8,128)(2,1)}, u32[]{:S(2)}, u32[]{:S(2)}) collective-permute-start(bf16[288,1536]{1,0:T(8,128)(2,1)S(1)} %pad_maximum_fusion.5.refs_6_.refs_0_), channel_id=1, source_target_pairs={{0,8},{8,0},{16,24},{24,16},{1,9},{9,1},{17,25},{25,17},{2,10},{10... | collective-permute-start | bytes 2654216 | tf_op jit(solution)/shard_map/ppermute | solution.py:272
  40.9 1.4 select_bitcast_fusion.2
  42.8 1.6 copy.21
  44.4 9.8 %dhidden.3 = f32[576,2048]{1,0:T(8,128)} custom-call(bf16[576,2048]{1,0:T(8,128)(2,1)} %bitcast.44, bf16[3584,2048]{1,0:T(8,128)(2,1)} %w_ref.3, f32[7,8,2048]{2,1,0:T(8,128)} %reshape_reshape.3.keep_ref.refs_7_), custom_call_target="tpu_custom_call" | custom-call | flops 4831838208 | bytes 13107200 | tf_op jit(solution)/shard_map/dhidden/pallas_call | solution.py:43
  54.2 3.2 %broadcast_select_fusion = bf16[288,2048]{1,0:T(8,128)(2,1)} fusion(bf16[288,2048]{1,0:T(8,128)(2,1)} %collective-permute-done.4.refs_2_, pred[]{:T(512)S(6)} %or.3, f32[576,2048]{1,0:T(8,128)} %dhidden.3, s32[]{:T(128)S(6)} %select_n.182), kind=kLoop, calls=%fused_computation.32 | loop fusion | flops 589824 | bytes 3538949 | tf_op jit(solution)/shard_map/jit(_where)/select_n | solution.py:311
  57.4 3.6 %collective-permute-done.7.refs_7_.refs_1_ = bf16[288,1536]{1,0:T(8,128)(2,1)} collective-permute-done((bf16[288,1536]{1,0:T(8,128)(2,1)S(1)}, bf16[288,1536]{1,0:T(8,128)(2,1)}, u32[]{:S(2)}, u32[]{:S(2)}) %collective-permute-start.7) | collective-permute-done | bytes 884768 | tf_op jit(solution)/shard_map/ppermute | solution.py:272
  61.0 1.7 collective-permute-start.9
  62.7 1.8 collective-permute-start.12
  64.5 8.9 %dhidden.2 = f32[576,1536]{1,0:T(8,128)} custom-call(bf16[576,2048]{1,0:T(8,128)(2,1)} %bitcast.45, bf16[3584,2048]{1,0:T(8,128)(2,1)} %w_ref.3, f32[7,8,2048]{2,1,0:T(8,128)} %reshape_reshape.3.keep_ref.refs_7_), custom_call_target="tpu_custom_call" | custom-call | flops 3623878656 | bytes 9830400 | tf_op jit(solution)/shard_map/dhidden/pallas_call | solution.py:43
  73.4 1.7 broadcast_select_fusion.1
  75.1 0.8 collective-permute-start.8
  75.9 14.3 %collective-permute-done.9.refs_4_ = bf16[288,2048]{1,0:T(8,128)(2,1)} collective-permute-done((bf16[288,2048]{1,0:T(8,128)(2,1)}, bf16[288,2048]{1,0:T(8,128)(2,1)}, u32[]{:S(2)}, u32[]{:S(2)}) %collective-permute-start.9) | collective-permute-done | bytes 1179680 | tf_op jit(solution)/shard_map/ppermute | solution.py:272
  90.2 2.6 add_convert_fusion
  92.8 1.7 collective-permute-start.10
  94.5 13.3 %collective-permute-done.8.refs_10_.refs_4_ = bf16[288,1536]{1,0:T(8,128)(2,1)S(1)} collective-permute-done((bf16[288,1536]{1,0:T(8,128)(2,1)S(1)}, bf16[288,1536]{1,0:T(8,128)(2,1)S(1)}, u32[]{:S(2)}, u32[]{:S(2)}) %collective-permute-start.8) | collective-permute-done | bytes 884768 | tf_op jit(solution)/shard_map/ppermute | solution.py:272
  107.8 1.4 collective-permute-start.13
  109.2 1.5 collective-permute-start.20
  111.4 5.0 %collective-permute-done.20 = bf16[72,2048]{1,0:T(8,128)(2,1)S(1)} collective-permute-done((bf16[72,2048]{1,0:T(8,128)(2,1)S(1)}, bf16[72,2048]{1,0:T(8,128)(2,1)S(1)}, u32[]{:S(2)}, u32[]{:S(2)}) %collective-permute-start.20) | collective-permute-done | bytes 294944 | tf_op jit(solution)/shard_map/ppermute | solution.py:376
  116.4 1.5 collective-permute-start.21
  117.9 5.2 %collective-permute-done.21 = bf16[72,2048]{1,0:T(8,128)(2,1)S(1)} collective-permute-done((bf16[72,2048]{1,0:T(8,128)(2,1)S(1)}, bf16[72,2048]{1,0:T(8,128)(2,1)S(1)}, u32[]{:S(2)}, u32[]{:S(2)}) %collective-permute-start.21) | collective-permute-done | bytes 294944 | tf_op jit(solution)/shard_map/ppermute | solution.py:376
  123.1 2.4 collective-permute-start.22
  126.2 1.7 add_convert_fusion.3
  127.9 6.8 %collective-permute-done.13.refs_5_ = bf16[288,2048]{1,0:T(8,128)(2,1)} collective-permute-done((bf16[288,2048]{1,0:T(8,128)(2,1)}, bf16[288,2048]{1,0:T(8,128)(2,1)}, u32[]{:S(2)}, u32[]{:S(2)}) %collective-permute-start.13) | collective-permute-done | bytes 1179680 | tf_op jit(solution)/shard_map/ppermute | solution.py:272
  134.8 5.6 %collective-permute-start.15 = (bf16[144,2048]{1,0:T(8,128)(2,1)S(1)}, bf16[144,2048]{1,0:T(8,128)(2,1)S(1)}, u32[]{:S(2)}, u32[]{:S(2)}) collective-permute-start(bf16[144,2048]{1,0:T(8,128)(2,1)S(1)} %add_convert_fusion.3), channel_id=1, source_target_pairs={{0,8},{8,0},{16,24},{24,16},{1,9},{9,1},{17,25},{25,17},{2,10},{10... | collective-permute-start | bytes 1769480 | tf_op jit(solution)/shard_map/ppermute | solution.py:272
  140.4 1.2 pad_maximum_fusion.4
  141.6 1.1 add_convert_fusion.1
  143.5 6.6 %collective-permute-done.15 = bf16[144,2048]{1,0:T(8,128)(2,1)S(1)} collective-permute-done((bf16[144,2048]{1,0:T(8,128)(2,1)S(1)}, bf16[144,2048]{1,0:T(8,128)(2,1)S(1)}, u32[]{:S(2)}, u32[]{:S(2)}) %collective-permute-start.15) | collective-permute-done | bytes 589856 | tf_op jit(solution)/shard_map/ppermute | solution.py:272
  150.1 1.7 add_convert_fusion.2.refs_0_
  151.8 2.1 collective-permute-start.18
  153.9 1.5 collective-permute-start.17
  155.3 14.3 %grad_down.2 = (bf16[3584,2048]{1,0:T(8,128)(2,1)}, f32[576,2048]{1,0:T(8,128)}, f32[576,2048]{1,0:T(8,128)}) custom-call(s32[7]{0:T(128)} %concatenate.11.at_ref, bf16[288,2048]{1,0:T(8,128)(2,1)} %pad_maximum_fusion.3.refs_0_, bf16[288,2048]{1,0:T(8,128)(2,1)} %collective-permute-done.3.refs_1_, bf16[288,2048]{1,0:T(8,128)(2,1)} %collective-permute-done.4.refs_2_, ...), custom_call_target="tpu_custom_call" | custom-call | flops 4831838208 | bytes 24903680 | tf_op jit(solution)/shard_map/grad_down/pallas_call | solution.py:101
  169.8 1.5 collective-permute-start.16
  171.3 0.9 collective-permute-start.26
  172.2 10.5 %collective-permute-start.19 = (bf16[144,2048]{1,0:T(8,128)(2,1)}, bf16[144,2048]{1,0:T(8,128)(2,1)S(1)}, u32[]{:S(2)}, u32[]{:S(2)}) collective-permute-start(bf16[144,2048]{1,0:T(8,128)(2,1)} %collective-permute-done.17.refs_2_), channel_id=1, source_target_pairs={{0,8},{8,0},{16,24},{24,16},{1,9},{9,1},{17,25},{25,17},{2,10},{10... | collective-permute-start | bytes 1769480 | tf_op jit(solution)/shard_map/ppermute | solution.py:272
  183.1 12.6 %collective-permute-done.19.refs_4_ = bf16[144,2048]{1,0:T(8,128)(2,1)S(1)} collective-permute-done((bf16[144,2048]{1,0:T(8,128)(2,1)}, bf16[144,2048]{1,0:T(8,128)(2,1)S(1)}, u32[]{:S(2)}, u32[]{:S(2)}) %collective-permute-start.19) | collective-permute-done | bytes 589856 | tf_op jit(solution)/shard_map/ppermute | solution.py:272
  195.8 1.7 collective-permute-start.27
  197.9 1.6 copy.22
  200.4 3.4 %collective-permute-start.24 = (bf16[144,1536]{1,0:T(8,128)(2,1)S(1)}, bf16[144,1536]{1,0:T(8,128)(2,1)S(1)}, u32[]{:S(2)}, u32[]{:S(2)}) collective-permute-start(bf16[144,1536]{1,0:T(8,128)(2,1)S(1)} %add_convert_fusion.4.refs_0_), channel_id=1, source_target_pairs={{0,8},{8,0},{16,24},{24,16},{1,9},{9,1},{17,25},{25,17},{2,10},{10... | collective-permute-start | bytes 1327112 | tf_op jit(solution)/shard_map/ppermute | solution.py:272
  203.7 8.3 %collective-permute-done.27.refs_5_ = bf16[144,2048]{1,0:T(8,128)(2,1)S(1)} collective-permute-done((bf16[144,2048]{1,0:T(8,128)(2,1)S(1)}, bf16[144,2048]{1,0:T(8,128)(2,1)S(1)}, u32[]{:S(2)}, u32[]{:S(2)}) %collective-permute-start.27) | collective-permute-done | bytes 589856 | tf_op jit(solution)/shard_map/ppermute | solution.py:272
  212.1 1.7 collective-permute-start.30
  213.8 19.6 %grad_x_part.2 = (f32[576,2048]{1,0:T(8,128)}, bf16[576,2048]{1,0:T(8,128)(2,1)}, bf16[576,2048]{1,0:T(8,128)(2,1)}) custom-call(s32[7]{0:T(128)} %concatenate.11.at_ref, bf16[144,2048]{1,0:T(8,128)(2,1)} %copy-done.8, bf16[144,2048]{1,0:T(8,128)(2,1)} %collective-permute-done.18.refs_1_, bf16[144,2048]{1,0:T(8,128)(2,1)} %collective-permute-done.17.refs_2_, ...), custom_call_target="tpu_custom_call" | custom-call | flops 9663676416 | bytes 26214400 | tf_op jit(solution)/shard_map/grad_x_part/pallas_call | solution.py:195
  234.2 3.4 %collective-permute-start.29 = (bf16[144,1536]{1,0:T(8,128)(2,1)S(1)}, bf16[144,1536]{1,0:T(8,128)(2,1)S(1)}, u32[]{:S(2)}, u32[]{:S(2)}) collective-permute-start(bf16[144,1536]{1,0:T(8,128)(2,1)S(1)} %collective-permute-done.25.refs_2_), channel_id=1, source_target_pairs={{0,8},{8,0},{16,24},{24,16},{1,9},{9,1},{17,25},{25,17},{2,10},{10... | collective-permute-start | bytes 1327112 | tf_op jit(solution)/shard_map/ppermute | solution.py:272
  237.6 10.8 %grad_gate_up.3 = (bf16[2048,3584]{1,0:T(8,128)(2,1)}, bf16[2048,3584]{1,0:T(8,128)(2,1)}) custom-call(bf16[576,2048]{1,0:T(8,128)(2,1)} %bitcast.50, bf16[576,2048]{1,0:T(8,128)(2,1)} %get-tuple-element.75.dg_ref, bf16[576,2048]{1,0:T(8,128)(2,1)} %get-tuple-element.76.du_ref, f32[32,3584]{1,0:T(8,128)} %reshape.31.refs_10_.kg_ref.refs_14_, ...), custom_call_target="tpu_custom_call" | custom-call | flops 4831838208 | bytes 10747904 | tf_op jit(solution)/shard_map/grad_gate_up/pallas_call | solution.py:245
  248.5 10.9 %grad_gate_up.4 = (bf16[2048,3584]{1,0:T(8,128)(2,1)}, bf16[2048,3584]{1,0:T(8,128)(2,1)}) custom-call(bf16[576,2048]{1,0:T(8,128)(2,1)} %bitcast.51, bf16[576,2048]{1,0:T(8,128)(2,1)} %get-tuple-element.75.dg_ref, bf16[576,2048]{1,0:T(8,128)(2,1)} %get-tuple-element.76.du_ref, ...), custom_call_target="tpu_custom_call", output_to_operand_aliasing={{0}: (5, {}), {1}: (6, {})} | custom-call | flops 4831838208 | bytes 10747904 | tf_op jit(solution)/shard_map/grad_gate_up/pallas_call | solution.py:245
  261.0 19.2 %grad_x_part.3 = (f32[576,2048]{1,0:T(8,128)}, bf16[576,1536]{1,0:T(8,128)(2,1)}, bf16[576,1536]{1,0:T(8,128)(2,1)}, f32[288,2048]{1,0:T(8,128)}) custom-call(s32[7]{0:T(128)} %concatenate.11.at_ref, bf16[144,1536]{1,0:T(8,128)(2,1)} %copy-done.9, bf16[144,1536]{1,0:T(8,128)(2,1)} %copy-done.17, ...), custom_call_target="tpu_custom_call", output_to_operand_aliasing={{0}: (17, {})} | custom-call | flops 7247757312 | bytes 22020096 | tf_op jit(solution)/shard_map/grad_x_part/pallas_call | solution.py:195
  280.3 11.3 %grad_down.3 = bf16[3584,2048]{1,0:T(8,128)(2,1)} custom-call(s32[7]{0:T(128)} %concatenate.11.at_ref, bf16[288,1536]{1,0:T(8,128)(2,1)} %copy-done.2, bf16[288,1536]{1,0:T(8,128)(2,1)} %collective-permute-done.7.refs_7_.refs_1_, bf16[288,1536]{1,0:T(8,128)(2,1)} %copy-done.3, bf16[288,1536]{1,0:T(8,128)(2,1)} %copy-done.5, ...), custom_call_target="tpu_custom_call", output_to_operand_aliasing={{}: (9, {})} | custom-call | flops 3623878656 | bytes 18677760 | tf_op jit(solution)/shard_map/grad_down/pallas_call | solution.py:101
  291.6 1.4 copy-done.7
  293.1 2.2 fusion.11
  295.4 1.6 collective-permute-start.33
  296.9 1.5 collective-permute-start.34
  298.9 14.1 %grad_gate_up.5 = (bf16[2048,3584]{1,0:T(8,128)(2,1)}, bf16[2048,3584]{1,0:T(8,128)(2,1)}) custom-call(bf16[576,2048]{1,0:T(8,128)(2,1)} %bitcast.52, bf16[576,1536]{1,0:T(8,128)(2,1)} %get-tuple-element.85.dg_ref, bf16[576,1536]{1,0:T(8,128)(2,1)} %get-tuple-element.86.du_ref, ...), custom_call_target="tpu_custom_call", output_to_operand_aliasing={{0}: (5, {}), {1}: (6, {})} | custom-call | flops 7247757312 | bytes 14942208 | tf_op jit(solution)/shard_map/grad_gate_up/pallas_call | solution.py:245
  313.1 0.9 fusion.10
  (120 shorter events, 11.2 us)
Async XLA Ops:
  0.7 7.0 %copy-start.21 = (bf16[72,2048]{1,0:T(8,128)(2,1)S(1)}, bf16[72,2048]{1,0:T(8,128)(2,1)}, u32[]{:S(2)}) copy-start(bf16[72,2048]{1,0:T(8,128)(2,1)} %param.11) | copy-start | bytes 884740
  0.7 10.5 %copy-start.25 = (s32[32,56]{1,0:T(8,128)S(1)}, s32[32,56]{1,0:T(8,128)}, u32[]{:S(2)}) copy-start(s32[32,56]{1,0:T(8,128)} %param.17) | copy-start | bytes 21508
  1.9 10.6 %copy-start.26 = (s32[32,56]{1,0:T(8,128)S(1)}, s32[32,56]{1,0:T(8,128)}, u32[]{:S(2)}) copy-start(s32[32,56]{1,0:T(8,128)} %param.18) | copy-start | bytes 21508
  3.0 29.3 %collective-permute-start.3 = (bf16[288,2048]{1,0:T(8,128)(2,1)}, bf16[288,2048]{1,0:T(8,128)(2,1)}, u32[]{:S(2)}, u32[]{:S(2)}) collective-permute-start(bf16[288,2048]{1,0:T(8,128)(2,1)} %pad_maximum_fusion.3.refs_0_), channel_id=1, source_target_pairs={{0,8},{8,0},{16,24},{24,16},{1,9},{9,1},{17,25},{25,17},{2,10},{10... | collective-permute-start | bytes 3538952 | tf_op jit(solution)/shard_map/ppermute | solution.py:272
  6.0 26.3 %collective-permute-start.4 = (bf16[288,2048]{1,0:T(8,128)(2,1)}, bf16[288,2048]{1,0:T(8,128)(2,1)}, u32[]{:S(2)}, u32[]{:S(2)}) collective-permute-start(bf16[288,2048]{1,0:T(8,128)(2,1)} %pad_maximum_fusion.3.refs_0_), channel_id=1, source_target_pairs={{8,16},{16,8},{9,17},{17,9},{10,18},{18,10},{11,19},{19,11},{12,20... | collective-permute-start | bytes 3538952 | tf_op jit(solution)/shard_map/ppermute | solution.py:272
  7.7 10.9 %collective-permute-start.2 = (bf16[72,2048]{1,0:T(8,128)(2,1)S(1)}, bf16[72,2048]{1,0:T(8,128)(2,1)S(1)}, u32[]{:S(2)}, u32[]{:S(2)}) collective-permute-start(bf16[72,2048]{1,0:T(8,128)(2,1)S(1)} %copy-done.21), channel_id=1, source_target_pairs={{0,6},{1,7},{2,4},{3,5},{4,2},{5,3},{6,0},{7,1},{8,14},{9,15},{10,... | collective-permute-start | bytes 884744 | tf_op jit(solution)/shard_map/ppermute | solution.py:376
  10.1 13.3 %collective-permute-start = (bf16[72,2048]{1,0:T(8,128)(2,1)S(1)}, bf16[72,2048]{1,0:T(8,128)(2,1)S(1)}, u32[]{:S(2)}, u32[]{:S(2)}) collective-permute-start(bf16[72,2048]{1,0:T(8,128)(2,1)S(1)} %copy-done.21), channel_id=1, source_target_pairs={{0,2},{1,3},{2,0},{3,1},{4,6},{5,7},{6,4},{7,5},{8,10},{9,11},{10,... | collective-permute-start | bytes 884744 | tf_op jit(solution)/shard_map/ppermute | solution.py:376
  10.7 12.8 %collective-permute-start.1 = (bf16[72,2048]{1,0:T(8,128)(2,1)S(1)}, bf16[72,2048]{1,0:T(8,128)(2,1)S(1)}, u32[]{:S(2)}, u32[]{:S(2)}) collective-permute-start(bf16[72,2048]{1,0:T(8,128)(2,1)S(1)} %copy-done.21), channel_id=1, source_target_pairs={{0,4},{1,5},{2,6},{3,7},{4,0},{5,1},{6,2},{7,3},{8,12},{9,13},{10,... | collective-permute-start | bytes 884744 | tf_op jit(solution)/shard_map/ppermute | solution.py:376
  11.5 2.4 copy-start.27
  12.8 11.5 %copy-start.22 = (bf16[72,2048]{1,0:T(8,128)(2,1)S(1)}, bf16[72,2048]{1,0:T(8,128)(2,1)}, u32[]{:S(2)}) copy-start(bf16[72,2048]{1,0:T(8,128)(2,1)} %param.11) | copy-start | bytes 884740
  24.3 8.0 %slice-start.3 = ((bf16[144,3584]{1,0:T(8,128)(2,1)}), bf16[144,1536]{1,0:T(8,128)(2,1)S(1)}, s32[]{:S(2)}) async-start(bf16[144,3584]{1,0:T(8,128)(2,1)} %param.12), calls=%async_computation.3 | async-start | bytes 884736 | tf_op jit(solution)/shard_map/slice | solution.py:446
  24.3 8.0 %slice-start.5 = ((bf16[144,3584]{1,0:T(8,128)(2,1)}), bf16[144,1536]{1,0:T(8,128)(2,1)S(1)}, s32[]{:S(2)}) async-start(bf16[144,3584]{1,0:T(8,128)(2,1)} %param.13), calls=%async_computation.5 | async-start | bytes 884736 | tf_op jit(solution)/shard_map/slice | solution.py:446
  32.3 8.6 %collective-permute-start.5 = (bf16[4,72,2048]{2,1,0:T(8,128)(2,1)S(1)}, bf16[4,72,2048]{2,1,0:T(8,128)(2,1)}, u32[]{:S(2)}, u32[]{:S(2)}) collective-permute-start(bf16[4,72,2048]{2,1,0:T(8,128)(2,1)S(1)} %pad_maximum_fusion.2), channel_id=1, source_target_pairs={{0,1},{1,0},{2,3},{3,2},{4,5},{5,4},{6,7},{7,6},{8,9},{9,8},{10,11... | collective-permute-start | bytes 3538952 | tf_op jit(solution)/shard_map/ppermute | solution.py:383
  32.4 9.9 %copy-start.2 = (bf16[288,1536]{1,0:T(8,128)(2,1)}, bf16[288,1536]{1,0:T(8,128)(2,1)S(1)}, u32[]{:S(2)}) copy-start(bf16[288,1536]{1,0:T(8,128)(2,1)S(1)} %pad_maximum_fusion.5.refs_6_.refs_0_) | copy-start | bytes 2654212
  32.4 25.0 %collective-permute-start.6 = (bf16[288,1536]{1,0:T(8,128)(2,1)S(1)}, bf16[288,1536]{1,0:T(8,128)(2,1)S(1)}, u32[]{:S(2)}, u32[]{:S(2)}) collective-permute-start(bf16[288,1536]{1,0:T(8,128)(2,1)S(1)} %pad_maximum_fusion.5.refs_6_.refs_0_), channel_id=1, source_target_pairs={{8,16},{16,8},{9,17},{17,9},{10,18},{18,10},{11,19},{19,11},{12,20... | collective-permute-start | bytes 2654216 | tf_op jit(solution)/shard_map/ppermute | solution.py:272
  33.1 27.9 %collective-permute-start.7 = (bf16[288,1536]{1,0:T(8,128)(2,1)S(1)}, bf16[288,1536]{1,0:T(8,128)(2,1)}, u32[]{:S(2)}, u32[]{:S(2)}) collective-permute-start(bf16[288,1536]{1,0:T(8,128)(2,1)S(1)} %pad_maximum_fusion.5.refs_6_.refs_0_), channel_id=1, source_target_pairs={{0,8},{8,0},{16,24},{24,16},{1,9},{9,1},{17,25},{25,17},{2,10},{10... | collective-permute-start | bytes 2654216 | tf_op jit(solution)/shard_map/ppermute | solution.py:272
  54.2 35.9 %slice-start = ((s8[4718592]{0:T(1024)(128)(4,1)}), s8[4194304]{0:T(1024)(128)(4,1)S(1)}, s32[]{:S(2)}) async-start(s8[4718592]{0:T(1024)(128)(4,1)} %bitcast.48), calls=%async_computation | async-start | bytes 8388608
  57.4 32.8 %slice-start.1 = ((s8[4718592]{0:T(1024)(128)(4,1)}), s8[524288]{0:T(1024)(128)(4,1)S(1)}, s32[]{:S(2)}) async-start(s8[4718592]{0:T(1024)(128)(4,1)} %bitcast.48), calls=%async_computation.1 | async-start | bytes 1048576
  57.4 15.9 %copy-start.3 = (bf16[288,1536]{1,0:T(8,128)(2,1)}, bf16[288,1536]{1,0:T(8,128)(2,1)S(1)}, u32[]{:S(2)}) copy-start(bf16[288,1536]{1,0:T(8,128)(2,1)S(1)} %collective-permute-done.6.refs_8_.refs_2_) | copy-start | bytes 2654212
  61.0 29.2 %collective-permute-start.9 = (bf16[288,2048]{1,0:T(8,128)(2,1)}, bf16[288,2048]{1,0:T(8,128)(2,1)}, u32[]{:S(2)}, u32[]{:S(2)}) collective-permute-start(bf16[288,2048]{1,0:T(8,128)(2,1)} %broadcast_select_fusion), channel_id=1, source_target_pairs={{0,8},{8,0},{16,24},{24,16},{1,9},{9,1},{17,25},{25,17},{2,10},{10... | collective-permute-start | bytes 3538952 | tf_op jit(solution)/shard_map/ppermute | solution.py:272
  62.7 45.0 %collective-permute-start.12 = (bf16[288,2048]{1,0:T(8,128)(2,1)}, bf16[288,2048]{1,0:T(8,128)(2,1)}, u32[]{:S(2)}, u32[]{:S(2)}) collective-permute-start(bf16[288,2048]{1,0:T(8,128)(2,1)} %collective-permute-done.3.refs_1_), channel_id=1, source_target_pairs={{8,16},{16,8},{9,17},{17,9},{10,18},{18,10},{11,19},{19,11},{12,20... | collective-permute-start | bytes 3538952 | tf_op jit(solution)/shard_map/ppermute | solution.py:272
  75.0 34.1 %copy-start.10 = (bf16[72,2048]{1,0:T(8,128)(2,1)S(1)}, bf16[72,2048]{1,0:T(8,128)(2,1)}, u32[]{:S(2)}) copy-start(bf16[72,2048]{1,0:T(8,128)(2,1)} %param.10) | copy-start | bytes 884740
  75.1 32.7 %collective-permute-start.8 = (bf16[288,1536]{1,0:T(8,128)(2,1)S(1)}, bf16[288,1536]{1,0:T(8,128)(2,1)S(1)}, u32[]{:S(2)}, u32[]{:S(2)}) collective-permute-start(bf16[288,1536]{1,0:T(8,128)(2,1)S(1)} %broadcast_select_fusion.1), channel_id=1, source_target_pairs={{0,8},{8,0},{16,24},{24,16},{1,9},{9,1},{17,25},{25,17},{2,10},{10... | collective-permute-start | bytes 2654216 | tf_op jit(solution)/shard_map/ppermute | solution.py:272
  92.8 33.4 %collective-permute-start.10 = (bf16[288,2048]{1,0:T(8,128)(2,1)}, bf16[288,2048]{1,0:T(8,128)(2,1)}, u32[]{:S(2)}, u32[]{:S(2)}) collective-permute-start(bf16[288,2048]{1,0:T(8,128)(2,1)} %add_convert_fusion), channel_id=1, source_target_pairs={{8,16},{16,8},{9,17},{17,9},{10,18},{18,10},{11,19},{19,11},{12,20... | collective-permute-start | bytes 3538952 | tf_op jit(solution)/shard_map/ppermute | solution.py:272
  107.8 33.8 %copy-start.4 = (bf16[288,1536]{1,0:T(8,128)(2,1)}, bf16[288,1536]{1,0:T(8,128)(2,1)S(1)}, u32[]{:S(2)}) copy-start(bf16[288,1536]{1,0:T(8,128)(2,1)S(1)} %collective-permute-done.8.refs_10_.refs_4_) | copy-start | bytes 2654212
  107.8 27.0 %collective-permute-start.13 = (bf16[288,2048]{1,0:T(8,128)(2,1)}, bf16[288,2048]{1,0:T(8,128)(2,1)}, u32[]{:S(2)}, u32[]{:S(2)}) collective-permute-start(bf16[288,2048]{1,0:T(8,128)(2,1)} %collective-permute-done.12.refs_3_), channel_id=1, source_target_pairs={{0,8},{8,0},{16,24},{24,16},{1,9},{9,1},{17,25},{25,17},{2,10},{10... | collective-permute-start | bytes 3538952 | tf_op jit(solution)/shard_map/ppermute | solution.py:272
  109.2 7.2 %collective-permute-start.20 = (bf16[72,2048]{1,0:T(8,128)(2,1)S(1)}, bf16[72,2048]{1,0:T(8,128)(2,1)S(1)}, u32[]{:S(2)}, u32[]{:S(2)}) collective-permute-start(bf16[72,2048]{1,0:T(8,128)(2,1)S(1)} %copy-done.10), channel_id=1, source_target_pairs={{0,2},{1,3},{2,0},{3,1},{4,6},{5,7},{6,4},{7,5},{8,10},{9,11},{10,... | collective-permute-start | bytes 884744 | tf_op jit(solution)/shard_map/ppermute | solution.py:376
  110.7 17.2 %collective-permute-start.14 = (bf16[288,1536]{1,0:T(8,128)(2,1)}, bf16[288,1536]{1,0:T(8,128)(2,1)S(1)}, u32[]{:S(2)}, u32[]{:S(2)}) collective-permute-start(bf16[288,1536]{1,0:T(8,128)(2,1)} %collective-permute-done.7.refs_7_.refs_1_), channel_id=1, source_target_pairs={{8,16},{16,8},{9,17},{17,9},{10,18},{18,10},{11,19},{19,11},{12,20... | collective-permute-start | bytes 2654216 | tf_op jit(solution)/shard_map/ppermute | solution.py:272
  116.4 6.7 %collective-permute-start.21 = (bf16[72,2048]{1,0:T(8,128)(2,1)S(1)}, bf16[72,2048]{1,0:T(8,128)(2,1)S(1)}, u32[]{:S(2)}, u32[]{:S(2)}) collective-permute-start(bf16[72,2048]{1,0:T(8,128)(2,1)S(1)} %copy-done.10), channel_id=1, source_target_pairs={{0,4},{1,5},{2,6},{3,7},{4,0},{5,1},{6,2},{7,3},{8,12},{9,13},{10,... | collective-permute-start | bytes 884744 | tf_op jit(solution)/shard_map/ppermute | solution.py:376
  123.1 17.2 %collective-permute-start.22 = (bf16[72,2048]{1,0:T(8,128)(2,1)S(1)}, bf16[72,2048]{1,0:T(8,128)(2,1)S(1)}, u32[]{:S(2)}, u32[]{:S(2)}) collective-permute-start(bf16[72,2048]{1,0:T(8,128)(2,1)S(1)} %copy-done.10), channel_id=1, source_target_pairs={{0,6},{1,7},{2,4},{3,5},{4,2},{5,3},{6,0},{7,1},{8,14},{9,15},{10,... | collective-permute-start | bytes 884744 | tf_op jit(solution)/shard_map/ppermute | solution.py:376
  126.2 15.4 %copy-start = (f32[576,1536]{1,0:T(8,128)S(1)}, f32[576,1536]{1,0:T(8,128)}, u32[]{:S(2)}) copy-start(f32[576,1536]{1,0:T(8,128)} %dhidden.2) | copy-start | bytes 10616836
  127.9 84.1 %copy-start.5 = (bf16[288,1536]{1,0:T(8,128)(2,1)}, bf16[288,1536]{1,0:T(8,128)(2,1)S(1)}, u32[]{:S(2)}) copy-start(bf16[288,1536]{1,0:T(8,128)(2,1)S(1)} %collective-permute-done.14.refs_9_.refs_3_) | copy-start | bytes 2654212
  134.8 15.3 %collective-permute-start.15 = (bf16[144,2048]{1,0:T(8,128)(2,1)S(1)}, bf16[144,2048]{1,0:T(8,128)(2,1)S(1)}, u32[]{:S(2)}, u32[]{:S(2)}) collective-permute-start(bf16[144,2048]{1,0:T(8,128)(2,1)S(1)} %add_convert_fusion.3), channel_id=1, source_target_pairs={{0,8},{8,0},{16,24},{24,16},{1,9},{9,1},{17,25},{25,17},{2,10},{10... | collective-permute-start | bytes 1769480 | tf_op jit(solution)/shard_map/ppermute | solution.py:272
  141.6 41.1 %collective-permute-start.23 = (bf16[4,72,2048]{2,1,0:T(8,128)(2,1)}, bf16[4,72,2048]{2,1,0:T(8,128)(2,1)S(1)}, u32[]{:S(2)}, u32[]{:S(2)}) collective-permute-start(bf16[4,72,2048]{2,1,0:T(8,128)(2,1)} %pad_maximum_fusion.4), channel_id=1, source_target_pairs={{0,1},{1,0},{2,3},{3,2},{4,5},{5,4},{6,7},{7,6},{8,9},{9,8},{10,11... | collective-permute-start | bytes 3538952 | tf_op jit(solution)/shard_map/ppermute | solution.py:383
  142.7 26.9 %collective-permute-start.11 = (bf16[288,1536]{1,0:T(8,128)(2,1)}, bf16[288,1536]{1,0:T(8,128)(2,1)S(1)}, u32[]{:S(2)}, u32[]{:S(2)}) collective-permute-start(bf16[288,1536]{1,0:T(8,128)(2,1)} %add_convert_fusion.1), channel_id=1, source_target_pairs={{8,16},{16,8},{9,17},{17,9},{10,18},{18,10},{11,19},{19,11},{12,20... | collective-permute-start | bytes 2654216 | tf_op jit(solution)/shard_map/ppermute | solution.py:272
  151.8 17.9 %copy-start.8 = (bf16[144,2048]{1,0:T(8,128)(2,1)}, bf16[144,2048]{1,0:T(8,128)(2,1)S(1)}, u32[]{:S(2)}) copy-start(bf16[144,2048]{1,0:T(8,128)(2,1)S(1)} %add_convert_fusion.2.refs_0_) | copy-start | bytes 1769476
  151.8 19.5 %collective-permute-start.18 = (bf16[144,2048]{1,0:T(8,128)(2,1)S(1)}, bf16[144,2048]{1,0:T(8,128)(2,1)}, u32[]{:S(2)}, u32[]{:S(2)}) collective-permute-start(bf16[144,2048]{1,0:T(8,128)(2,1)S(1)} %add_convert_fusion.2.refs_0_), channel_id=1, source_target_pairs={{0,8},{8,0},{16,24},{24,16},{1,9},{9,1},{17,25},{25,17},{2,10},{10... | collective-permute-start | bytes 1769480 | tf_op jit(solution)/shard_map/ppermute | solution.py:272
  153.9 17.4 %collective-permute-start.17 = (bf16[144,2048]{1,0:T(8,128)(2,1)S(1)}, bf16[144,2048]{1,0:T(8,128)(2,1)}, u32[]{:S(2)}, u32[]{:S(2)}) collective-permute-start(bf16[144,2048]{1,0:T(8,128)(2,1)S(1)} %add_convert_fusion.2.refs_0_), channel_id=1, source_target_pairs={{8,16},{16,8},{9,17},{17,9},{10,18},{18,10},{11,19},{19,11},{12,20... | collective-permute-start | bytes 1769480 | tf_op jit(solution)/shard_map/ppermute | solution.py:272
  169.7 13.2 %copy-start.11 = (bf16[288,1536]{1,0:T(8,128)(2,1)}, bf16[288,1536]{1,0:T(8,128)(2,1)S(1)}, u32[]{:S(2)}) copy-start(bf16[288,1536]{1,0:T(8,128)(2,1)S(1)} %collective-permute-done.11) | copy-start | bytes 2654212
  169.8 13.3 %collective-permute-start.16 = (bf16[144,1536]{1,0:T(8,128)(2,1)S(1)}, bf16[144,1536]{1,0:T(8,128)(2,1)S(1)}, u32[]{:S(2)}, u32[]{:S(2)}) collective-permute-start(bf16[144,1536]{1,0:T(8,128)(2,1)S(1)} %add_convert_fusion.5), channel_id=1, source_target_pairs={{0,8},{8,0},{16,24},{24,16},{1,9},{9,1},{17,25},{25,17},{2,10},{10... | collective-permute-start | bytes 1327112 | tf_op jit(solution)/shard_map/ppermute | solution.py:272
  171.3 11.8 %collective-permute-start.26 = (bf16[144,2048]{1,0:T(8,128)(2,1)}, bf16[144,2048]{1,0:T(8,128)(2,1)S(1)}, u32[]{:S(2)}, u32[]{:S(2)}) collective-permute-start(bf16[144,2048]{1,0:T(8,128)(2,1)} %collective-permute-done.18.refs_1_), channel_id=1, source_target_pairs={{8,16},{16,8},{9,17},{17,9},{10,18},{18,10},{11,19},{19,11},{12,20... | collective-permute-start | bytes 1769480 | tf_op jit(solution)/shard_map/ppermute | solution.py:272
  172.2 23.6 %collective-permute-start.19 = (bf16[144,2048]{1,0:T(8,128)(2,1)}, bf16[144,2048]{1,0:T(8,128)(2,1)S(1)}, u32[]{:S(2)}, u32[]{:S(2)}) collective-permute-start(bf16[144,2048]{1,0:T(8,128)(2,1)} %collective-permute-done.17.refs_2_), channel_id=1, source_target_pairs={{0,8},{8,0},{16,24},{24,16},{1,9},{9,1},{17,25},{25,17},{2,10},{10... | collective-permute-start | bytes 1769480 | tf_op jit(solution)/shard_map/ppermute | solution.py:272
  183.1 14.7 %copy-start.13 = (bf16[144,2048]{1,0:T(8,128)(2,1)}, bf16[144,2048]{1,0:T(8,128)(2,1)S(1)}, u32[]{:S(2)}) copy-start(bf16[144,2048]{1,0:T(8,128)(2,1)S(1)} %collective-permute-done.26.refs_3_) | copy-start | bytes 1769476
  195.8 1.7 copy-start.14
  195.8 16.3 %collective-permute-start.27 = (bf16[144,2048]{1,0:T(8,128)(2,1)S(1)}, bf16[144,2048]{1,0:T(8,128)(2,1)S(1)}, u32[]{:S(2)}, u32[]{:S(2)}) collective-permute-start(bf16[144,2048]{1,0:T(8,128)(2,1)S(1)} %collective-permute-done.26.refs_3_), channel_id=1, source_target_pairs={{0,8},{8,0},{16,24},{24,16},{1,9},{9,1},{17,25},{25,17},{2,10},{10... | collective-permute-start | bytes 1769480 | tf_op jit(solution)/shard_map/ppermute | solution.py:272
  197.8 1.7 copy-start.12
  199.7 33.8 %copy-start.9 = (bf16[144,1536]{1,0:T(8,128)(2,1)}, bf16[144,1536]{1,0:T(8,128)(2,1)S(1)}, u32[]{:S(2)}) copy-start(bf16[144,1536]{1,0:T(8,128)(2,1)S(1)} %add_convert_fusion.4.refs_0_) | copy-start | bytes 1327108
  199.7 34.5 %collective-permute-start.25 = (bf16[144,1536]{1,0:T(8,128)(2,1)S(1)}, bf16[144,1536]{1,0:T(8,128)(2,1)S(1)}, u32[]{:S(2)}, u32[]{:S(2)}) collective-permute-start(bf16[144,1536]{1,0:T(8,128)(2,1)S(1)} %add_convert_fusion.4.refs_0_), channel_id=1, source_target_pairs={{8,16},{16,8},{9,17},{17,9},{10,18},{18,10},{11,19},{19,11},{12,20... | collective-permute-start | bytes 1327112 | tf_op jit(solution)/shard_map/ppermute | solution.py:272
  200.4 33.1 %collective-permute-start.24 = (bf16[144,1536]{1,0:T(8,128)(2,1)S(1)}, bf16[144,1536]{1,0:T(8,128)(2,1)S(1)}, u32[]{:S(2)}, u32[]{:S(2)}) collective-permute-start(bf16[144,1536]{1,0:T(8,128)(2,1)S(1)} %add_convert_fusion.4.refs_0_), channel_id=1, source_target_pairs={{0,8},{8,0},{16,24},{24,16},{1,9},{9,1},{17,25},{25,17},{2,10},{10... | collective-permute-start | bytes 1327112 | tf_op jit(solution)/shard_map/ppermute | solution.py:272
  212.1 1.7 copy-start.15
  212.1 36.3 %collective-permute-start.30 = (bf16[288,1536]{1,0:T(8,128)(2,1)S(1)}, bf16[288,1536]{1,0:T(8,128)(2,1)S(1)}, u32[]{:S(2)}, u32[]{:S(2)}) collective-permute-start(bf16[288,1536]{1,0:T(8,128)(2,1)S(1)} %collective-permute-done.14.refs_9_.refs_3_), channel_id=1, source_target_pairs={{0,8},{8,0},{16,24},{24,16},{1,9},{9,1},{17,25},{25,17},{2,10},{10... | collective-permute-start | bytes 2654216 | tf_op jit(solution)/shard_map/ppermute | solution.py:272
  233.5 14.9 %copy-start.17 = (bf16[144,1536]{1,0:T(8,128)(2,1)}, bf16[144,1536]{1,0:T(8,128)(2,1)S(1)}, u32[]{:S(2)}) copy-start(bf16[144,1536]{1,0:T(8,128)(2,1)S(1)} %collective-permute-done.24.refs_1_) | copy-start | bytes 1327108
  233.5 14.9 %collective-permute-start.28 = (bf16[144,1536]{1,0:T(8,128)(2,1)S(1)}, bf16[144,1536]{1,0:T(8,128)(2,1)S(1)}, u32[]{:S(2)}, u32[]{:S(2)}) collective-permute-start(bf16[144,1536]{1,0:T(8,128)(2,1)S(1)} %collective-permute-done.24.refs_1_), channel_id=1, source_target_pairs={{8,16},{16,8},{9,17},{17,9},{10,18},{18,10},{11,19},{19,11},{12,20... | collective-permute-start | bytes 1327112 | tf_op jit(solution)/shard_map/ppermute | solution.py:272
  234.2 14.2 %copy-start.16 = (bf16[144,1536]{1,0:T(8,128)(2,1)}, bf16[144,1536]{1,0:T(8,128)(2,1)S(1)}, u32[]{:S(2)}) copy-start(bf16[144,1536]{1,0:T(8,128)(2,1)S(1)} %collective-permute-done.25.refs_2_) | copy-start | bytes 1327108
  234.2 25.2 %collective-permute-start.29 = (bf16[144,1536]{1,0:T(8,128)(2,1)S(1)}, bf16[144,1536]{1,0:T(8,128)(2,1)S(1)}, u32[]{:S(2)}, u32[]{:S(2)}) collective-permute-start(bf16[144,1536]{1,0:T(8,128)(2,1)S(1)} %collective-permute-done.25.refs_2_), channel_id=1, source_target_pairs={{0,8},{8,0},{16,24},{24,16},{1,9},{9,1},{17,25},{25,17},{2,10},{10... | collective-permute-start | bytes 1327112 | tf_op jit(solution)/shard_map/ppermute | solution.py:272
  248.4 11.1 %copy-start.18 = (bf16[144,1536]{1,0:T(8,128)(2,1)}, bf16[144,1536]{1,0:T(8,128)(2,1)S(1)}, u32[]{:S(2)}) copy-start(bf16[144,1536]{1,0:T(8,128)(2,1)S(1)} %collective-permute-done.28.refs_3_) | copy-start | bytes 1327108
  248.4 11.0 %copy-start.6 = (bf16[288,1536]{1,0:T(8,128)(2,1)}, bf16[288,1536]{1,0:T(8,128)(2,1)S(1)}, u32[]{:S(2)}) copy-start(bf16[288,1536]{1,0:T(8,128)(2,1)S(1)} %collective-permute-done.30.refs_11_.refs_5_) | copy-start | bytes 2654212
  248.4 11.1 %collective-permute-start.31 = (bf16[144,1536]{1,0:T(8,128)(2,1)S(1)}, bf16[144,1536]{1,0:T(8,128)(2,1)S(1)}, u32[]{:S(2)}, u32[]{:S(2)}) collective-permute-start(bf16[144,1536]{1,0:T(8,128)(2,1)S(1)} %collective-permute-done.28.refs_3_), channel_id=1, source_target_pairs={{0,8},{8,0},{16,24},{24,16},{1,9},{9,1},{17,25},{25,17},{2,10},{10... | collective-permute-start | bytes 1327112 | tf_op jit(solution)/shard_map/ppermute | solution.py:272
  280.2 11.4 %collective-permute-start.32 = (f32[4,72,2048]{2,1,0:T(8,128)}, f32[4,72,2048]{2,1,0:T(8,128)S(1)}, u32[]{:S(2)}, u32[]{:S(2)}) collective-permute-start(f32[4,72,2048]{2,1,0:T(8,128)} %bitcast.66), channel_id=1, source_target_pairs={{0,1},{1,0},{2,3},{3,2},{4,5},{5,4},{6,7},{7,6},{8,9},{9,8},{10,11... | collective-permute-start | bytes 7077896 | tf_op jit(solution)/shard_map/ppermute | solution.py:396
  280.3 12.8 %copy-start.1 = (f32[576,2048]{1,0:T(8,128)S(1)}, f32[576,2048]{1,0:T(8,128)}, u32[]{:S(2)}) copy-start(f32[576,2048]{1,0:T(8,128)} %get-tuple-element.82) | copy-start | bytes 14155780
  291.6 1.4 copy-start.7
  295.4 17.7 %collective-permute-start.33 = (bf16[72,2048]{1,0:T(8,128)(2,1)S(1)}, bf16[72,2048]{1,0:T(8,128)(2,1)S(1)}, u32[]{:S(2)}, u32[]{:S(2)}) collective-permute-start(bf16[72,2048]{1,0:T(8,128)(2,1)S(1)} %get-tuple-element.108), channel_id=1, source_target_pairs={{0,2},{1,3},{2,0},{3,1},{4,6},{5,7},{6,4},{7,5},{8,10},{9,11},{10,... | collective-permute-start | bytes 884744 | tf_op jit(solution)/shard_map/ppermute | solution.py:405
  296.9 16.1 %collective-permute-start.34 = (bf16[72,2048]{1,0:T(8,128)(2,1)S(1)}, bf16[72,2048]{1,0:T(8,128)(2,1)S(1)}, u32[]{:S(2)}, u32[]{:S(2)}) collective-permute-start(bf16[72,2048]{1,0:T(8,128)(2,1)S(1)} %get-tuple-element.110), channel_id=1, source_target_pairs={{0,4},{1,5},{2,6},{3,7},{4,0},{5,1},{6,2},{7,3},{8,12},{9,13},{10,... | collective-permute-start | bytes 884744 | tf_op jit(solution)/shard_map/ppermute | solution.py:405
  298.5 14.6 %collective-permute-start.35 = (bf16[72,2048]{1,0:T(8,128)(2,1)S(1)}, bf16[72,2048]{1,0:T(8,128)(2,1)S(1)}, u32[]{:S(2)}, u32[]{:S(2)}) collective-permute-start(bf16[72,2048]{1,0:T(8,128)(2,1)S(1)} %get-tuple-element.109), channel_id=1, source_target_pairs={{0,6},{1,7},{2,4},{3,5},{4,2},{5,3},{6,0},{7,1},{8,14},{9,15},{10,... | collective-permute-start | bytes 884744 | tf_op jit(solution)/shard_map/ppermute | solution.py:405
  (6 other events, 5.4 us)

commit v4 on v3

--- a/solution.py
+++ b/solution.py
@@ -78,13 +78,16 @@
     grad_ref, keep_ref = refs[:2]
     buf, outs = refs[-1], refs[:-1]
     gdown_ref = outs[-3] if factors else outs[-1]
-    gate = in_order(at_ref, buf, pairs, rows, 0)
-    up = in_order(at_ref, buf, pairs, rows, 1)
-    gate_val, up_val, sig, silu = gate_parts(gate, up)
-    if factors:
-        outs[-2][...] = up_val * sig * (1.0 + gate_val * (1.0 - sig))
-        outs[-1][...] = silu
-    hidden = (silu * up_val).astype(BF16)
+    if n == 1:
+        hidden = pairs[0][...]
+    else:
+        gate = in_order(at_ref, buf, pairs, rows, 0)
+        up = in_order(at_ref, buf, pairs, rows, 1)
+        gate_val, up_val, sig, silu = gate_parts(gate, up)
+        if factors:
+            outs[-2][...] = up_val * sig * (1.0 + gate_val * (1.0 - sig))
+            outs[-1][...] = silu
+        hidden = (silu * up_val).astype(BF16)
     out = lax.dot_general(
         hidden, grad_ref[...], (((0,), (0,)), ((), ())), preferred_element_type=F32
     )
@@ -144,6 +147,8 @@
             gate_val, up_val, sig, silu = gate_parts(gate, up)
             d_gate = (d_hidden * up_val * sig * (1.0 + gate_val * (1.0 - sig))).astype(BF16)
             d_up = (d_hidden * silu).astype(BF16)
+            if last:
+                rest[4][...] = (silu * up_val).astype(BF16)
         dg_ref[...] = d_gate
         du_ref[...] = d_up
         dg_all[c] = d_gate
@@ -199,7 +204,11 @@
             jax.ShapeDtypeStruct((T, width), BF16),
             jax.ShapeDtypeStruct((T, width), BF16),
         ]
-        + ([jax.ShapeDtypeStruct((T // 2, D), F32)] if last else []),
+        + (
+            [jax.ShapeDtypeStruct((T // 2, D), F32), jax.ShapeDtypeStruct((T, width), BF16)]
+            if last
+            else []
+        ),
         grid_spec=pltpu.PrefetchScalarGridSpec(
             num_scalar_prefetch=1,
             grid=(D // dt, chunks),
@@ -208,7 +217,7 @@
             + [weight, weight, keep, keep]
             + ([] if first else [gx]),
             out_specs=[gx, tall, tall]
-            + ([pl.BlockSpec((T // 2, dt), lambda d, c, *_: (0, d))] if last else []),
+            + ([pl.BlockSpec((T // 2, dt), lambda d, c, *_: (0, d)), tall] if last else []),
             scratch_shapes=[
                 pltpu.VMEM(((n_row + 1) * rows, ft), BF16),
                 pltpu.VMEM((chunks, T, ft), BF16),
@@ -537,9 +546,9 @@
     h_b.spread_next()
     held = weights(0, d_gate, d_up, held, (half, cut - half))
     total = after(total, held[0])
-    total, d_gate, d_up, send = use(1, h_b.pieces(), b.pieces(), total)
+    total, d_gate, d_up, send, hidden = use(1, h_b.pieces(), b.pieces(), total)
     summed = pair_sums(total, send, n_col, col)
-    (grad_down,) = down(1, b.pieces(), grad_down)
+    (grad_down,) = down(1, [hidden], grad_down)
     grad_x = pair_reduce(summed, n_col, col).astype(BF16)
     held = weights(1, after(d_gate, summed), d_up, held)
     return (grad_x, held[0], held[1], grad_down)

time: 315 us -> 311 us (0.987)
    ppermute x24, waiting for transfers between devices: 72.3 us -> 68.7 us  [issue(): x = lax.ppermute(x, 'row', self.perm)]
where the time goes in v4:
time: 311 us; the launch traced here: 310 us
  Pallas kernels  118 us (38%)
  waiting for transfers between devices  88.8 us (29%)
  starting transfers between devices  68.5 us (22%)
  other arithmetic  19.6 us (6%)
  local copies, waits for them, and re-layouts  13.3 us (4%)
    ppermute x24, waiting for transfers between devices, issue(): x = lax.ppermute(x, 'row', self.perm)  68.7 us
    ppermute x24, starting transfers between devices, issue(): x = lax.ppermute(x, 'row', self.perm)  55.8 us
    pallas_call x2, Pallas kernels, input_grad(): pl.pallas_call(functools.partial(input_kernel, n, rows, len(pairs), first...  39.6 us
    pallas_call x3, Pallas kernels, weight_grads(): pl.pallas_call(weight_kernel, out_shape=(jax.ShapeDtypeStruct((D, F), BF1...  35.8 us
    pallas_call x2, Pallas kernels, down_grad(): pl.pallas_call(functools.partial(down_kernel, n, rows // 2, factors), out...  24.2 us
    ppermute x6, waiting for transfers between devices, pairs_gather(): got.append(lax.ppermute(send, 'col', [(i, i ^ 2 * k) for i in range(n)]))  20.1 us
    pallas_call x2, Pallas kernels, dhidden_part(): pl.pallas_call(dhidden_kernel, out_shape=jax.ShapeDtypeStruct((T, width),...  18.8 us
    ppermute x6, starting transfers between devices, pairs_gather(): got.append(lax.ppermute(send, 'col', [(i, i ^ 2 * k) for i in range(n)]))  9.01 us
  transfers between devices with their start and end apart: 36, of which 12 were waited for; matrix products, arithmetic and copies ran while one was open for 8% of the time, Pallas kernels for 32%

profile of v4, /device:TPU:0, one launch (start us, length us, event | category | flops | bytes accessed | tf_op | source)
XLA Modules:
  0.0 309.8 jit_solution(6428800726380456926)
XLA Ops:
  0.7 1.0 slice-done.2
  1.9 1.1 pad_maximum_fusion.3.refs_0_
  3.0 3.0 collective-permute-start.3
  6.7 2.5 collective-permute-start.2
  10.6 1.0 reshape.31.refs_10_.kg_ref.refs_14_
  12.0 1.0 reshape.32.refs_11_.ku_ref.refs_15_
  13.4 1.1 reshape_reshape.3.keep_ref.refs_7_.refs_2_
  14.5 3.2 %collective-permute-done.2 = bf16[72,2048]{1,0:T(8,128)(2,1)S(1)} collective-permute-done((bf16[72,2048]{1,0:T(8,128)(2,1)S(1)}, bf16[72,2048]{1,0:T(8,128)(2,1)S(1)}, u32[]{:S(2)}, u32[]{:S(2)}) %collective-permute-start.2) | collective-permute-done | bytes 294944 | tf_op jit(solution)/shard_map/ppermute | solution.py:385
  17.7 4.9 %collective-permute-done = bf16[72,2048]{1,0:T(8,128)(2,1)S(1)} collective-permute-done((bf16[72,2048]{1,0:T(8,128)(2,1)S(1)}, bf16[72,2048]{1,0:T(8,128)(2,1)S(1)}, u32[]{:S(2)}, u32[]{:S(2)}) %collective-permute-start) | collective-permute-done | bytes 294944 | tf_op jit(solution)/shard_map/ppermute | solution.py:385
  22.8 9.5 %collective-permute-done.3.refs_1_ = bf16[288,2048]{1,0:T(8,128)(2,1)} collective-permute-done((bf16[288,2048]{1,0:T(8,128)(2,1)}, bf16[288,2048]{1,0:T(8,128)(2,1)}, u32[]{:S(2)}, u32[]{:S(2)}) %collective-permute-start.3) | collective-permute-done | bytes 1179680 | tf_op jit(solution)/shard_map/ppermute | solution.py:281
  32.3 1.0 copy-done.9
  34.1 7.6 %collective-permute-start.7 = (bf16[288,1536]{1,0:T(8,128)(2,1)S(1)}, bf16[288,1536]{1,0:T(8,128)(2,1)}, u32[]{:S(2)}, u32[]{:S(2)}) collective-permute-start(bf16[288,1536]{1,0:T(8,128)(2,1)S(1)} %pad_maximum_fusion.5.refs_6_), channel_id=1, source_target_pairs={{0,8},{8,0},{16,24},{24,16},{1,9},{9,1},{17,25},{25,17},{2,10},{10... | collective-permute-start | bytes 2654216 | tf_op jit(solution)/shard_map/ppermute | solution.py:281
  41.8 1.4 select_bitcast_fusion.2
  43.7 1.6 copy.21
  45.3 9.9 %dhidden.3 = f32[576,2048]{1,0:T(8,128)} custom-call(bf16[576,2048]{1,0:T(8,128)(2,1)} %bitcast.44, bf16[3584,2048]{1,0:T(8,128)(2,1)} %w_ref.3, f32[7,8,2048]{2,1,0:T(8,128)} %reshape_reshape.3.keep_ref.refs_7_.refs_2_), custom_call_target="tpu_custom_call" | custom-call | flops 4831838208 | bytes 13107200 | tf_op jit(solution)/shard_map/dhidden/pallas_call | solution.py:43
  55.2 3.2 %broadcast_select_fusion = bf16[288,2048]{1,0:T(8,128)(2,1)} fusion(bf16[288,2048]{1,0:T(8,128)(2,1)S(1)} %copy-done.10, pred[]{:T(512)S(6)} %or.3, f32[576,2048]{1,0:T(8,128)} %dhidden.3, s32[]{:T(128)S(6)} %select_n.182), kind=kLoop, calls=%fused_computation.32 | loop fusion | flops 589824 | bytes 3538949 | tf_op jit(solution)/shard_map/jit(_where)/select_n | solution.py:320
  58.4 2.5 collective-permute-done.7.refs_7_
  60.9 1.7 collective-permute-start.9
  62.6 1.8 collective-permute-start.12
  64.4 8.9 %dhidden.2 = f32[576,1536]{1,0:T(8,128)} custom-call(bf16[576,2048]{1,0:T(8,128)(2,1)} %bitcast.45, bf16[3584,2048]{1,0:T(8,128)(2,1)} %w_ref.3, f32[7,8,2048]{2,1,0:T(8,128)} %reshape_reshape.3.keep_ref.refs_7_.refs_2_), custom_call_target="tpu_custom_call" | custom-call | flops 3623878656 | bytes 9830400 | tf_op jit(solution)/shard_map/dhidden/pallas_call | solution.py:43
  73.3 1.7 broadcast_select_fusion.1
  75.0 0.8 collective-permute-start.8
  75.8 14.3 %collective-permute-done.9.refs_4_ = bf16[288,2048]{1,0:T(8,128)(2,1)} collective-permute-done((bf16[288,2048]{1,0:T(8,128)(2,1)}, bf16[288,2048]{1,0:T(8,128)(2,1)}, u32[]{:S(2)}, u32[]{:S(2)}) %collective-permute-start.9) | collective-permute-done | bytes 1179680 | tf_op jit(solution)/shard_map/ppermute | solution.py:281
  90.1 1.6 add_convert_fusion
  91.7 1.7 collective-permute-start.10
  93.4 13.1 %collective-permute-done.8.refs_10_ = bf16[288,1536]{1,0:T(8,128)(2,1)S(1)} collective-permute-done((bf16[288,1536]{1,0:T(8,128)(2,1)S(1)}, bf16[288,1536]{1,0:T(8,128)(2,1)S(1)}, u32[]{:S(2)}, u32[]{:S(2)}) %collective-permute-start.8) | collective-permute-done | bytes 884768 | tf_op jit(solution)/shard_map/ppermute | solution.py:281
  106.5 1.5 collective-permute-start.13
  108.0 1.5 collective-permute-start.20
  109.5 1.6 collective-permute-start.14
  111.1 3.6 %collective-permute-done.20 = bf16[72,2048]{1,0:T(8,128)(2,1)S(1)} collective-permute-done((bf16[72,2048]{1,0:T(8,128)(2,1)S(1)}, bf16[72,2048]{1,0:T(8,128)(2,1)S(1)}, u32[]{:S(2)}, u32[]{:S(2)}) %collective-permute-start.20) | collective-permute-done | bytes 294944 | tf_op jit(solution)/shard_map/ppermute | solution.py:385
  114.7 1.5 collective-permute-start.21
  116.2 8.4 %collective-permute-done.21 = bf16[72,2048]{1,0:T(8,128)(2,1)S(1)} collective-permute-done((bf16[72,2048]{1,0:T(8,128)(2,1)S(1)}, bf16[72,2048]{1,0:T(8,128)(2,1)S(1)}, u32[]{:S(2)}, u32[]{:S(2)}) %collective-permute-start.21) | collective-permute-done | bytes 294944 | tf_op jit(solution)/shard_map/ppermute | solution.py:385
  124.6 2.4 collective-permute-start.22
  127.7 1.7 add_convert_fusion.3
  129.4 3.2 %collective-permute-done.13.refs_5_ = bf16[288,2048]{1,0:T(8,128)(2,1)} collective-permute-done((bf16[288,2048]{1,0:T(8,128)(2,1)}, bf16[288,2048]{1,0:T(8,128)(2,1)}, u32[]{:S(2)}, u32[]{:S(2)}) %collective-permute-start.13) | collective-permute-done | bytes 1179680 | tf_op jit(solution)/shard_map/ppermute | solution.py:281
  132.6 4.3 %collective-permute-start.15 = (bf16[144,2048]{1,0:T(8,128)(2,1)S(1)}, bf16[144,2048]{1,0:T(8,128)(2,1)S(1)}, u32[]{:S(2)}, u32[]{:S(2)}) collective-permute-start(bf16[144,2048]{1,0:T(8,128)(2,1)S(1)} %add_convert_fusion.3), channel_id=1, source_target_pairs={{0,8},{8,0},{16,24},{24,16},{1,9},{9,1},{17,25},{25,17},{2,10},{10... | collective-permute-start | bytes 1769480 | tf_op jit(solution)/shard_map/ppermute | solution.py:281
  136.9 1.2 pad_maximum_fusion.4
  138.1 1.2 add_convert_fusion.1
  140.0 4.8 %collective-permute-done.15 = bf16[144,2048]{1,0:T(8,128)(2,1)S(1)} collective-permute-done((bf16[144,2048]{1,0:T(8,128)(2,1)S(1)}, bf16[144,2048]{1,0:T(8,128)(2,1)S(1)}, u32[]{:S(2)}, u32[]{:S(2)}) %collective-permute-start.15) | collective-permute-done | bytes 589856 | tf_op jit(solution)/shard_map/ppermute | solution.py:281
  144.9 1.7 add_convert_fusion.2.refs_0_
  146.5 2.3 collective-permute-start.18
  148.8 1.5 collective-permute-start.17
  150.3 14.3 %grad_down.2 = (bf16[3584,2048]{1,0:T(8,128)(2,1)}, f32[576,2048]{1,0:T(8,128)}, f32[576,2048]{1,0:T(8,128)}) custom-call(s32[7]{0:T(128)} %concatenate.11.at_ref, bf16[288,2048]{1,0:T(8,128)(2,1)} %pad_maximum_fusion.3.refs_0_, bf16[288,2048]{1,0:T(8,128)(2,1)} %collective-permute-done.3.refs_1_, bf16[288,2048]{1,0:T(8,128)(2,1)} %copy-done.9, ...), custom_call_target="tpu_custom_call" | custom-call | flops 4831838208 | bytes 24903680 | tf_op jit(solution)/shard_map/grad_down/pallas_call | solution.py:104
  164.8 0.9 collective-permute-start.16
  165.7 0.9 collective-permute-start.26
  166.6 12.5 %collective-permute-start.19 = (bf16[144,2048]{1,0:T(8,128)(2,1)}, bf16[144,2048]{1,0:T(8,128)(2,1)S(1)}, u32[]{:S(2)}, u32[]{:S(2)}) collective-permute-start(bf16[144,2048]{1,0:T(8,128)(2,1)} %collective-permute-done.17.refs_2_), channel_id=1, source_target_pairs={{0,8},{8,0},{16,24},{24,16},{1,9},{9,1},{17,25},{25,17},{2,10},{10... | collective-permute-start | bytes 1769480 | tf_op jit(solution)/shard_map/ppermute | solution.py:281
  179.5 12.7 %collective-permute-done.19.refs_4_ = bf16[144,2048]{1,0:T(8,128)(2,1)S(1)} collective-permute-done((bf16[144,2048]{1,0:T(8,128)(2,1)}, bf16[144,2048]{1,0:T(8,128)(2,1)S(1)}, u32[]{:S(2)}, u32[]{:S(2)}) %collective-permute-start.19) | collective-permute-done | bytes 589856 | tf_op jit(solution)/shard_map/ppermute | solution.py:281
  192.2 1.7 collective-permute-start.27
  194.2 1.6 copy.22
  196.7 3.2 %collective-permute-start.24 = (bf16[144,1536]{1,0:T(8,128)(2,1)S(1)}, bf16[144,1536]{1,0:T(8,128)(2,1)S(1)}, u32[]{:S(2)}, u32[]{:S(2)}) collective-permute-start(bf16[144,1536]{1,0:T(8,128)(2,1)S(1)} %add_convert_fusion.4.refs_0_), channel_id=1, source_target_pairs={{0,8},{8,0},{16,24},{24,16},{1,9},{9,1},{17,25},{25,17},{2,10},{10... | collective-permute-start | bytes 1327112 | tf_op jit(solution)/shard_map/ppermute | solution.py:281
  199.9 8.5 %collective-permute-done.27.refs_5_ = bf16[144,2048]{1,0:T(8,128)(2,1)S(1)} collective-permute-done((bf16[144,2048]{1,0:T(8,128)(2,1)S(1)}, bf16[144,2048]{1,0:T(8,128)(2,1)S(1)}, u32[]{:S(2)}, u32[]{:S(2)}) %collective-permute-start.27) | collective-permute-done | bytes 589856 | tf_op jit(solution)/shard_map/ppermute | solution.py:281
  208.5 1.7 collective-permute-start.30
  210.2 19.7 %grad_x_part.2 = (f32[576,2048]{1,0:T(8,128)}, bf16[576,2048]{1,0:T(8,128)(2,1)}, bf16[576,2048]{1,0:T(8,128)(2,1)}) custom-call(s32[7]{0:T(128)} %concatenate.11.at_ref, bf16[144,2048]{1,0:T(8,128)(2,1)} %copy-done.6, bf16[144,2048]{1,0:T(8,128)(2,1)} %copy-done.12, bf16[144,2048]{1,0:T(8,128)(2,1)} %collective-permute-done.17.refs_2_, ...), custom_call_target="tpu_custom_call" | custom-call | flops 9663676416 | bytes 26214400 | tf_op jit(solution)/shard_map/grad_x_part/pallas_call | solution.py:200
  230.6 3.5 %collective-permute-start.29 = (bf16[144,1536]{1,0:T(8,128)(2,1)S(1)}, bf16[144,1536]{1,0:T(8,128)(2,1)S(1)}, u32[]{:S(2)}, u32[]{:S(2)}) collective-permute-start(bf16[144,1536]{1,0:T(8,128)(2,1)S(1)} %collective-permute-done.25.refs_2_), channel_id=1, source_target_pairs={{0,8},{8,0},{16,24},{24,16},{1,9},{9,1},{17,25},{25,17},{2,10},{10... | collective-permute-start | bytes 1327112 | tf_op jit(solution)/shard_map/ppermute | solution.py:281
  234.1 10.8 %grad_gate_up.3 = (bf16[2048,3584]{1,0:T(8,128)(2,1)}, bf16[2048,3584]{1,0:T(8,128)(2,1)}) custom-call(bf16[576,2048]{1,0:T(8,128)(2,1)} %bitcast.50, bf16[576,2048]{1,0:T(8,128)(2,1)} %get-tuple-element.76.dg_ref, bf16[576,2048]{1,0:T(8,128)(2,1)} %get-tuple-element.77.du_ref, f32[32,3584]{1,0:T(8,128)} %reshape.31.refs_10_.kg_ref.refs_14_, ...), custom_call_target="tpu_custom_call" | custom-call | flops 4831838208 | bytes 10747904 | tf_op jit(solution)/shard_map/grad_gate_up/pallas_call | solution.py:254
  245.1 10.9 %grad_gate_up.4 = (bf16[2048,3584]{1,0:T(8,128)(2,1)}, bf16[2048,3584]{1,0:T(8,128)(2,1)}) custom-call(bf16[576,2048]{1,0:T(8,128)(2,1)} %bitcast.51, bf16[576,2048]{1,0:T(8,128)(2,1)} %get-tuple-element.76.dg_ref, bf16[576,2048]{1,0:T(8,128)(2,1)} %get-tuple-element.77.du_ref, ...), custom_call_target="tpu_custom_call", output_to_operand_aliasing={{0}: (5, {}), {1}: (6, {})} | custom-call | flops 4831838208 | bytes 10747904 | tf_op jit(solution)/shard_map/grad_gate_up/pallas_call | solution.py:254
  257.5 19.9 %grad_x_part.3 = (f32[576,2048]{1,0:T(8,128)}, bf16[576,1536]{1,0:T(8,128)(2,1)}, bf16[576,1536]{1,0:T(8,128)(2,1)}, f32[288,2048]{1,0:T(8,128)}, bf16[576,1536]{1,0:T(8,128)(2,1)}) custom-call(s32[7]{0:T(128)} %concatenate.11.at_ref, bf16[144,1536]{1,0:T(8,128)(2,1)} %copy-done.7, bf16[144,1536]{1,0:T(8,128)(2,1)} %copy-done.17, ...), custom_call_target="tpu_custom_call", output_to_operand_aliasing={{0}: (17, {})} | custom-call | flops 7247757312 | bytes 22020096 | tf_op jit(solution)/shard_map/grad_x_part/pallas_call | solution.py:200
  277.5 9.9 %grad_down.3 = bf16[3584,2048]{1,0:T(8,128)(2,1)} custom-call(s32[7]{0:T(128)} %concatenate.11.at_ref, bf16[576,1536]{1,0:T(8,128)(2,1)} %get-tuple-element.91.refs_0_, bf16[576,2048]{1,0:T(8,128)(2,1)} %bitcast.47, f32[7,8,2048]{2,1,0:T(8,128)} %reshape_reshape.3.keep_ref.refs_7_.refs_2_, ...), custom_call_target="tpu_custom_call", output_to_operand_aliasing={{}: (4, {})} | custom-call | flops 3623878656 | bytes 18677760 | tf_op jit(solution)/shard_map/grad_down/pallas_call | solution.py:104
  287.5 1.4 copy-done.5
  288.9 2.2 fusion.11
  291.2 1.6 collective-permute-start.33
  292.8 1.5 collective-permute-start.34
  294.8 14.1 %grad_gate_up.5 = (bf16[2048,3584]{1,0:T(8,128)(2,1)}, bf16[2048,3584]{1,0:T(8,128)(2,1)}) custom-call(bf16[576,2048]{1,0:T(8,128)(2,1)} %bitcast.52, bf16[576,1536]{1,0:T(8,128)(2,1)} %get-tuple-element.86.dg_ref, bf16[576,1536]{1,0:T(8,128)(2,1)} %get-tuple-element.87.du_ref, ...), custom_call_target="tpu_custom_call", output_to_operand_aliasing={{0}: (5, {}), {1}: (6, {})} | custom-call | flops 7247757312 | bytes 14942208 | tf_op jit(solution)/shard_map/grad_gate_up/pallas_call | solution.py:254
  308.9 0.9 fusion.10
  (114 shorter events, 10.6 us)
Async XLA Ops:
  0.6 1.1 slice-start.2
  0.6 1.2 slice-start.4
  0.7 6.1 %copy-start.21 = (bf16[72,2048]{1,0:T(8,128)(2,1)S(1)}, bf16[72,2048]{1,0:T(8,128)(2,1)}, u32[]{:S(2)}) copy-start(bf16[72,2048]{1,0:T(8,128)(2,1)} %param.11) | copy-start | bytes 884740
  0.7 9.6 %copy-start.22 = (s32[32,56]{1,0:T(8,128)S(1)}, s32[32,56]{1,0:T(8,128)}, u32[]{:S(2)}) copy-start(s32[32,56]{1,0:T(8,128)} %param.17) | copy-start | bytes 21508
  1.9 9.8 %copy-start.23 = (s32[32,56]{1,0:T(8,128)S(1)}, s32[32,56]{1,0:T(8,128)}, u32[]{:S(2)}) copy-start(s32[32,56]{1,0:T(8,128)} %param.18) | copy-start | bytes 21508
  3.0 29.3 %collective-permute-start.3 = (bf16[288,2048]{1,0:T(8,128)(2,1)}, bf16[288,2048]{1,0:T(8,128)(2,1)}, u32[]{:S(2)}, u32[]{:S(2)}) collective-permute-start(bf16[288,2048]{1,0:T(8,128)(2,1)} %pad_maximum_fusion.3.refs_0_), channel_id=1, source_target_pairs={{0,8},{8,0},{16,24},{24,16},{1,9},{9,1},{17,25},{25,17},{2,10},{10... | collective-permute-start | bytes 3538952 | tf_op jit(solution)/shard_map/ppermute | solution.py:281
  6.0 26.3 %collective-permute-start.4 = (bf16[288,2048]{1,0:T(8,128)(2,1)}, bf16[288,2048]{1,0:T(8,128)(2,1)S(1)}, u32[]{:S(2)}, u32[]{:S(2)}) collective-permute-start(bf16[288,2048]{1,0:T(8,128)(2,1)} %pad_maximum_fusion.3.refs_0_), channel_id=1, source_target_pairs={{8,16},{16,8},{9,17},{17,9},{10,18},{18,10},{11,19},{19,11},{12,20... | collective-permute-start | bytes 3538952 | tf_op jit(solution)/shard_map/ppermute | solution.py:281
  6.7 10.9 %collective-permute-start.2 = (bf16[72,2048]{1,0:T(8,128)(2,1)S(1)}, bf16[72,2048]{1,0:T(8,128)(2,1)S(1)}, u32[]{:S(2)}, u32[]{:S(2)}) collective-permute-start(bf16[72,2048]{1,0:T(8,128)(2,1)S(1)} %copy-done.21), channel_id=1, source_target_pairs={{0,6},{1,7},{2,4},{3,5},{4,2},{5,3},{6,0},{7,1},{8,14},{9,15},{10,... | collective-permute-start | bytes 884744 | tf_op jit(solution)/shard_map/ppermute | solution.py:385
  9.3 13.3 %collective-permute-start = (bf16[72,2048]{1,0:T(8,128)(2,1)S(1)}, bf16[72,2048]{1,0:T(8,128)(2,1)S(1)}, u32[]{:S(2)}, u32[]{:S(2)}) collective-permute-start(bf16[72,2048]{1,0:T(8,128)(2,1)S(1)} %copy-done.21), channel_id=1, source_target_pairs={{0,2},{1,3},{2,0},{3,1},{4,6},{5,7},{6,4},{7,5},{8,10},{9,11},{10,... | collective-permute-start | bytes 884744 | tf_op jit(solution)/shard_map/ppermute | solution.py:385
  9.8 12.8 %collective-permute-start.1 = (bf16[72,2048]{1,0:T(8,128)(2,1)S(1)}, bf16[72,2048]{1,0:T(8,128)(2,1)S(1)}, u32[]{:S(2)}, u32[]{:S(2)}) collective-permute-start(bf16[72,2048]{1,0:T(8,128)(2,1)S(1)} %copy-done.21), channel_id=1, source_target_pairs={{0,4},{1,5},{2,6},{3,7},{4,0},{5,1},{6,2},{7,3},{8,12},{9,13},{10,... | collective-permute-start | bytes 884744 | tf_op jit(solution)/shard_map/ppermute | solution.py:385
  10.6 2.4 copy-start.24
  22.6 10.7 %slice-start.3 = ((bf16[144,3584]{1,0:T(8,128)(2,1)}), bf16[144,1536]{1,0:T(8,128)(2,1)S(1)}, s32[]{:S(2)}) async-start(bf16[144,3584]{1,0:T(8,128)(2,1)} %param.12), calls=%async_computation.3 | async-start | bytes 884736 | tf_op jit(solution)/shard_map/slice | solution.py:455
  22.6 10.7 %slice-start.5 = ((bf16[144,3584]{1,0:T(8,128)(2,1)}), bf16[144,1536]{1,0:T(8,128)(2,1)S(1)}, s32[]{:S(2)}) async-start(bf16[144,3584]{1,0:T(8,128)(2,1)} %param.13), calls=%async_computation.5 | async-start | bytes 884736 | tf_op jit(solution)/shard_map/slice | solution.py:455
  32.3 9.5 %collective-permute-start.5 = (bf16[4,72,2048]{2,1,0:T(8,128)(2,1)S(1)}, bf16[4,72,2048]{2,1,0:T(8,128)(2,1)}, u32[]{:S(2)}, u32[]{:S(2)}) collective-permute-start(bf16[4,72,2048]{2,1,0:T(8,128)(2,1)S(1)} %pad_maximum_fusion.2), channel_id=1, source_target_pairs={{0,1},{1,0},{2,3},{3,2},{4,5},{5,4},{6,7},{7,6},{8,9},{9,8},{10,11... | collective-permute-start | bytes 3538952 | tf_op jit(solution)/shard_map/ppermute | solution.py:392
  33.4 9.8 %copy-start.2 = (bf16[288,1536]{1,0:T(8,128)(2,1)}, bf16[288,1536]{1,0:T(8,128)(2,1)S(1)}, u32[]{:S(2)}) copy-start(bf16[288,1536]{1,0:T(8,128)(2,1)S(1)} %pad_maximum_fusion.5.refs_6_) | copy-start | bytes 2654212
  33.4 25.0 %collective-permute-start.6 = (bf16[288,1536]{1,0:T(8,128)(2,1)S(1)}, bf16[288,1536]{1,0:T(8,128)(2,1)S(1)}, u32[]{:S(2)}, u32[]{:S(2)}) collective-permute-start(bf16[288,1536]{1,0:T(8,128)(2,1)S(1)} %pad_maximum_fusion.5.refs_6_), channel_id=1, source_target_pairs={{8,16},{16,8},{9,17},{17,9},{10,18},{18,10},{11,19},{19,11},{12,20... | collective-permute-start | bytes 2654216 | tf_op jit(solution)/shard_map/ppermute | solution.py:281
  34.1 26.8 %collective-permute-start.7 = (bf16[288,1536]{1,0:T(8,128)(2,1)S(1)}, bf16[288,1536]{1,0:T(8,128)(2,1)}, u32[]{:S(2)}, u32[]{:S(2)}) collective-permute-start(bf16[288,1536]{1,0:T(8,128)(2,1)S(1)} %pad_maximum_fusion.5.refs_6_), channel_id=1, source_target_pairs={{0,8},{8,0},{16,24},{24,16},{1,9},{9,1},{17,25},{25,17},{2,10},{10... | collective-permute-start | bytes 2654216 | tf_op jit(solution)/shard_map/ppermute | solution.py:281
  45.3 9.9 %copy-start.10 = (bf16[288,2048]{1,0:T(8,128)(2,1)S(1)}, bf16[288,2048]{1,0:T(8,128)(2,1)}, u32[]{:S(2)}) copy-start(bf16[288,2048]{1,0:T(8,128)(2,1)} %copy-done.9) | copy-start | bytes 3538948
  55.2 34.9 %slice-start = ((s8[4718592]{0:T(1024)(128)(4,1)}), s8[4194304]{0:T(1024)(128)(4,1)S(1)}, s32[]{:S(2)}) async-start(s8[4718592]{0:T(1024)(128)(4,1)} %bitcast.48), calls=%async_computation | async-start | bytes 8388608
  58.4 31.7 %slice-start.1 = ((s8[4718592]{0:T(1024)(128)(4,1)}), s8[524288]{0:T(1024)(128)(4,1)S(1)}, s32[]{:S(2)}) async-start(s8[4718592]{0:T(1024)(128)(4,1)} %bitcast.48), calls=%async_computation.1 | async-start | bytes 1048576
  58.4 14.9 %copy-start.3 = (bf16[288,1536]{1,0:T(8,128)(2,1)}, bf16[288,1536]{1,0:T(8,128)(2,1)S(1)}, u32[]{:S(2)}) copy-start(bf16[288,1536]{1,0:T(8,128)(2,1)S(1)} %collective-permute-done.6.refs_8_) | copy-start | bytes 2654212
  60.9 29.2 %collective-permute-start.9 = (bf16[288,2048]{1,0:T(8,128)(2,1)}, bf16[288,2048]{1,0:T(8,128)(2,1)}, u32[]{:S(2)}, u32[]{:S(2)}) collective-permute-start(bf16[288,2048]{1,0:T(8,128)(2,1)} %broadcast_select_fusion), channel_id=1, source_target_pairs={{0,8},{8,0},{16,24},{24,16},{1,9},{9,1},{17,25},{25,17},{2,10},{10... | collective-permute-start | bytes 3538952 | tf_op jit(solution)/shard_map/ppermute | solution.py:281
  62.6 43.9 %collective-permute-start.12 = (bf16[288,2048]{1,0:T(8,128)(2,1)}, bf16[288,2048]{1,0:T(8,128)(2,1)}, u32[]{:S(2)}, u32[]{:S(2)}) collective-permute-start(bf16[288,2048]{1,0:T(8,128)(2,1)} %collective-permute-done.3.refs_1_), channel_id=1, source_target_pairs={{8,16},{16,8},{9,17},{17,9},{10,18},{18,10},{11,19},{19,11},{12,20... | collective-permute-start | bytes 3538952 | tf_op jit(solution)/shard_map/ppermute | solution.py:281
  74.9 33.0 %copy-start.8 = (bf16[72,2048]{1,0:T(8,128)(2,1)S(1)}, bf16[72,2048]{1,0:T(8,128)(2,1)}, u32[]{:S(2)}) copy-start(bf16[72,2048]{1,0:T(8,128)(2,1)} %param.10) | copy-start | bytes 884740
  75.0 31.5 %collective-permute-start.8 = (bf16[288,1536]{1,0:T(8,128)(2,1)S(1)}, bf16[288,1536]{1,0:T(8,128)(2,1)S(1)}, u32[]{:S(2)}, u32[]{:S(2)}) collective-permute-start(bf16[288,1536]{1,0:T(8,128)(2,1)S(1)} %broadcast_select_fusion.1), channel_id=1, source_target_pairs={{0,8},{8,0},{16,24},{24,16},{1,9},{9,1},{17,25},{25,17},{2,10},{10... | collective-permute-start | bytes 2654216 | tf_op jit(solution)/shard_map/ppermute | solution.py:281
  91.7 35.9 %collective-permute-start.10 = (bf16[288,2048]{1,0:T(8,128)(2,1)S(1)}, bf16[288,2048]{1,0:T(8,128)(2,1)}, u32[]{:S(2)}, u32[]{:S(2)}) collective-permute-start(bf16[288,2048]{1,0:T(8,128)(2,1)S(1)} %add_convert_fusion), channel_id=1, source_target_pairs={{8,16},{16,8},{9,17},{17,9},{10,18},{18,10},{11,19},{19,11},{12,20... | collective-permute-start | bytes 3538952 | tf_op jit(solution)/shard_map/ppermute | solution.py:281
  106.5 31.6 %copy-start.4 = (bf16[288,1536]{1,0:T(8,128)(2,1)}, bf16[288,1536]{1,0:T(8,128)(2,1)S(1)}, u32[]{:S(2)}) copy-start(bf16[288,1536]{1,0:T(8,128)(2,1)S(1)} %collective-permute-done.8.refs_10_) | copy-start | bytes 2654212
  106.5 26.1 %collective-permute-start.13 = (bf16[288,2048]{1,0:T(8,128)(2,1)}, bf16[288,2048]{1,0:T(8,128)(2,1)}, u32[]{:S(2)}, u32[]{:S(2)}) collective-permute-start(bf16[288,2048]{1,0:T(8,128)(2,1)} %collective-permute-done.12.refs_3_), channel_id=1, source_target_pairs={{0,8},{8,0},{16,24},{24,16},{1,9},{9,1},{17,25},{25,17},{2,10},{10... | collective-permute-start | bytes 3538952 | tf_op jit(solution)/shard_map/ppermute | solution.py:281
  108.0 6.7 %collective-permute-start.20 = (bf16[72,2048]{1,0:T(8,128)(2,1)S(1)}, bf16[72,2048]{1,0:T(8,128)(2,1)S(1)}, u32[]{:S(2)}, u32[]{:S(2)}) collective-permute-start(bf16[72,2048]{1,0:T(8,128)(2,1)S(1)} %copy-done.8), channel_id=1, source_target_pairs={{0,2},{1,3},{2,0},{3,1},{4,6},{5,7},{6,4},{7,5},{8,10},{9,11},{10,... | collective-permute-start | bytes 884744 | tf_op jit(solution)/shard_map/ppermute | solution.py:385
  109.5 19.9 %collective-permute-start.14 = (bf16[288,1536]{1,0:T(8,128)(2,1)}, bf16[288,1536]{1,0:T(8,128)(2,1)}, u32[]{:S(2)}, u32[]{:S(2)}) collective-permute-start(bf16[288,1536]{1,0:T(8,128)(2,1)} %collective-permute-done.7.refs_7_), channel_id=1, source_target_pairs={{8,16},{16,8},{9,17},{17,9},{10,18},{18,10},{11,19},{19,11},{12,20... | collective-permute-start | bytes 2654216 | tf_op jit(solution)/shard_map/ppermute | solution.py:281
  114.7 9.9 %collective-permute-start.21 = (bf16[72,2048]{1,0:T(8,128)(2,1)S(1)}, bf16[72,2048]{1,0:T(8,128)(2,1)S(1)}, u32[]{:S(2)}, u32[]{:S(2)}) collective-permute-start(bf16[72,2048]{1,0:T(8,128)(2,1)S(1)} %copy-done.8), channel_id=1, source_target_pairs={{0,4},{1,5},{2,6},{3,7},{4,0},{5,1},{6,2},{7,3},{8,12},{9,13},{10,... | collective-permute-start | bytes 884744 | tf_op jit(solution)/shard_map/ppermute | solution.py:385
  124.6 12.3 %collective-permute-start.22 = (bf16[72,2048]{1,0:T(8,128)(2,1)S(1)}, bf16[72,2048]{1,0:T(8,128)(2,1)S(1)}, u32[]{:S(2)}, u32[]{:S(2)}) collective-permute-start(bf16[72,2048]{1,0:T(8,128)(2,1)S(1)} %copy-done.8), channel_id=1, source_target_pairs={{0,6},{1,7},{2,4},{3,5},{4,2},{5,3},{6,0},{7,1},{8,14},{9,15},{10,... | collective-permute-start | bytes 884744 | tf_op jit(solution)/shard_map/ppermute | solution.py:385
  127.7 10.5 %copy-start = (f32[576,1536]{1,0:T(8,128)S(1)}, f32[576,1536]{1,0:T(8,128)}, u32[]{:S(2)}) copy-start(f32[576,1536]{1,0:T(8,128)} %dhidden.2) | copy-start | bytes 10616836
  132.6 12.3 %collective-permute-start.15 = (bf16[144,2048]{1,0:T(8,128)(2,1)S(1)}, bf16[144,2048]{1,0:T(8,128)(2,1)S(1)}, u32[]{:S(2)}, u32[]{:S(2)}) collective-permute-start(bf16[144,2048]{1,0:T(8,128)(2,1)S(1)} %add_convert_fusion.3), channel_id=1, source_target_pairs={{0,8},{8,0},{16,24},{24,16},{1,9},{9,1},{17,25},{25,17},{2,10},{10... | collective-permute-start | bytes 1769480 | tf_op jit(solution)/shard_map/ppermute | solution.py:281
  138.1 40.9 %collective-permute-start.23 = (bf16[4,72,2048]{2,1,0:T(8,128)(2,1)}, bf16[4,72,2048]{2,1,0:T(8,128)(2,1)S(1)}, u32[]{:S(2)}, u32[]{:S(2)}) collective-permute-start(bf16[4,72,2048]{2,1,0:T(8,128)(2,1)} %pad_maximum_fusion.4), channel_id=1, source_target_pairs={{0,1},{1,0},{2,3},{3,2},{4,5},{5,4},{6,7},{7,6},{8,9},{9,8},{10,11... | collective-permute-start | bytes 3538952 | tf_op jit(solution)/shard_map/ppermute | solution.py:392
  139.3 25.3 %collective-permute-start.11 = (bf16[288,1536]{1,0:T(8,128)(2,1)}, bf16[288,1536]{1,0:T(8,128)(2,1)S(1)}, u32[]{:S(2)}, u32[]{:S(2)}) collective-permute-start(bf16[288,1536]{1,0:T(8,128)(2,1)} %add_convert_fusion.1), channel_id=1, source_target_pairs={{8,16},{16,8},{9,17},{17,9},{10,18},{18,10},{11,19},{19,11},{12,20... | collective-permute-start | bytes 2654216 | tf_op jit(solution)/shard_map/ppermute | solution.py:281
  146.5 18.1 %copy-start.6 = (bf16[144,2048]{1,0:T(8,128)(2,1)}, bf16[144,2048]{1,0:T(8,128)(2,1)S(1)}, u32[]{:S(2)}) copy-start(bf16[144,2048]{1,0:T(8,128)(2,1)S(1)} %add_convert_fusion.2.refs_0_) | copy-start | bytes 1769476
  146.5 19.1 %collective-permute-start.18 = (bf16[144,2048]{1,0:T(8,128)(2,1)S(1)}, bf16[144,2048]{1,0:T(8,128)(2,1)S(1)}, u32[]{:S(2)}, u32[]{:S(2)}) collective-permute-start(bf16[144,2048]{1,0:T(8,128)(2,1)S(1)} %add_convert_fusion.2.refs_0_), channel_id=1, source_target_pairs={{0,8},{8,0},{16,24},{24,16},{1,9},{9,1},{17,25},{25,17},{2,10},{10... | collective-permute-start | bytes 1769480 | tf_op jit(solution)/shard_map/ppermute | solution.py:281
  148.8 16.9 %collective-permute-start.17 = (bf16[144,2048]{1,0:T(8,128)(2,1)S(1)}, bf16[144,2048]{1,0:T(8,128)(2,1)}, u32[]{:S(2)}, u32[]{:S(2)}) collective-permute-start(bf16[144,2048]{1,0:T(8,128)(2,1)S(1)} %add_convert_fusion.2.refs_0_), channel_id=1, source_target_pairs={{8,16},{16,8},{9,17},{17,9},{10,18},{18,10},{11,19},{19,11},{12,20... | collective-permute-start | bytes 1769480 | tf_op jit(solution)/shard_map/ppermute | solution.py:281
  164.8 14.7 %collective-permute-start.16 = (bf16[144,1536]{1,0:T(8,128)(2,1)S(1)}, bf16[144,1536]{1,0:T(8,128)(2,1)S(1)}, u32[]{:S(2)}, u32[]{:S(2)}) collective-permute-start(bf16[144,1536]{1,0:T(8,128)(2,1)S(1)} %add_convert_fusion.5), channel_id=1, source_target_pairs={{0,8},{8,0},{16,24},{24,16},{1,9},{9,1},{17,25},{25,17},{2,10},{10... | collective-permute-start | bytes 1327112 | tf_op jit(solution)/shard_map/ppermute | solution.py:281
  165.7 13.6 %copy-start.12 = (bf16[144,2048]{1,0:T(8,128)(2,1)}, bf16[144,2048]{1,0:T(8,128)(2,1)S(1)}, u32[]{:S(2)}) copy-start(bf16[144,2048]{1,0:T(8,128)(2,1)S(1)} %collective-permute-done.18.refs_1_) | copy-start | bytes 1769476
  165.7 13.8 %collective-permute-start.26 = (bf16[144,2048]{1,0:T(8,128)(2,1)S(1)}, bf16[144,2048]{1,0:T(8,128)(2,1)S(1)}, u32[]{:S(2)}, u32[]{:S(2)}) collective-permute-start(bf16[144,2048]{1,0:T(8,128)(2,1)S(1)} %collective-permute-done.18.refs_1_), channel_id=1, source_target_pairs={{8,16},{16,8},{9,17},{17,9},{10,18},{18,10},{11,19},{19,11},{12,20... | collective-permute-start | bytes 1769480 | tf_op jit(solution)/shard_map/ppermute | solution.py:281
  166.6 25.6 %collective-permute-start.19 = (bf16[144,2048]{1,0:T(8,128)(2,1)}, bf16[144,2048]{1,0:T(8,128)(2,1)S(1)}, u32[]{:S(2)}, u32[]{:S(2)}) collective-permute-start(bf16[144,2048]{1,0:T(8,128)(2,1)} %collective-permute-done.17.refs_2_), channel_id=1, source_target_pairs={{0,8},{8,0},{16,24},{24,16},{1,9},{9,1},{17,25},{25,17},{2,10},{10... | collective-permute-start | bytes 1769480 | tf_op jit(solution)/shard_map/ppermute | solution.py:281
  179.5 14.7 %copy-start.13 = (bf16[144,2048]{1,0:T(8,128)(2,1)}, bf16[144,2048]{1,0:T(8,128)(2,1)S(1)}, u32[]{:S(2)}) copy-start(bf16[144,2048]{1,0:T(8,128)(2,1)S(1)} %collective-permute-done.26.refs_3_) | copy-start | bytes 1769476
  192.2 2.1 copy-start.14
  192.2 16.3 %collective-permute-start.27 = (bf16[144,2048]{1,0:T(8,128)(2,1)S(1)}, bf16[144,2048]{1,0:T(8,128)(2,1)S(1)}, u32[]{:S(2)}, u32[]{:S(2)}) collective-permute-start(bf16[144,2048]{1,0:T(8,128)(2,1)S(1)} %collective-permute-done.26.refs_3_), channel_id=1, source_target_pairs={{0,8},{8,0},{16,24},{24,16},{1,9},{9,1},{17,25},{25,17},{2,10},{10... | collective-permute-start | bytes 1769480 | tf_op jit(solution)/shard_map/ppermute | solution.py:281
  196.0 33.8 %copy-start.7 = (bf16[144,1536]{1,0:T(8,128)(2,1)}, bf16[144,1536]{1,0:T(8,128)(2,1)S(1)}, u32[]{:S(2)}) copy-start(bf16[144,1536]{1,0:T(8,128)(2,1)S(1)} %add_convert_fusion.4.refs_0_) | copy-start | bytes 1327108
  196.0 34.6 %collective-permute-start.25 = (bf16[144,1536]{1,0:T(8,128)(2,1)S(1)}, bf16[144,1536]{1,0:T(8,128)(2,1)S(1)}, u32[]{:S(2)}, u32[]{:S(2)}) collective-permute-start(bf16[144,1536]{1,0:T(8,128)(2,1)S(1)} %add_convert_fusion.4.refs_0_), channel_id=1, source_target_pairs={{8,16},{16,8},{9,17},{17,9},{10,18},{18,10},{11,19},{19,11},{12,20... | collective-permute-start | bytes 1327112 | tf_op jit(solution)/shard_map/ppermute | solution.py:281
  196.7 33.2 %collective-permute-start.24 = (bf16[144,1536]{1,0:T(8,128)(2,1)S(1)}, bf16[144,1536]{1,0:T(8,128)(2,1)S(1)}, u32[]{:S(2)}, u32[]{:S(2)}) collective-permute-start(bf16[144,1536]{1,0:T(8,128)(2,1)S(1)} %add_convert_fusion.4.refs_0_), channel_id=1, source_target_pairs={{0,8},{8,0},{16,24},{24,16},{1,9},{9,1},{17,25},{25,17},{2,10},{10... | collective-permute-start | bytes 1327112 | tf_op jit(solution)/shard_map/ppermute | solution.py:281
  208.4 1.7 copy-start.15
  208.5 36.5 %collective-permute-start.30 = (bf16[288,1536]{1,0:T(8,128)(2,1)}, bf16[288,1536]{1,0:T(8,128)(2,1)S(1)}, u32[]{:S(2)}, u32[]{:S(2)}) collective-permute-start(bf16[288,1536]{1,0:T(8,128)(2,1)} %collective-permute-done.14.refs_9_), channel_id=1, source_target_pairs={{0,8},{8,0},{16,24},{24,16},{1,9},{9,1},{17,25},{25,17},{2,10},{10... | collective-permute-start | bytes 2654216 | tf_op jit(solution)/shard_map/ppermute | solution.py:281
  229.9 15.0 %copy-start.17 = (bf16[144,1536]{1,0:T(8,128)(2,1)}, bf16[144,1536]{1,0:T(8,128)(2,1)S(1)}, u32[]{:S(2)}) copy-start(bf16[144,1536]{1,0:T(8,128)(2,1)S(1)} %collective-permute-done.24.refs_1_) | copy-start | bytes 1327108
  229.9 15.0 %collective-permute-start.28 = (bf16[144,1536]{1,0:T(8,128)(2,1)S(1)}, bf16[144,1536]{1,0:T(8,128)(2,1)S(1)}, u32[]{:S(2)}, u32[]{:S(2)}) collective-permute-start(bf16[144,1536]{1,0:T(8,128)(2,1)S(1)} %collective-permute-done.24.refs_1_), channel_id=1, source_target_pairs={{8,16},{16,8},{9,17},{17,9},{10,18},{18,10},{11,19},{19,11},{12,20... | collective-permute-start | bytes 1327112 | tf_op jit(solution)/shard_map/ppermute | solution.py:281
  230.6 14.3 %copy-start.16 = (bf16[144,1536]{1,0:T(8,128)(2,1)}, bf16[144,1536]{1,0:T(8,128)(2,1)S(1)}, u32[]{:S(2)}) copy-start(bf16[144,1536]{1,0:T(8,128)(2,1)S(1)} %collective-permute-done.25.refs_2_) | copy-start | bytes 1327108
  230.6 25.3 %collective-permute-start.29 = (bf16[144,1536]{1,0:T(8,128)(2,1)S(1)}, bf16[144,1536]{1,0:T(8,128)(2,1)S(1)}, u32[]{:S(2)}, u32[]{:S(2)}) collective-permute-start(bf16[144,1536]{1,0:T(8,128)(2,1)S(1)} %collective-permute-done.25.refs_2_), channel_id=1, source_target_pairs={{0,8},{8,0},{16,24},{24,16},{1,9},{9,1},{17,25},{25,17},{2,10},{10... | collective-permute-start | bytes 1327112 | tf_op jit(solution)/shard_map/ppermute | solution.py:281
  244.9 11.1 %copy-start.18 = (bf16[144,1536]{1,0:T(8,128)(2,1)}, bf16[144,1536]{1,0:T(8,128)(2,1)S(1)}, u32[]{:S(2)}) copy-start(bf16[144,1536]{1,0:T(8,128)(2,1)S(1)} %collective-permute-done.28.refs_3_) | copy-start | bytes 1327108
  244.9 11.0 %copy-start.11 = (bf16[288,1536]{1,0:T(8,128)(2,1)}, bf16[288,1536]{1,0:T(8,128)(2,1)S(1)}, u32[]{:S(2)}) copy-start(bf16[288,1536]{1,0:T(8,128)(2,1)S(1)} %collective-permute-done.30.refs_11_) | copy-start | bytes 2654212
  244.9 11.1 %collective-permute-start.31 = (bf16[144,1536]{1,0:T(8,128)(2,1)S(1)}, bf16[144,1536]{1,0:T(8,128)(2,1)S(1)}, u32[]{:S(2)}, u32[]{:S(2)}) collective-permute-start(bf16[144,1536]{1,0:T(8,128)(2,1)S(1)} %collective-permute-done.28.refs_3_), channel_id=1, source_target_pairs={{0,8},{8,0},{16,24},{24,16},{1,9},{9,1},{17,25},{25,17},{2,10},{10... | collective-permute-start | bytes 1327112 | tf_op jit(solution)/shard_map/ppermute | solution.py:281
  277.5 10.0 %collective-permute-start.32 = (f32[4,72,2048]{2,1,0:T(8,128)}, f32[4,72,2048]{2,1,0:T(8,128)S(1)}, u32[]{:S(2)}, u32[]{:S(2)}) collective-permute-start(f32[4,72,2048]{2,1,0:T(8,128)} %bitcast.66), channel_id=1, source_target_pairs={{0,1},{1,0},{2,3},{3,2},{4,5},{5,4},{6,7},{7,6},{8,9},{9,8},{10,11... | collective-permute-start | bytes 7077896 | tf_op jit(solution)/shard_map/ppermute | solution.py:405
  277.5 11.4 %copy-start.1 = (f32[576,2048]{1,0:T(8,128)S(1)}, f32[576,2048]{1,0:T(8,128)}, u32[]{:S(2)}) copy-start(f32[576,2048]{1,0:T(8,128)} %get-tuple-element.83) | copy-start | bytes 14155780
  287.5 1.4 copy-start.5
  291.2 17.7 %collective-permute-start.33 = (bf16[72,2048]{1,0:T(8,128)(2,1)S(1)}, bf16[72,2048]{1,0:T(8,128)(2,1)S(1)}, u32[]{:S(2)}, u32[]{:S(2)}) collective-permute-start(bf16[72,2048]{1,0:T(8,128)(2,1)S(1)} %get-tuple-element.110), channel_id=1, source_target_pairs={{0,2},{1,3},{2,0},{3,1},{4,6},{5,7},{6,4},{7,5},{8,10},{9,11},{10,... | collective-permute-start | bytes 884744 | tf_op jit(solution)/shard_map/ppermute | solution.py:414
  292.8 16.1 %collective-permute-start.34 = (bf16[72,2048]{1,0:T(8,128)(2,1)S(1)}, bf16[72,2048]{1,0:T(8,128)(2,1)S(1)}, u32[]{:S(2)}, u32[]{:S(2)}) collective-permute-start(bf16[72,2048]{1,0:T(8,128)(2,1)S(1)} %get-tuple-element.112), channel_id=1, source_target_pairs={{0,4},{1,5},{2,6},{3,7},{4,0},{5,1},{6,2},{7,3},{8,12},{9,13},{10,... | collective-permute-start | bytes 884744 | tf_op jit(solution)/shard_map/ppermute | solution.py:414
  294.3 14.6 %collective-permute-start.35 = (bf16[72,2048]{1,0:T(8,128)(2,1)S(1)}, bf16[72,2048]{1,0:T(8,128)(2,1)S(1)}, u32[]{:S(2)}, u32[]{:S(2)}) collective-permute-start(bf16[72,2048]{1,0:T(8,128)(2,1)S(1)} %get-tuple-element.111), channel_id=1, source_target_pairs={{0,6},{1,7},{2,4},{3,5},{4,2},{5,3},{6,0},{7,1},{8,14},{9,15},{10,... | collective-permute-start | bytes 884744 | tf_op jit(solution)/shard_map/ppermute | solution.py:414
  (3 other events, 2.6 us)
